TPU v7x, 512 devices: a whole 4x4x16 slice. The times are simulated.
512 devices in a mesh: space: 128 (over z, y, core), lead: 4 (over x).
Axes of the slice: x: 4, y: 4, z: 16, core: 2. Of those that a mesh axis runs over, the one named last changes fastest.
Arguments:
- tiles: bfloat16 [128, 16, 32, 256], P('space'), may hold values from -6 to 6
- station_obs: bfloat16 [32768, 128], P('space'), may hold values from -6 to 6
- station_tile: int32 [32768, 1], P('space'), may hold values from 0 to 127; in each aligned block of 256 rows (0 to 255, 256 to 511, ...) at most 4 rows name the same one
- station_pixel: int32 [32768], P('space'), may hold values from 0 to 511
- station_embed: bfloat16 [128, 256], replicated, may hold values from -0.5 to 0.5
- conv_fine: bfloat16 [3, 3, 256, 256], replicated, may hold values from -0.125 to 0.125
- conv_mid: bfloat16 [3, 3, 256, 256], replicated, may hold values from -0.125 to 0.125
- conv_coarse: bfloat16 [3, 3, 256, 256], replicated, may hold values from -0.125 to 0.125
- norm_gains: bfloat16 [4, 256], replicated, may hold values from 0.099609375 to 1.8984375
- film_table: bfloat16 [720, 512], P('lead'), may hold values from -3 to 3
- horizon_step_list: int32 [4], replicated, may hold values from 0 to 719
- out_proj: bfloat16 [256, 256], replicated, may hold values from -0.375 to 0.375
- gauge_bin_projector: bfloat16 [256, 256], replicated, may hold values from -0.375 to 0.375
Outputs:
- horizon_feature_maps: bfloat16 [4, 128, 16, 32, 256], P('lead', 'space')
- gauge_horizon_scores: bfloat16 [4, 32768, 256], P('lead', 'space')
Inputs may be any that keep to these rules, and one draw needn't show every extreme that they name: `station_tile`: among the 256 stations of one index of space no tile is named more than 4 times, a bound that some block reaches; every tile is named by some station.
All inputs are finite; a program needn't handle non-finite values.
Results may differ from a plain program's by a relative error of at most 0.015.
Values may be sent and summed in bfloat16 or wider, within the bound.
No kernel may reach another device: no remote copies, remote signals or barrier semaphores. Data moves between devices by JAX's collectives and lax.ppermute only.
A program may use at most 64 MiB of HBM per device.

v0:
```python
import jax
import jax.numpy as jnp
from jax import lax
from jax.sharding import PartitionSpec as P

TILE_COLS = 8


EPS = 1e-06


def from_behind(value, axis, steps):
    count = lax.axis_size(axis)
    first, last = (max(0, -steps), min(count, count - steps))
    return lax.ppermute(value, axis, [(source, source + steps) for source in range(first, last)])


def rms_scale(values, gain):
    mean_sq = jnp.mean(values * values, axis=-1, keepdims=True)
    return values * lax.rsqrt(mean_sq + EPS) * gain


def conv_valid(padded, weight):
    result = lax.conv_general_dilated(
        padded[None],
        weight,
        (1, 1),
        "VALID",
        dimension_numbers=("NHWC", "HWIO", "NHWC"),
        preferred_element_type=jnp.float32,
    )
    return result[0]


def pool_four(picture):
    height, width, feature_depth = picture.shape
    return jnp.mean(picture.reshape(height // 4, 4, width // 4, 4, feature_depth), axis=(1, 3))


def spread_four(picture):
    return jnp.repeat(jnp.repeat(picture, 4, axis=0), 4, axis=1)


def neighbour(source, offset):
    return from_behind(source, "space", offset)


def with_rims(source):
    column = lax.axis_index("space") % TILE_COLS
    west = neighbour(source[:, -1:], 1) * (column > 0).astype(source.dtype)
    east = neighbour(source[:, :1], -1) * (column < TILE_COLS - 1).astype(source.dtype)
    widened = jnp.concatenate([west, source, east], axis=1)
    north = neighbour(widened[-1:], TILE_COLS)
    south = neighbour(widened[:1], -TILE_COLS)
    return jnp.concatenate([north, widened, south], axis=0)


def body(
    tiles,
    station_obs,
    station_tile,
    station_pixel,
    station_embed,
    conv_fine,
    conv_mid,
    conv_coarse,
    norm_gains,
    film_table,
    horizon_step_list,
    out_proj,
    gauge_bin_projector,
):
    space_count = lax.axis_size("space")
    lead_count = lax.axis_size("lead")
    tile_rows, tile_cols, feature_depth = (tiles.shape[1], tiles.shape[2], tiles.shape[3])
    patch_cell_total = tile_rows * tile_cols
    local_count = station_obs.shape[0]
    capacity = max(4, 2 * local_count // space_count)
    slot_count = space_count * capacity
    gain_rows = norm_gains.astype(jnp.float32)
    dest_tile = station_tile[:, 0]
    dest_hot = (dest_tile[:, None] == jnp.arange(space_count, dtype=jnp.int32)[None, :]).astype(
        jnp.float32
    )
    station_order = jnp.arange(local_count, dtype=jnp.int32)
    earlier_mask = (station_order[None, :] < station_order[:, None]).astype(jnp.float32)
    prior_counts = jnp.dot(earlier_mask, dest_hot, precision=lax.Precision.HIGHEST)
    position = jnp.sum(prior_counts * dest_hot, axis=1).astype(jnp.int32)
    slot_index = dest_tile * capacity + position
    slot_match = slot_index[:, None] == jnp.arange(slot_count, dtype=jnp.int32)[None, :]
    slot_hot = slot_match.astype(jnp.bfloat16)
    pixel_out = (
        jnp.sum(jnp.where(slot_match, station_pixel[:, None] - patch_cell_total, 0), axis=0)
        + patch_cell_total
    )
    embedded = jnp.dot(station_obs, station_embed, preferred_element_type=jnp.float32).astype(
        jnp.bfloat16
    )
    payload = jnp.einsum(
        "sk,sf->kf", slot_hot, embedded, preferred_element_type=jnp.float32
    ).astype(jnp.bfloat16)
    arrived, arrived_pixel = (
        lax.all_to_all(
            payload.reshape(space_count, capacity, -1),
            "space",
            split_axis=0,
            concat_axis=0,
            tiled=True,
        ),
        lax.all_to_all(
            pixel_out.reshape(space_count, capacity),
            "space",
            split_axis=0,
            concat_axis=0,
            tiled=True,
        ),
    )
    arrived = arrived.reshape(slot_count, -1)
    pixel_hot = (
        arrived_pixel.reshape(slot_count)[:, None]
        == jnp.arange(patch_cell_total, dtype=jnp.int32)[None, :]
    ).astype(jnp.bfloat16)
    inject = jnp.einsum("kp,kc->pc", pixel_hot, arrived, preferred_element_type=jnp.float32)
    fine_in = tiles[0].astype(jnp.float32) + inject.reshape(tile_rows, tile_cols, feature_depth)
    normed = rms_scale(fine_in, gain_rows[0]).astype(jnp.bfloat16)
    padded = with_rims(normed)
    enc_fine = (fine_in + jax.nn.silu(conv_valid(padded, conv_fine))).astype(jnp.bfloat16)
    mid_in = pool_four(enc_fine.astype(jnp.float32))
    mid_normed = rms_scale(mid_in, gain_rows[1]).astype(jnp.bfloat16)
    enc_mid = mid_in + jax.nn.silu(conv_valid(with_rims(mid_normed), conv_mid))
    coarse_in = pool_four(enc_mid)
    coarse_normed = rms_scale(coarse_in, gain_rows[2]).astype(jnp.bfloat16)
    coarse_conv = conv_valid(with_rims(coarse_normed), conv_coarse)
    context = coarse_in + jax.nn.silu(coarse_conv)
    merged = enc_fine.astype(jnp.float32) + spread_four(enc_mid + spread_four(context))
    table_rows = film_table.shape[0]
    row_offset = lax.axis_index("lead") * table_rows
    lead_hot = (
        horizon_step_list[:, None] == row_offset + jnp.arange(table_rows, dtype=jnp.int32)[None, :]
    ).astype(jnp.bfloat16)
    partial_value = jnp.dot(lead_hot, film_table, preferred_element_type=jnp.float32)
    film_all = lax.psum(partial_value.astype(jnp.bfloat16), "lead").astype(jnp.float32)
    device_horizon_steps = horizon_step_list.shape[0] // lead_count
    film_own = lax.dynamic_slice_in_dim(
        film_all, lax.axis_index("lead") * device_horizon_steps, device_horizon_steps, 0
    )
    normed_out = rms_scale(merged, gain_rows[3])
    scale_row = film_own[0, :feature_depth]
    shift_row = film_own[0, feature_depth:]
    decoded = jax.nn.silu(normed_out * (1.0 + scale_row) + shift_row).astype(jnp.bfloat16)
    mixed = jnp.dot(
        decoded.reshape(patch_cell_total, feature_depth),
        out_proj,
        preferred_element_type=jnp.float32,
    )
    result_entries = [(merged + mixed.reshape(merged.shape)).astype(jnp.bfloat16)]
    horizon_feature_maps = jnp.stack(result_entries, axis=0)
    gathered_entries = jnp.einsum(
        "kp,lpc->lkc",
        pixel_hot,
        horizon_feature_maps.reshape(device_horizon_steps, patch_cell_total, feature_depth),
        preferred_element_type=jnp.float32,
    ).astype(jnp.bfloat16)
    unnormalised_scores = jnp.dot(
        gathered_entries.reshape(device_horizon_steps * slot_count, feature_depth),
        gauge_bin_projector,
        preferred_element_type=jnp.float32,
    ).astype(jnp.bfloat16)
    returned = lax.all_to_all(
        unnormalised_scores.reshape(device_horizon_steps, space_count, capacity, -1),
        "space",
        split_axis=1,
        concat_axis=1,
        tiled=True,
    )
    gauge_horizon_scores = jnp.einsum(
        "sk,lkq->lsq",
        slot_hot,
        returned.reshape(device_horizon_steps, slot_count, -1),
        preferred_element_type=jnp.float32,
    ).astype(jnp.bfloat16)
    return (horizon_feature_maps[:, None], gauge_horizon_scores)


def solution(mesh):
    in_specs = (
        P("space", None, None, None),
        P("space", None),
        P("space", None),
        P("space"),
        P(),
        P(),
        P(),
        P(),
        P(),
        P("lead", None),
        P(),
        P(),
        P(),
    )
    out_specs = (P("lead", "space", None, None, None), P("lead", "space", None))
    return jax.shard_map(body, mesh=mesh, in_specs=in_specs, out_specs=out_specs, check_vma=False)
```

profile of v0, /device:TPU:33, one launch (start us, length us, event | category | flops | bytes accessed | tf_op | source)
XLA Modules:
  0.0 173.4 jit_solution(15897040878588630894)
XLA Ops:
  0.7 1.0 fusion.3
  4.0 19.6 %all-to-all-start = ((s32[128,1,4]{2,1,0:T(1,128)}), s32[128,1,4]{2,1,0:T(1,128)S(1)}, u32[]{:S(2)}, u32[]{:S(2)}) async-start(s32[128,1,4]{2,1,0:T(1,128)} %bitcast.4), calls=%async_computation | async-start | bytes 131072 | tf_op jit(solution)/shard_map/all_to_all | solution.py:110
  23.6 1.3 convolution_convert_fusion.2
  25.7 12.1 %all-to-all-done = s32[128,1,4]{2,1,0:T(1,128)S(1)} async-done(((s32[128,1,4]{2,1,0:T(1,128)}), s32[128,1,4]{2,1,0:T(1,128)S(1)}, u32[]{:S(2)}, u32[]{:S(2)}) %all-to-all-start) | async-done | bytes 2080 | tf_op jit(solution)/shard_map/all_to_all | solution.py:110
  37.7 6.4 %all-to-all-start.1 = ((bf16[128,4,256]{2,1,0:T(4,128)(2,1)}), bf16[128,4,256]{2,1,0:T(4,128)(2,1)S(1)}, u32[]{:S(2)}, u32[]{:S(2)}) async-start(bf16[128,4,256]{2,1,0:T(4,128)(2,1)} %reshape.234), calls=%async_computation.1 | async-start | bytes 524288 | tf_op jit(solution)/shard_map/all_to_all | solution.py:103
  45.6 21.1 %all-to-all-done.1 = bf16[128,4,256]{2,1,0:T(4,128)(2,1)S(1)} async-done(((bf16[128,4,256]{2,1,0:T(4,128)(2,1)}), bf16[128,4,256]{2,1,0:T(4,128)(2,1)S(1)}, u32[]{:S(2)}, u32[]{:S(2)}) %all-to-all-start.1) | async-done | bytes 262176 | tf_op jit(solution)/shard_map/all_to_all | solution.py:103
  67.4 2.2 %collective-permute-start = (bf16[16,1,256]{2,1,0:T(2,128)(2,1)S(1)}, bf16[16,1,256]{2,1,0:T(2,128)(2,1)S(1)}, u32[]{:S(2)}, u32[]{:S(2)}) collective-permute-start(bf16[16,1,256]{2,1,0:T(2,128)(2,1)S(1)} %get-tuple-element.14), channel_id=1, source_target_pairs={{0,4},{4,8},{8,12},{12,16},{16,20},{20,24},{24,28},{28,32},{32,36}... | collective-permute-start | bytes 24584 | tf_op jit(solution)/shard_map/ppermute | solution.py:15
  69.7 2.1 %collective-permute-start.1 = (bf16[16,1,256]{2,1,0:T(2,128)(2,1)S(1)}, bf16[16,1,256]{2,1,0:T(2,128)(2,1)S(1)}, u32[]{:S(2)}, u32[]{:S(2)}) collective-permute-start(bf16[16,1,256]{2,1,0:T(2,128)(2,1)S(1)} %get-tuple-element.15), channel_id=1, source_target_pairs={{4,0},{8,4},{12,8},{16,12},{20,16},{24,20},{28,24},{32,28},{36,32}... | collective-permute-start | bytes 24584 | tf_op jit(solution)/shard_map/ppermute | solution.py:15
  71.8 2.9 %collective-permute-done.1 = bf16[16,1,256]{2,1,0:T(2,128)(2,1)S(1)} collective-permute-done((bf16[16,1,256]{2,1,0:T(2,128)(2,1)S(1)}, bf16[16,1,256]{2,1,0:T(2,128)(2,1)S(1)}, u32[]{:S(2)}, u32[]{:S(2)}) %collective-permute-start.1) | collective-permute-done | bytes 8224 | tf_op jit(solution)/shard_map/ppermute | solution.py:15
  74.8 2.4 %collective-permute-start.2 = (bf16[1,34,256]{2,1,0:T(8,128)(2,1)S(1)}, bf16[1,34,256]{2,1,0:T(8,128)(2,1)S(1)}, u32[]{:S(2)}, u32[]{:S(2)}) collective-permute-start(bf16[1,34,256]{2,1,0:T(8,128)(2,1)S(1)} %get-tuple-element.12), channel_id=1, source_target_pairs={{0,32},{4,36},{8,40},{12,44},{16,48},{20,52},{24,56},{28,60},{32,6... | collective-permute-start | bytes 52232 | tf_op jit(solution)/shard_map/ppermute | solution.py:15
  77.2 2.9 %collective-permute-start.3 = (bf16[1,34,256]{2,1,0:T(8,128)(2,1)S(1)}, bf16[1,34,256]{2,1,0:T(8,128)(2,1)S(1)}, u32[]{:S(2)}, u32[]{:S(2)}) collective-permute-start(bf16[1,34,256]{2,1,0:T(8,128)(2,1)S(1)} %get-tuple-element.13), channel_id=1, source_target_pairs={{32,0},{36,4},{40,8},{44,12},{48,16},{52,20},{56,24},{60,28},{64,3... | collective-permute-start | bytes 52232 | tf_op jit(solution)/shard_map/ppermute | solution.py:15
  80.1 1.6 collective-permute-done.3
  84.7 3.4 %collective-permute-start.4 = (bf16[4,1,256]{2,1,0:T(2,128)(2,1)S(1)}, bf16[4,1,256]{2,1,0:T(2,128)(2,1)S(1)}, u32[]{:S(2)}, u32[]{:S(2)}) collective-permute-start(bf16[4,1,256]{2,1,0:T(2,128)(2,1)S(1)} %get-tuple-element.18), channel_id=1, source_target_pairs={{0,4},{4,8},{8,12},{12,16},{16,20},{20,24},{24,28},{28,32},{32,36}... | collective-permute-start | bytes 6152 | tf_op jit(solution)/shard_map/ppermute | solution.py:15
  88.1 3.9 %collective-permute-start.5 = (bf16[4,1,256]{2,1,0:T(2,128)(2,1)S(1)}, bf16[4,1,256]{2,1,0:T(2,128)(2,1)S(1)}, u32[]{:S(2)}, u32[]{:S(2)}) collective-permute-start(bf16[4,1,256]{2,1,0:T(2,128)(2,1)S(1)} %get-tuple-element.19), channel_id=1, source_target_pairs={{4,0},{8,4},{12,8},{16,12},{20,16},{24,20},{28,24},{32,28},{36,32}... | collective-permute-start | bytes 6152 | tf_op jit(solution)/shard_map/ppermute | solution.py:15
  93.1 2.3 %collective-permute-start.6 = (bf16[1,10,256]{2,1,0:T(8,128)(2,1)S(1)}, bf16[1,10,256]{2,1,0:T(8,128)(2,1)S(1)}, u32[]{:S(2)}, u32[]{:S(2)}) collective-permute-start(bf16[1,10,256]{2,1,0:T(8,128)(2,1)S(1)} %get-tuple-element.16), channel_id=1, source_target_pairs={{0,32},{4,36},{8,40},{12,44},{16,48},{20,52},{24,56},{28,60},{32,6... | collective-permute-start | bytes 15368 | tf_op jit(solution)/shard_map/ppermute | solution.py:15
  95.4 2.9 %collective-permute-start.7 = (bf16[1,10,256]{2,1,0:T(8,128)(2,1)S(1)}, bf16[1,10,256]{2,1,0:T(8,128)(2,1)S(1)}, u32[]{:S(2)}, u32[]{:S(2)}) collective-permute-start(bf16[1,10,256]{2,1,0:T(8,128)(2,1)S(1)} %get-tuple-element.17), channel_id=1, source_target_pairs={{32,0},{36,4},{40,8},{44,12},{48,16},{52,20},{56,24},{60,28},{64,3... | collective-permute-start | bytes 15368 | tf_op jit(solution)/shard_map/ppermute | solution.py:15
  98.6 8.4 %psum.7 = bf16[4,512]{1,0:T(4,128)(2,1)S(1)} all-reduce(bf16[4,512]{1,0:T(4,128)(2,1)S(1)} %convolution_convert_fusion.5), channel_id=1, replica_groups=mesh['space'=128,'lead'=4] {'lead'}, use_global_device_ids=true, to_apply=%region_9.10 | all-reduce | flops 2048 | bytes 8192 | tf_op jit(solution)/shard_map/psum | solution.py:142
  107.1 1.7 fusion.27
  109.1 4.5 %collective-permute-start.8 = (bf16[1,1,256]{2,1,0:T(2,128)(2,1)S(1)}, bf16[1,1,256]{2,1,0:T(2,128)(2,1)S(1)}, u32[]{:S(2)}, u32[]{:S(2)}) collective-permute-start(bf16[1,1,256]{2,1,0:T(2,128)(2,1)S(1)} %get-tuple-element.26), channel_id=1, source_target_pairs={{0,4},{4,8},{8,12},{12,16},{16,20},{20,24},{24,28},{28,32},{32,36}... | collective-permute-start | bytes 1544 | tf_op jit(solution)/shard_map/ppermute | solution.py:15
  113.7 6.0 %collective-permute-start.9 = (bf16[1,1,256]{2,1,0:T(2,128)(2,1)S(1)}, bf16[1,1,256]{2,1,0:T(2,128)(2,1)S(1)}, u32[]{:S(2)}, u32[]{:S(2)}) collective-permute-start(bf16[1,1,256]{2,1,0:T(2,128)(2,1)S(1)} %get-tuple-element.27), channel_id=1, source_target_pairs={{4,0},{8,4},{12,8},{16,12},{20,16},{24,20},{28,24},{32,28},{36,32}... | collective-permute-start | bytes 1544 | tf_op jit(solution)/shard_map/ppermute | solution.py:15
  120.5 3.7 %collective-permute-start.10 = (bf16[1,4,256]{2,1,0:T(4,128)(2,1)S(1)}, bf16[1,4,256]{2,1,0:T(4,128)(2,1)S(1)}, u32[]{:S(2)}, u32[]{:S(2)}) collective-permute-start(bf16[1,4,256]{2,1,0:T(4,128)(2,1)S(1)} %pad_maximum_fusion.6), channel_id=1, source_target_pairs={{0,32},{4,36},{8,40},{12,44},{16,48},{20,52},{24,56},{28,60},{32,6... | collective-permute-start | bytes 6152 | tf_op jit(solution)/shard_map/ppermute | solution.py:15
  124.3 1.9 %collective-permute-start.11 = (bf16[1,4,256]{2,1,0:T(4,128)(2,1)S(1)}, bf16[1,4,256]{2,1,0:T(4,128)(2,1)S(1)}, u32[]{:S(2)}, u32[]{:S(2)}) collective-permute-start(bf16[1,4,256]{2,1,0:T(4,128)(2,1)S(1)} %pad_maximum_fusion.6), channel_id=1, source_target_pairs={{32,0},{36,4},{40,8},{44,12},{48,16},{52,20},{56,24},{60,28},{64,3... | collective-permute-start | bytes 6152 | tf_op jit(solution)/shard_map/ppermute | solution.py:15
  126.2 2.7 %collective-permute-done.11 = bf16[1,4,256]{2,1,0:T(4,128)(2,1)S(1)} collective-permute-done((bf16[1,4,256]{2,1,0:T(4,128)(2,1)S(1)}, bf16[1,4,256]{2,1,0:T(4,128)(2,1)S(1)}, u32[]{:S(2)}, u32[]{:S(2)}) %collective-permute-start.11) | collective-permute-done | bytes 2080 | tf_op jit(solution)/shard_map/ppermute | solution.py:15
  132.0 40.2 %all_to_all.16 = bf16[1,128,4,256]{3,2,0,1:T(4,128)(2,1)S(1)} all-to-all(bf16[1,128,4,256]{3,2,0,1:T(4,128)(2,1)S(1)} %bitcast.95), channel_id=1, replica_groups=mesh['space'=128,'lead'=4] {'space'}, dimensions={1} | all-to-all | bytes 524288 | tf_op jit(solution)/shard_map/all_to_all | solution.py:169
  (99 shorter events, 14.7 us)
Async XLA Ops:
  0.6 81.5 %copy-start = (bf16[3,3,256,256]{3,2,1,0:T(8,128)(2,1)S(1)}, bf16[3,3,256,256]{3,2,1,0:T(8,128)(2,1)}, u32[]{:S(2)}) copy-start(bf16[3,3,256,256]{3,2,1,0:T(8,128)(2,1)} %param.18) | copy-start | bytes 3538948
  0.6 43.5 %copy-start.2 = (bf16[4,256]{1,0:T(4,128)(2,1)S(1)}, bf16[4,256]{1,0:T(4,128)(2,1)}, u32[]{:S(2)}) copy-start(bf16[4,256]{1,0:T(4,128)(2,1)} %param.21) | copy-start | bytes 6148
  4.0 62.8 %copy-start.3 = (bf16[1,16,32,256]{3,2,1,0:T(8,128)(2,1)S(1)}, bf16[1,16,32,256]{3,2,1,0:T(8,128)(2,1)}, u32[]{:S(2)}) copy-start(bf16[1,16,32,256]{3,2,1,0:T(8,128)(2,1)} %param.13) | copy-start | bytes 786436
  4.0 33.8 %all-to-all-start = ((s32[128,1,4]{2,1,0:T(1,128)}), s32[128,1,4]{2,1,0:T(1,128)S(1)}, u32[]{:S(2)}, u32[]{:S(2)}) async-start(s32[128,1,4]{2,1,0:T(1,128)} %bitcast.4), calls=%async_computation | async-start | bytes 131072 | tf_op jit(solution)/shard_map/all_to_all | solution.py:110
  37.7 29.0 %all-to-all-start.1 = ((bf16[128,4,256]{2,1,0:T(4,128)(2,1)}), bf16[128,4,256]{2,1,0:T(4,128)(2,1)S(1)}, u32[]{:S(2)}, u32[]{:S(2)}) async-start(bf16[128,4,256]{2,1,0:T(4,128)(2,1)} %reshape.234), calls=%async_computation.1 | async-start | bytes 524288 | tf_op jit(solution)/shard_map/all_to_all | solution.py:103
  67.4 4.4 %collective-permute-start = (bf16[16,1,256]{2,1,0:T(2,128)(2,1)S(1)}, bf16[16,1,256]{2,1,0:T(2,128)(2,1)S(1)}, u32[]{:S(2)}, u32[]{:S(2)}) collective-permute-start(bf16[16,1,256]{2,1,0:T(2,128)(2,1)S(1)} %get-tuple-element.14), channel_id=1, source_target_pairs={{0,4},{4,8},{8,12},{12,16},{16,20},{20,24},{24,28},{28,32},{32,36}... | collective-permute-start | bytes 24584 | tf_op jit(solution)/shard_map/ppermute | solution.py:15
  69.7 5.1 %collective-permute-start.1 = (bf16[16,1,256]{2,1,0:T(2,128)(2,1)S(1)}, bf16[16,1,256]{2,1,0:T(2,128)(2,1)S(1)}, u32[]{:S(2)}, u32[]{:S(2)}) collective-permute-start(bf16[16,1,256]{2,1,0:T(2,128)(2,1)S(1)} %get-tuple-element.15), channel_id=1, source_target_pairs={{4,0},{8,4},{12,8},{16,12},{20,16},{24,20},{28,24},{32,28},{36,32}... | collective-permute-start | bytes 24584 | tf_op jit(solution)/shard_map/ppermute | solution.py:15
  74.8 5.3 %collective-permute-start.2 = (bf16[1,34,256]{2,1,0:T(8,128)(2,1)S(1)}, bf16[1,34,256]{2,1,0:T(8,128)(2,1)S(1)}, u32[]{:S(2)}, u32[]{:S(2)}) collective-permute-start(bf16[1,34,256]{2,1,0:T(8,128)(2,1)S(1)} %get-tuple-element.12), channel_id=1, source_target_pairs={{0,32},{4,36},{8,40},{12,44},{16,48},{20,52},{24,56},{28,60},{32,6... | collective-permute-start | bytes 52232 | tf_op jit(solution)/shard_map/ppermute | solution.py:15
  77.2 4.5 %collective-permute-start.3 = (bf16[1,34,256]{2,1,0:T(8,128)(2,1)S(1)}, bf16[1,34,256]{2,1,0:T(8,128)(2,1)S(1)}, u32[]{:S(2)}, u32[]{:S(2)}) collective-permute-start(bf16[1,34,256]{2,1,0:T(8,128)(2,1)S(1)} %get-tuple-element.13), channel_id=1, source_target_pairs={{32,0},{36,4},{40,8},{44,12},{48,16},{52,20},{56,24},{60,28},{64,3... | collective-permute-start | bytes 52232 | tf_op jit(solution)/shard_map/ppermute | solution.py:15
  82.0 0.7 copy-start.9
  84.2 14.2 %copy-start.4 = (bf16[180,512]{1,0:T(8,128)(2,1)S(1)}, bf16[180,512]{1,0:T(8,128)(2,1)}, u32[]{:S(2)}) copy-start(bf16[180,512]{1,0:T(8,128)(2,1)} %param.22) | copy-start | bytes 552964
  84.2 14.2 %copy-start.7 = (s32[4]{0:T(128)S(1)}, s32[4]{0:T(128)}, u32[]{:S(2)}) copy-start(s32[4]{0:T(128)} %param.23) | copy-start | bytes 52
  84.7 7.3 %collective-permute-start.4 = (bf16[4,1,256]{2,1,0:T(2,128)(2,1)S(1)}, bf16[4,1,256]{2,1,0:T(2,128)(2,1)S(1)}, u32[]{:S(2)}, u32[]{:S(2)}) collective-permute-start(bf16[4,1,256]{2,1,0:T(2,128)(2,1)S(1)} %get-tuple-element.18), channel_id=1, source_target_pairs={{0,4},{4,8},{8,12},{12,16},{16,20},{20,24},{24,28},{28,32},{32,36}... | collective-permute-start | bytes 6152 | tf_op jit(solution)/shard_map/ppermute | solution.py:15
  88.1 4.9 %collective-permute-start.5 = (bf16[4,1,256]{2,1,0:T(2,128)(2,1)S(1)}, bf16[4,1,256]{2,1,0:T(2,128)(2,1)S(1)}, u32[]{:S(2)}, u32[]{:S(2)}) collective-permute-start(bf16[4,1,256]{2,1,0:T(2,128)(2,1)S(1)} %get-tuple-element.19), channel_id=1, source_target_pairs={{4,0},{8,4},{12,8},{16,12},{20,16},{24,20},{28,24},{32,28},{36,32}... | collective-permute-start | bytes 6152 | tf_op jit(solution)/shard_map/ppermute | solution.py:15
  93.1 14.0 %collective-permute-start.6 = (bf16[1,10,256]{2,1,0:T(8,128)(2,1)S(1)}, bf16[1,10,256]{2,1,0:T(8,128)(2,1)S(1)}, u32[]{:S(2)}, u32[]{:S(2)}) collective-permute-start(bf16[1,10,256]{2,1,0:T(8,128)(2,1)S(1)} %get-tuple-element.16), channel_id=1, source_target_pairs={{0,32},{4,36},{8,40},{12,44},{16,48},{20,52},{24,56},{28,60},{32,6... | collective-permute-start | bytes 15368 | tf_op jit(solution)/shard_map/ppermute | solution.py:15
  95.4 11.6 %collective-permute-start.7 = (bf16[1,10,256]{2,1,0:T(8,128)(2,1)S(1)}, bf16[1,10,256]{2,1,0:T(8,128)(2,1)S(1)}, u32[]{:S(2)}, u32[]{:S(2)}) collective-permute-start(bf16[1,10,256]{2,1,0:T(8,128)(2,1)S(1)} %get-tuple-element.17), channel_id=1, source_target_pairs={{32,0},{36,4},{40,8},{44,12},{48,16},{52,20},{56,24},{60,28},{64,3... | collective-permute-start | bytes 15368 | tf_op jit(solution)/shard_map/ppermute | solution.py:15
  107.1 21.8 %copy-start.1 = (bf16[3,3,256,256]{3,2,1,0:T(8,128)(2,1)S(1)}, bf16[3,3,256,256]{3,2,1,0:T(8,128)(2,1)}, u32[]{:S(2)}) copy-start(bf16[3,3,256,256]{3,2,1,0:T(8,128)(2,1)} %param.20) | copy-start | bytes 3538948
  109.1 10.6 %collective-permute-start.8 = (bf16[1,1,256]{2,1,0:T(2,128)(2,1)S(1)}, bf16[1,1,256]{2,1,0:T(2,128)(2,1)S(1)}, u32[]{:S(2)}, u32[]{:S(2)}) collective-permute-start(bf16[1,1,256]{2,1,0:T(2,128)(2,1)S(1)} %get-tuple-element.26), channel_id=1, source_target_pairs={{0,4},{4,8},{8,12},{12,16},{16,20},{20,24},{24,28},{28,32},{32,36}... | collective-permute-start | bytes 1544 | tf_op jit(solution)/shard_map/ppermute | solution.py:15
  113.7 6.8 %collective-permute-start.9 = (bf16[1,1,256]{2,1,0:T(2,128)(2,1)S(1)}, bf16[1,1,256]{2,1,0:T(2,128)(2,1)S(1)}, u32[]{:S(2)}, u32[]{:S(2)}) collective-permute-start(bf16[1,1,256]{2,1,0:T(2,128)(2,1)S(1)} %get-tuple-element.27), channel_id=1, source_target_pairs={{4,0},{8,4},{12,8},{16,12},{20,16},{24,20},{28,24},{32,28},{36,32}... | collective-permute-start | bytes 1544 | tf_op jit(solution)/shard_map/ppermute | solution.py:15
  120.5 5.7 %collective-permute-start.10 = (bf16[1,4,256]{2,1,0:T(4,128)(2,1)S(1)}, bf16[1,4,256]{2,1,0:T(4,128)(2,1)S(1)}, u32[]{:S(2)}, u32[]{:S(2)}) collective-permute-start(bf16[1,4,256]{2,1,0:T(4,128)(2,1)S(1)} %pad_maximum_fusion.6), channel_id=1, source_target_pairs={{0,32},{4,36},{8,40},{12,44},{16,48},{20,52},{24,56},{28,60},{32,6... | collective-permute-start | bytes 6152 | tf_op jit(solution)/shard_map/ppermute | solution.py:15
  124.3 4.6 %collective-permute-start.11 = (bf16[1,4,256]{2,1,0:T(4,128)(2,1)S(1)}, bf16[1,4,256]{2,1,0:T(4,128)(2,1)S(1)}, u32[]{:S(2)}, u32[]{:S(2)}) collective-permute-start(bf16[1,4,256]{2,1,0:T(4,128)(2,1)S(1)} %pad_maximum_fusion.6), channel_id=1, source_target_pairs={{32,0},{36,4},{40,8},{44,12},{48,16},{52,20},{56,24},{60,28},{64,3... | collective-permute-start | bytes 6152 | tf_op jit(solution)/shard_map/ppermute | solution.py:15
  129.4 0.9 copy-start.5
  130.3 0.9 copy-start.6
  130.7 41.6 %copy-start.8 = (bf16[16,32,256]{2,1,0:T(8,128)(2,1)}, bf16[16,32,256]{2,1,0:T(8,128)(2,1)S(1)}, u32[]{:S(2)}) copy-start(bf16[16,32,256]{2,1,0:T(8,128)(2,1)S(1)} %fusion) | copy-start | bytes 786436
where the time goes:
time: 174 us; the launch traced here: 173 us
  starting transfers between devices  64.4 us (37%)
  blocking collectives  48.7 us (28%)
  waiting for transfers between devices  42.1 us (24%)
  matrix products  7.31 us (4%)
  local copies, waits for them, and re-layouts  5.7 us (3%)
  other arithmetic  3.97 us (2%)
    all_to_all x1, blocking collectives, body(): lax.all_to_all(unnormalised_scores.reshape(device_horizon_steps, space_co...  40.2 us
    ppermute x12, starting transfers between devices, from_behind(): lax.ppermute(value, axis, [(source, source + steps) for source in range(f...  38.4 us
    all_to_all x1, waiting for transfers between devices, body(): lax.all_to_all(payload.reshape(space_count, capacity, -1), 'space', split...  21.1 us
    all_to_all x1, starting transfers between devices, body(): lax.all_to_all(pixel_out.reshape(space_count, capacity), 'space', split_a...  19.6 us
    all_to_all x1, waiting for transfers between devices, body(): lax.all_to_all(pixel_out.reshape(space_count, capacity), 'space', split_a...  12.1 us
    ppermute x12, waiting for transfers between devices, from_behind(): lax.ppermute(value, axis, [(source, source + steps) for source in range(f...  8.88 us
    psum x1, blocking collectives, body(): lax.psum(partial_value.astype(jnp.bfloat16), 'lead').astype(jnp.float32)  8.45 us
    all_to_all x1, starting transfers between devices, body(): lax.all_to_all(payload.reshape(space_count, capacity, -1), 'space', split...  6.39 us
  transfers between devices with their start and end apart: 14, of which 7 were waited for; matrix products, arithmetic and copies ran while one was open for 2% of the time, Pallas kernels for 0%

commit v1 on v0

v1 whole, which is shorter than its diff:
```python
import jax
import jax.numpy as jnp
from jax import lax
from jax.sharding import PartitionSpec as P

TILE_COLS = 8
EPS = 1e-06
HALO = 5
F32 = jnp.float32
BF16 = jnp.bfloat16


def rms_scale(values, gain):
    mean_sq = jnp.mean(values * values, axis=-1, keepdims=True)
    return values * lax.rsqrt(mean_sq + EPS) * gain


def conv3(picture, weight, padding):
    return lax.conv_general_dilated(
        picture[None],
        weight,
        (1, 1),
        padding,
        dimension_numbers=("NHWC", "HWIO", "NHWC"),
        preferred_element_type=F32,
    )[0]


def pool_four(picture):
    height, width, depth = picture.shape
    return jnp.mean(picture.reshape(height // 4, 4, width // 4, 4, depth), axis=(1, 3))


def spread(picture, times):
    return jnp.repeat(jnp.repeat(picture, times, axis=0), times, axis=1)


def shifted(value, row_step, col_step):
    count = lax.axis_size("space")
    pairs = []
    for source in range(count):
        row, col = source // TILE_COLS + row_step, source % TILE_COLS + col_step
        if 0 <= row < count // TILE_COLS and 0 <= col < TILE_COLS:
            pairs.append((source, row * TILE_COLS + col))
    return lax.ppermute(value, "space", pairs)


def body(
    tiles,
    station_obs,
    station_tile,
    station_pixel,
    station_embed,
    conv_fine,
    conv_mid,
    conv_coarse,
    norm_gains,
    film_table,
    horizon_step_list,
    out_proj,
    gauge_bin_projector,
):
    space_count = lax.axis_size("space")
    tile_rows, tile_cols, depth = tiles.shape[1:]
    cells = tile_rows * tile_cols
    count, readings = station_obs.shape
    gains = norm_gains.astype(F32)
    space_at = lax.axis_index("space")
    row_at, col_at = space_at // TILE_COLS, space_at % TILE_COLS

    table_rows = film_table.shape[0]
    own_rows = lax.axis_index("lead") * table_rows + jnp.arange(table_rows, dtype=jnp.int32)
    lead_hot = (horizon_step_list[:, None] == own_rows[None, :]).astype(BF16)
    film_part = jnp.dot(lead_hot, film_table, preferred_element_type=F32).astype(BF16)
    film_parts = lax.all_gather(film_part, "lead")

    dest = station_tile[:, 0]
    dest_hot = (dest[None, :] == jnp.arange(space_count, dtype=jnp.int32)[:, None]).astype(BF16)
    order = jnp.arange(count, dtype=jnp.int32)
    earlier = (order[:, None] < order[None, :]).astype(BF16)
    prior = jnp.dot(dest_hot, earlier, preferred_element_type=F32)
    position = jnp.sum(prior * dest_hot.astype(F32), axis=0).astype(jnp.int32)
    key = dest * 2 + position % 2 + 2 * space_count * (position // 2)
    slot_rows = jnp.arange(2 * space_count, dtype=jnp.int32)
    first = key[None, :] == slot_rows[:, None]
    second = key[None, :] == slot_rows[:, None] + 2 * space_count
    match = jnp.concatenate([first, second], axis=1).astype(BF16)
    high = (station_pixel // 16).astype(BF16)[:, None]
    low = (station_pixel % 16).astype(BF16)[:, None]
    blank = jnp.zeros((count, readings), BF16)
    zero_two = jnp.zeros((count, 2), BF16)
    tail = jnp.zeros((count, readings - 4), BF16)
    records = jnp.concatenate(
        [
            jnp.concatenate([station_obs, blank, high, low, zero_two, tail], axis=1),
            jnp.concatenate([blank, station_obs, zero_two, high, low, tail], axis=1),
        ],
        axis=0,
    )
    payload = jnp.dot(match, records, preferred_element_type=F32).astype(BF16)
    arrived = lax.all_to_all(
        payload.reshape(space_count, 2, 3 * readings), "space", 0, 0, tiled=True
    ).reshape(2 * space_count, 3 * readings)
    embedded = jnp.dot(
        jnp.concatenate([arrived[:, :readings], arrived[:, readings : 2 * readings]], axis=0),
        station_embed,
        preferred_element_type=F32,
    ).astype(BF16)
    places = arrived[:, 2 * readings : 2 * readings + 4].astype(F32)
    pixel = jnp.concatenate(
        [places[:, 0] * 16 + places[:, 1], places[:, 2] * 16 + places[:, 3]], axis=0
    ).astype(jnp.int32)
    pixel_hot = (pixel[:, None] == jnp.arange(cells, dtype=jnp.int32)[None, :]).astype(BF16)
    inject = jnp.einsum("kp,kc->pc", pixel_hot, embedded, preferred_element_type=F32)
    fine_own = tiles[0].astype(F32) + inject.reshape(tile_rows, tile_cols, depth)

    rim = fine_own.astype(BF16)
    west = shifted(rim[:, -HALO:], 0, 1)
    east = shifted(rim[:, :HALO], 0, -1)
    wide = jnp.concatenate([west, rim, east], axis=1)
    north = shifted(wide[-HALO:], 1, 0)
    south = shifted(wide[:HALO], -1, 0)
    middle = jnp.concatenate([west.astype(F32), fine_own, east.astype(F32)], axis=1)
    fine_in = jnp.concatenate([north.astype(F32), middle, south.astype(F32)], axis=0)

    normed = rms_scale(fine_in, gains[0]).astype(BF16)
    enc_fine = (
        fine_in[1:-1, 1:-1] + jax.nn.silu(conv3(normed, conv_fine, "VALID"))
    ).astype(BF16)
    mid_in = pool_four(enc_fine.astype(F32))
    mid_rows = row_at * (tile_rows // 4) - 1 + jnp.arange(mid_in.shape[0], dtype=jnp.int32)
    mid_cols = col_at * (tile_cols // 4) - 1 + jnp.arange(mid_in.shape[1], dtype=jnp.int32)
    last_row = space_count // TILE_COLS * (tile_rows // 4)
    last_col = TILE_COLS * (tile_cols // 4)
    inside = ((mid_rows >= 0) & (mid_rows < last_row))[:, None, None] & (
        (mid_cols >= 0) & (mid_cols < last_col)
    )[None, :, None]
    mid_normed = jnp.where(inside, rms_scale(mid_in, gains[1]), 0.0).astype(BF16)
    enc_mid = mid_in[1:-1, 1:-1] + jax.nn.silu(conv3(mid_normed, conv_mid, "VALID"))
    coarse_own = pool_four(enc_mid)
    partial = enc_fine[4:-4, 4:-4].astype(F32) + spread(enc_mid, 4)

    found = jnp.dot(
        pixel_hot, partial.astype(BF16).reshape(cells, depth), preferred_element_type=F32
    ).astype(BF16)
    found = jnp.concatenate(
        [
            found[: 2 * space_count].reshape(space_count, 2, depth),
            found[2 * space_count :].reshape(space_count, 2, depth),
        ],
        axis=1,
    )
    coarse_rows = coarse_own.astype(BF16).reshape(1, 4, depth // 2)
    parcel = jnp.concatenate(
        [found, jnp.broadcast_to(coarse_rows, (space_count, 4, depth // 2))], axis=2
    )
    returned = lax.all_to_all(parcel, "space", 0, 0, tiled=True)

    grid_rows, grid_cols = space_count // TILE_COLS, TILE_COLS * 2
    coarse_in = returned[:, :, depth:].reshape(grid_rows, grid_cols, depth).astype(F32)
    coarse_normed = rms_scale(coarse_in, gains[2]).astype(BF16)
    context = coarse_in + jax.nn.silu(conv3(coarse_normed, conv_coarse, "SAME"))
    context_own = lax.dynamic_slice(context, (row_at, col_at * 2, 0), (1, 2, depth))
    merged = partial + spread(context_own, 16)

    film = jnp.sum(film_parts.astype(F32), axis=0)
    film = lax.dynamic_slice_in_dim(film, lax.axis_index("lead"), 1, 0)
    scale_row, shift_row = film[0, :depth], film[0, depth:]

    def decode(values):
        hidden = rms_scale(values, gains[3]) * (1.0 + scale_row) + shift_row
        mixed = jnp.dot(
            jax.nn.silu(hidden).astype(BF16), out_proj, preferred_element_type=F32
        )
        return (values + mixed).astype(BF16)

    maps = decode(merged.reshape(cells, depth))

    slot = dest * 4 + position
    coarse_at = (dest // TILE_COLS) * grid_cols + (dest % TILE_COLS) * 2 + (station_pixel % 32) // 16
    slot_hot = slot[:, None] == jnp.arange(4 * space_count, dtype=jnp.int32)[None, :]
    coarse_hot = coarse_at[:, None] == jnp.arange(grid_rows * grid_cols, dtype=jnp.int32)[None, :]
    pick = jnp.concatenate([slot_hot, coarse_hot], axis=1).astype(BF16)
    sources = jnp.concatenate(
        [
            returned[:, :, :depth].reshape(4 * space_count, depth),
            context.astype(BF16).reshape(grid_rows * grid_cols, depth),
        ],
        axis=0,
    )
    at_stations = decode(jnp.dot(pick, sources, preferred_element_type=F32))
    scores = jnp.dot(at_stations, gauge_bin_projector, preferred_element_type=F32).astype(BF16)
    return (
        maps.reshape(1, 1, tile_rows, tile_cols, depth),
        scores.reshape(1, count, -1),
    )


def solution(mesh):
    in_specs = (
        P("space", None, None, None),
        P("space", None),
        P("space", None),
        P("space"),
        P(),
        P(),
        P(),
        P(),
        P(),
        P("lead", None),
        P(),
        P(),
        P(),
    )
    out_specs = (P("lead", "space", None, None, None), P("lead", "space", None))
    return jax.shard_map(body, mesh=mesh, in_specs=in_specs, out_specs=out_specs, check_vma=False)
```

time: 174 us -> 118 us (0.68)
  the two profiles are of different devices: /device:TPU:33 before, /device:TPU:35 now
where the time goes in v1:
time: 118 us
  waiting for transfers between devices  42.4 us (36%)
  starting transfers between devices  41.6 us (35%)
  blocking collectives  9.72 us (8%)
  matrix products  8.78 us (7%)
  local copies, waits for them, and re-layouts  8.07 us (7%)
  other arithmetic  5.78 us (5%)
  between operations  1.45 us (1%)
    all_to_all x1, waiting for transfers between devices, body(): lax.all_to_all(payload.reshape(space_count, 2, 3 * readings), 'space', 0,...  19.7 us
    all_to_all x1, starting transfers between devices, body(): lax.all_to_all(payload.reshape(space_count, 2, 3 * readings), 'space', 0,...  19.6 us
    all_to_all x1, waiting for transfers between devices, body(): returned = lax.all_to_all(parcel, 'space', 0, 0, tiled=True)  17.8 us
    all_to_all x1, starting transfers between devices, body(): returned = lax.all_to_all(parcel, 'space', 0, 0, tiled=True)  11.2 us
    ppermute x4, starting transfers between devices, shifted(): return lax.ppermute(value, 'space', pairs)  10.8 us
    all_gather x1, blocking collectives, body(): film_parts = lax.all_gather(film_part, 'lead')  9.72 us
    ppermute x4, waiting for transfers between devices, shifted(): return lax.ppermute(value, 'space', pairs)  4.88 us
    conv_general_dilated x3, matrix products, conv3(): lax.conv_general_dilated(picture[None], weight, (1, 1), padding, dimensio...  3.83 us
  transfers between devices with their start and end apart: 6, of which 5 were waited for; matrix products, arithmetic and copies ran while one was open for 1% of the time, Pallas kernels for 0%

profile of v1, /device:TPU:35, one launch (start us, length us, event | category | flops | bytes accessed | tf_op | source)
XLA Modules:
  0.0 117.8 jit_solution(15865751241869377676)
XLA Ops:
  0.6 1.0 fusion.7
  1.6 0.7 fusion.83
  2.6 1.0 concatenate.64
  3.6 1.0 concatenate.63
  5.1 0.8 reshape.330
  5.8 19.6 %all-to-all-start = ((bf16[128,2,384]{2,1,0:T(2,128)(2,1)}), bf16[128,2,384]{2,1,0:T(2,128)(2,1)S(1)}, u32[]{:S(2)}, u32[]{:S(2)}) async-start(bf16[128,2,384]{2,1,0:T(2,128)(2,1)} %reshape.330), calls=%async_computation | async-start | bytes 393216 | tf_op jit(solution)/shard_map/all_to_all | solution.py:101
  25.5 19.7 %all-to-all-done = bf16[128,2,384]{2,1,0:T(2,128)(2,1)S(1)} async-done(((bf16[128,2,384]{2,1,0:T(2,128)(2,1)}), bf16[128,2,384]{2,1,0:T(2,128)(2,1)S(1)}, u32[]{:S(2)}, u32[]{:S(2)}) %all-to-all-start) | async-done | bytes 196640 | tf_op jit(solution)/shard_map/all_to_all | solution.py:101
  46.7 2.3 %collective-permute-start.1 = (bf16[16,5,256]{2,0,1:T(8,128)(2,1)S(1)}, bf16[16,5,256]{2,0,1:T(8,128)(2,1)S(1)}, u32[]{:S(2)}, u32[]{:S(2)}) collective-permute-start(bf16[16,5,256]{2,0,1:T(8,128)(2,1)S(1)} %get-tuple-element.17), channel_id=1, source_target_pairs={{4,0},{8,4},{12,8},{16,12},{20,16},{24,20},{28,24},{36,32},{40,36}... | collective-permute-start | bytes 122888 | tf_op jit(solution)/shard_map/ppermute | solution.py:45
  49.0 3.3 %collective-permute-start = (bf16[16,5,256]{2,0,1:T(8,128)(2,1)S(1)}, bf16[16,5,256]{2,0,1:T(8,128)(2,1)S(1)}, u32[]{:S(2)}, u32[]{:S(2)}) collective-permute-start(bf16[16,5,256]{2,0,1:T(8,128)(2,1)S(1)} %get-tuple-element.16), channel_id=1, source_target_pairs={{0,4},{4,8},{8,12},{12,16},{16,20},{20,24},{24,28},{32,36},{36,40}... | collective-permute-start | bytes 122888 | tf_op jit(solution)/shard_map/ppermute | solution.py:45
  52.4 1.0 collective-permute-done
  53.5 1.9 %collective-permute-start.3 = (bf16[5,42,256]{2,0,1:T(8,128)(2,1)S(1)}, bf16[5,42,256]{2,0,1:T(8,128)(2,1)S(1)}, u32[]{:S(2)}, u32[]{:S(2)}) collective-permute-start(bf16[5,42,256]{2,0,1:T(8,128)(2,1)S(1)} %get-tuple-element.11), channel_id=1, source_target_pairs={{32,0},{36,4},{40,8},{44,12},{48,16},{52,20},{56,24},{60,28},{64,3... | collective-permute-start | bytes 322568 | tf_op jit(solution)/shard_map/ppermute | solution.py:45
  55.4 3.4 %collective-permute-start.2 = (bf16[5,42,256]{2,0,1:T(8,128)(2,1)S(1)}, bf16[5,42,256]{2,0,1:T(8,128)(2,1)S(1)}, u32[]{:S(2)}, u32[]{:S(2)}) collective-permute-start(bf16[5,42,256]{2,0,1:T(8,128)(2,1)S(1)} %get-tuple-element.10), channel_id=1, source_target_pairs={{0,32},{4,36},{8,40},{12,44},{16,48},{20,52},{24,56},{28,60},{32,6... | collective-permute-start | bytes 322568 | tf_op jit(solution)/shard_map/ppermute | solution.py:45
  58.9 2.3 %collective-permute-done.3 = bf16[5,42,256]{2,0,1:T(8,128)(2,1)S(1)} collective-permute-done((bf16[5,42,256]{2,0,1:T(8,128)(2,1)S(1)}, bf16[5,42,256]{2,0,1:T(8,128)(2,1)S(1)}, u32[]{:S(2)}, u32[]{:S(2)}) %collective-permute-start.3) | collective-permute-done | bytes 107552 | tf_op jit(solution)/shard_map/ppermute | solution.py:45
  61.2 1.6 %collective-permute-done.2 = bf16[5,42,256]{2,0,1:T(8,128)(2,1)S(1)} collective-permute-done((bf16[5,42,256]{2,0,1:T(8,128)(2,1)S(1)}, bf16[5,42,256]{2,0,1:T(8,128)(2,1)S(1)}, u32[]{:S(2)}, u32[]{:S(2)}) %collective-permute-start.2) | collective-permute-done | bytes 107552 | tf_op jit(solution)/shard_map/ppermute | solution.py:45
  64.2 1.6 %convolution_select_fusion = f32[24,8,6,256]{3,1,2,0:T(8,128)S(1)} fusion(bf16[3,3,256,256]{3,2,1,0:T(8,128)(2,1)S(1)} %copy-done, bf16[26,1,7,2,256]{4,2,3,0,1:T(8,128)(2,1)S(1)} %slice.114, bf16[26,1,8,6,256]{4,2,3,0,1:T(8,128)(2,1)S(1)} %copy.177, pred[8,6]{0,1:T(8,128)(4,1)S(1)} %copy-done.10), kind=kOutput, calls=%fused_computation.7 | convolution fusion | flops 1361805312 | bytes 3184688 | tf_op jit(solution)/shard_map/conv_general_dilated | solution.py:19
  65.8 0.7 copy.178
  67.6 1.6 %fusion.69 = f32[1,4,8,256]{3,0,2,1:T(1,128)S(1)} fusion(bf16[3,3,256,256]{3,2,1,0:T(8,128)(2,1)} %param.19, bf16[1,6,10,256]{3,1,2,0:T(8,128)(2,1)S(1)} %fusion.67), kind=kOutput, calls=%fused_computation.108 | convolution fusion | flops 37748736 | bytes 1243136 | tf_op jit(solution)/shard_map/conv_general_dilated | solution.py:19
  70.2 1.1 pad_maximum_fusion.1
  71.3 11.2 %all-to-all-start.1 = ((bf16[128,4,384]{2,1,0:T(4,128)(2,1)}), bf16[128,4,384]{2,1,0:T(4,128)(2,1)S(1)}, u32[]{:S(2)}, u32[]{:S(2)}) async-start(bf16[128,4,384]{2,1,0:T(4,128)(2,1)} %pad_maximum_fusion.1), calls=%async_computation.1 | async-start | bytes 786432 | tf_op jit(solution)/shard_map/all_to_all | solution.py:157
  82.8 9.7 %all-gather.1 = bf16[4,4,512]{2,1,0:T(4,128)(2,1)S(1)} all-gather(bf16[1,4,512]{2,1,0:T(4,128)(2,1)S(1)} %fusion.8), channel_id=2, replica_groups=mesh['space'=128,'lead'=4] {'lead'}, dimensions={0}, use_global_device_ids=true | all-gather | bytes 20480 | tf_op jit(solution)/shard_map/all_gather | solution.py:75
  92.8 17.8 %all-to-all-done.1 = bf16[128,4,384]{2,1,0:T(4,128)(2,1)S(1)} async-done(((bf16[128,4,384]{2,1,0:T(4,128)(2,1)}), bf16[128,4,384]{2,1,0:T(4,128)(2,1)S(1)}, u32[]{:S(2)}, u32[]{:S(2)}) %all-to-all-start.1) | async-done | bytes 393248 | tf_op jit(solution)/shard_map/all_to_all | solution.py:157
  111.5 0.8 copy-done.5
  115.7 0.9 fusion.3
  116.6 1.2 %fusion.6 = bf16[1,256,256]{2,1,0:T(8,128)(2,1)} fusion(bf16[256,256]{1,0:T(8,128)(2,1)S(1)} %copy-done.7, f32[256,256]{0,1:T(8,128)S(1)} %get-tuple-element.39, bf16[256,256]{1,0:T(8,128)(2,1)S(1)} %copy-done.2, f32[256]{0:T(256)S(1)} %bitcast.116, f32[256]{0:T(256)S(1)} %bitcast.114, f32[256]{0:T(256)S(1)} %bitcast.119, f32[256]{0:T(256)S(1)} %add_rsqrt_fusion.3), kind=kOutput, calls=%fused_computation.18 | convolution fusion | flops 67895296 | bytes 659456 | tf_op jit(solution)/shard_map/dot_general | solution.py:192
  (118 shorter events, 10.2 us)
Async XLA Ops:
  0.6 63.4 %copy-start = (bf16[3,3,256,256]{3,2,1,0:T(8,128)(2,1)S(1)}, bf16[3,3,256,256]{3,2,1,0:T(8,128)(2,1)}, u32[]{:S(2)}) copy-start(bf16[3,3,256,256]{3,2,1,0:T(8,128)(2,1)} %param.18) | copy-start | bytes 3538948
  3.6 21.9 %copy-start.3 = (bf16[4,256]{1,0:T(4,128)(2,1)S(1)}, bf16[4,256]{1,0:T(4,128)(2,1)}, u32[]{:S(2)}) copy-start(bf16[4,256]{1,0:T(4,128)(2,1)} %param.21) | copy-start | bytes 6148
  5.1 40.6 %copy-start.8 = (bf16[128,256]{1,0:T(8,128)(2,1)S(1)}, bf16[128,256]{1,0:T(8,128)(2,1)}, u32[]{:S(2)}) copy-start(bf16[128,256]{1,0:T(8,128)(2,1)} %param.17) | copy-start | bytes 196612
  5.8 40.4 %copy-start.1 = (bf16[1,16,32,256]{3,2,1,0:T(8,128)(2,1)S(1)}, bf16[1,16,32,256]{3,2,1,0:T(8,128)(2,1)}, u32[]{:S(2)}) copy-start(bf16[1,16,32,256]{3,2,1,0:T(8,128)(2,1)} %param.13) | copy-start | bytes 786436
  5.8 39.4 %all-to-all-start = ((bf16[128,2,384]{2,1,0:T(2,128)(2,1)}), bf16[128,2,384]{2,1,0:T(2,128)(2,1)S(1)}, u32[]{:S(2)}, u32[]{:S(2)}) async-start(bf16[128,2,384]{2,1,0:T(2,128)(2,1)} %reshape.330), calls=%async_computation | async-start | bytes 393216 | tf_op jit(solution)/shard_map/all_to_all | solution.py:101
  46.7 5.7 %collective-permute-start.1 = (bf16[16,5,256]{2,0,1:T(8,128)(2,1)S(1)}, bf16[16,5,256]{2,0,1:T(8,128)(2,1)S(1)}, u32[]{:S(2)}, u32[]{:S(2)}) collective-permute-start(bf16[16,5,256]{2,0,1:T(8,128)(2,1)S(1)} %get-tuple-element.17), channel_id=1, source_target_pairs={{4,0},{8,4},{12,8},{16,12},{20,16},{24,20},{28,24},{36,32},{40,36}... | collective-permute-start | bytes 122888 | tf_op jit(solution)/shard_map/ppermute | solution.py:45
  49.0 4.3 %collective-permute-start = (bf16[16,5,256]{2,0,1:T(8,128)(2,1)S(1)}, bf16[16,5,256]{2,0,1:T(8,128)(2,1)S(1)}, u32[]{:S(2)}, u32[]{:S(2)}) collective-permute-start(bf16[16,5,256]{2,0,1:T(8,128)(2,1)S(1)} %get-tuple-element.16), channel_id=1, source_target_pairs={{0,4},{4,8},{8,12},{12,16},{16,20},{20,24},{24,28},{32,36},{36,40}... | collective-permute-start | bytes 122888 | tf_op jit(solution)/shard_map/ppermute | solution.py:45
  53.5 7.7 %collective-permute-start.3 = (bf16[5,42,256]{2,0,1:T(8,128)(2,1)S(1)}, bf16[5,42,256]{2,0,1:T(8,128)(2,1)S(1)}, u32[]{:S(2)}, u32[]{:S(2)}) collective-permute-start(bf16[5,42,256]{2,0,1:T(8,128)(2,1)S(1)} %get-tuple-element.11), channel_id=1, source_target_pairs={{32,0},{36,4},{40,8},{44,12},{48,16},{52,20},{56,24},{60,28},{64,3... | collective-permute-start | bytes 322568 | tf_op jit(solution)/shard_map/ppermute | solution.py:45
  55.4 7.4 %collective-permute-start.2 = (bf16[5,42,256]{2,0,1:T(8,128)(2,1)S(1)}, bf16[5,42,256]{2,0,1:T(8,128)(2,1)S(1)}, u32[]{:S(2)}, u32[]{:S(2)}) collective-permute-start(bf16[5,42,256]{2,0,1:T(8,128)(2,1)S(1)} %get-tuple-element.10), channel_id=1, source_target_pairs={{0,32},{4,36},{8,40},{12,44},{16,48},{20,52},{24,56},{28,60},{32,6... | collective-permute-start | bytes 322568 | tf_op jit(solution)/shard_map/ppermute | solution.py:45
  63.5 0.7 copy-start.10
  70.0 12.6 %copy-start.6 = (bf16[180,512]{1,0:T(8,128)(2,1)S(1)}, bf16[180,512]{1,0:T(8,128)(2,1)}, u32[]{:S(2)}) copy-start(bf16[180,512]{1,0:T(8,128)(2,1)} %param.22) | copy-start | bytes 552964
  70.0 12.5 %copy-start.9 = (s32[4]{0:T(128)S(1)}, s32[4]{0:T(128)}, u32[]{:S(2)}) copy-start(s32[4]{0:T(128)} %param.23) | copy-start | bytes 52
  70.1 22.5 %copy-start.4 = (s32[256,1]{0,1:T(1,128)S(1)}, s32[256,1]{0,1:T(1,128)}, u32[]{:S(2)}) copy-start(s32[256,1]{0,1:T(1,128)} %param.15) | copy-start | bytes 3076
  71.3 39.4 %all-to-all-start.1 = ((bf16[128,4,384]{2,1,0:T(4,128)(2,1)}), bf16[128,4,384]{2,1,0:T(4,128)(2,1)S(1)}, u32[]{:S(2)}, u32[]{:S(2)}) async-start(bf16[128,4,384]{2,1,0:T(4,128)(2,1)} %pad_maximum_fusion.1), calls=%async_computation.1 | async-start | bytes 786432 | tf_op jit(solution)/shard_map/all_to_all | solution.py:157
  110.7 0.7 copy-start.11
  111.0 1.3 %copy-start.5 = (bf16[3,3,256,256]{3,2,1,0:T(8,128)(2,1)S(1)}, bf16[3,3,256,256]{3,2,1,0:T(8,128)(2,1)}, u32[]{:S(2)}) copy-start(bf16[3,3,256,256]{3,2,1,0:T(8,128)(2,1)} %param.20) | copy-start | bytes 3538948
  114.8 0.9 copy-start.2
  115.2 1.4 %copy-start.7 = (bf16[256,256]{1,0:T(8,128)(2,1)S(1)}, bf16[256,256]{1,0:T(8,128)(2,1)}, u32[]{:S(2)}) copy-start(bf16[256,256]{1,0:T(8,128)(2,1)} %param.25) | copy-start | bytes 393220

commit v2 on v1

v2 whole, which is shorter than its diff:
```python
import jax
import jax.numpy as jnp
import numpy as np
from jax import lax
from jax.experimental import pallas as pl
from jax.experimental.pallas import tpu as pltpu
from jax.sharding import PartitionSpec as P

TILE_COLS = 8
TILE_H, TILE_W, DEPTH = 16, 32, 256
CELLS = TILE_H * TILE_W
EPS = 1e-06
HALO = 5
SIDE = 8
FRAME_H, FRAME_W = TILE_H + 2 * HALO, TILE_W + 2 * SIDE
ENC_H = FRAME_H - 2
BAND = 8
MID_W = 16
F32 = jnp.float32
BF16 = jnp.bfloat16


def dot(a, b):
    return jnp.dot(a, b, preferred_element_type=F32)


def dot_wide(a, b):
    high = b.astype(BF16)
    return dot(a, high) + dot(a, (b - high.astype(F32)).astype(BF16))


def silu(v):
    return v / (1.0 + jnp.exp(-v))


def rms_scale(values, gain):
    mean_sq = jnp.mean(values * values, axis=-1, keepdims=True)
    return values * lax.rsqrt(mean_sq + EPS) * gain


def pool_fine_matrix():
    q = np.arange(BAND * FRAME_W)
    y, x = q // FRAME_W, q % FRAME_W
    rows = np.arange(BAND // 4 * MID_W)
    hit = (y // 4 == rows[:, None] // MID_W) & (x // 4 - 1 == rows[:, None] % MID_W)
    return jnp.asarray(hit & (rows[:, None] % MID_W < 10), BF16) / 16


def spread_mid_matrix():
    q = np.arange(CELLS)
    at = q // TILE_W // 4 * MID_W + q % TILE_W // 4 + 1
    return jnp.asarray(at[:, None] == np.arange(4 * MID_W)[None, :], BF16)


def pool_mid_matrix():
    x = np.arange(4 * MID_W) % MID_W - 1
    rows = np.arange(16)
    return jnp.asarray((x >= 0) & (x < 8) & (x // 4 == rows[:, None]), BF16) / 16


def trunk_kernel(
    place, north, south, west, east, own, conv_fine, conv_mid, gains,
    pool_fine, spread_mid, pool_mid, pixel_hot,
    partial_ref, found_ref, coarse_ref,
    frame, taps, enc, mid_in, mid_taps,
):
    frame[:HALO] = north[...].astype(F32)
    frame[HALO + TILE_H :] = south[...].astype(F32)
    frame[HALO : HALO + TILE_H, :SIDE] = west[...].astype(F32)
    frame[HALO : HALO + TILE_H, SIDE : SIDE + TILE_W] = own[...]
    frame[HALO : HALO + TILE_H, SIDE + TILE_W :] = east[...].astype(F32)
    gain = gains[0:1].astype(F32)
    for y in range(FRAME_H):
        normed = rms_scale(frame[y], gain)
        rows = slice(y * FRAME_W, (y + 1) * FRAME_W)
        taps[rows, :DEPTH] = pltpu.roll(normed, 1, 0).astype(BF16)
        taps[rows, DEPTH : 2 * DEPTH] = normed.astype(BF16)
        taps[rows, 2 * DEPTH :] = pltpu.roll(normed, FRAME_W - 1, 0).astype(BF16)
    size = BAND * FRAME_W
    mid_size = BAND // 4 * MID_W
    for band in range(ENC_H // BAND):
        first = band * BAND
        conv = 0.0
        for dy in range(3):
            start = (first + dy) * FRAME_W
            conv += dot(taps[start : start + size], conv_fine[dy])
        rows = frame[first + 1 : first + 1 + BAND].reshape(size, DEPTH)
        done = (rows + silu(conv)).astype(BF16)
        enc[first : first + BAND] = done.astype(F32).reshape(BAND, FRAME_W, DEPTH)
        mid_in[band * mid_size : (band + 1) * mid_size] = dot(pool_fine[...], done)

    mid = mid_in[...]
    normed = rms_scale(mid, gains[1:2].astype(F32))
    at = lax.broadcasted_iota(jnp.int32, mid.shape, 0)
    row = place[0] * (TILE_H // 4) - 1 + at // MID_W
    col = place[1] * (TILE_W // 4) - 1 + at % MID_W
    inside = (row >= 0) & (row < place[2] * (TILE_H // 4))
    inside = inside & (col >= 0) & (col < TILE_COLS * (TILE_W // 4))
    normed = jnp.where(inside, normed, 0.0)
    mid_taps[:, :DEPTH] = pltpu.roll(normed, 1, 0).astype(BF16)
    mid_taps[:, DEPTH : 2 * DEPTH] = normed.astype(BF16)
    mid_taps[:, 2 * DEPTH :] = pltpu.roll(normed, mid.shape[0] - 1, 0).astype(BF16)
    conv = 0.0
    for dy in range(3):
        conv += dot(mid_taps[dy * MID_W : (dy + 4) * MID_W], conv_mid[dy])
    enc_mid = mid[MID_W : 5 * MID_W] + silu(conv)
    coarse_ref[...] = dot_wide(pool_mid[...], enc_mid).astype(BF16)
    centre = enc[HALO - 1 : HALO - 1 + TILE_H, SIDE : SIDE + TILE_W]
    partial = centre.reshape(CELLS, DEPTH) + dot_wide(spread_mid[...], enc_mid)
    partial_ref[...] = partial
    found_ref[...] = dot(pixel_hot[...], partial.astype(BF16)).astype(BF16)


def tail_kernel(
    place, slots, coarse_in, conv_coarse, gains, partial, film, pick, out_proj, projector,
    maps_ref, scores_ref,
    taps,
):
    cells, wide = coarse_in.shape[0], TILE_COLS * 2
    coarse = coarse_in[...].astype(F32)
    normed = rms_scale(coarse, gains[2:3].astype(F32))
    col = lax.broadcasted_iota(jnp.int32, coarse.shape, 0) % wide
    taps[:wide] = jnp.zeros((wide, 3 * DEPTH), BF16)
    taps[wide + cells :] = jnp.zeros((wide, 3 * DEPTH), BF16)
    inner = slice(wide, wide + cells)
    left, right = pltpu.roll(normed, 1, 0), pltpu.roll(normed, cells - 1, 0)
    taps[inner, :DEPTH] = jnp.where(col == 0, 0.0, left).astype(BF16)
    taps[inner, DEPTH : 2 * DEPTH] = normed.astype(BF16)
    taps[inner, 2 * DEPTH :] = jnp.where(col == wide - 1, 0.0, right).astype(BF16)
    conv = 0.0
    for dy in range(3):
        conv += dot(taps[dy * wide : dy * wide + cells], conv_coarse[dy])
    context = coarse + silu(conv)
    high = context.astype(BF16)
    low = (context - high.astype(F32)).astype(BF16)

    gain = gains[3:4].astype(F32)
    scale, shift = 1.0 + film[0:1], film[1:2]

    def decode(values):
        hidden = rms_scale(values, gain) * scale + shift
        return (values + dot(silu(hidden).astype(BF16), out_proj[...])).astype(BF16)

    at = lax.broadcasted_iota(jnp.int32, (CELLS, cells), 0)
    here = place[0] * wide + place[1] * 2 + (at % TILE_W) // (TILE_W // 2)
    mine = (lax.broadcasted_iota(jnp.int32, (CELLS, cells), 1) == here).astype(F32).astype(BF16)
    maps_ref[...] = decode(partial[...] + (dot(mine, high) + dot(mine, low)))

    count = slots.shape[0]
    at_stations = dot(pick[:, :count], slots[...])
    at_stations += dot(pick[:, count:], high) + dot(pick[:, count:], low)
    scores_ref[...] = dot(decode(at_stations), projector[...]).astype(BF16)


def call(kernel, outs, scratch, operands):
    vmem = pl.BlockSpec(memory_space=pltpu.VMEM)
    smem = pl.BlockSpec(memory_space=pltpu.SMEM)
    return pl.pallas_call(
        kernel,
        out_shape=outs,
        in_specs=[smem] + [vmem] * (len(operands) - 1),
        out_specs=[vmem] * len(outs),
        scratch_shapes=[pltpu.VMEM(shape, dtype) for shape, dtype in scratch],
        compiler_params=pltpu.CompilerParams(vmem_limit_bytes=32 * 2**20),
    )(*operands)


def trunk(place, north, south, west, east, own, conv_fine, conv_mid, gains, pixel_hot):
    slot_count = pixel_hot.shape[0]
    return call(
        trunk_kernel,
        [
            jax.ShapeDtypeStruct((CELLS, DEPTH), F32),
            jax.ShapeDtypeStruct((slot_count, DEPTH), BF16),
            jax.ShapeDtypeStruct((16, DEPTH), BF16),
        ],
        [
            ((FRAME_H, FRAME_W, DEPTH), F32),
            ((FRAME_H * FRAME_W, 3 * DEPTH), BF16),
            ((ENC_H, FRAME_W, DEPTH), F32),
            ((ENC_H // 4 * MID_W, DEPTH), F32),
            ((ENC_H // 4 * MID_W, 3 * DEPTH), BF16),
        ],
        [
            place, north, south, west, east, own,
            conv_fine.reshape(3, 3 * DEPTH, DEPTH),
            conv_mid.reshape(3, 3 * DEPTH, DEPTH),
            gains, pool_fine_matrix(), spread_mid_matrix(), pool_mid_matrix(), pixel_hot,
        ],
    )


def tail(place, slots, coarse_in, conv_coarse, gains, partial, film, pick, out_proj, projector):
    cells = coarse_in.shape[0]
    return call(
        tail_kernel,
        [
            jax.ShapeDtypeStruct((CELLS, DEPTH), BF16),
            jax.ShapeDtypeStruct((pick.shape[0], projector.shape[1]), BF16),
        ],
        [((cells + 4 * TILE_COLS, 3 * DEPTH), BF16)],
        [
            place, slots, coarse_in, conv_coarse.reshape(3, 3 * DEPTH, DEPTH), gains,
            partial, film, pick, out_proj, projector,
        ],
    )


def shifted(value, row_step, col_step):
    count = lax.axis_size("space")
    pairs = []
    for source in range(count):
        row, col = source // TILE_COLS + row_step, source % TILE_COLS + col_step
        if 0 <= row < count // TILE_COLS and 0 <= col < TILE_COLS:
            pairs.append((source, row * TILE_COLS + col))
    return lax.ppermute(value, "space", pairs)


def body(
    tiles,
    station_obs,
    station_tile,
    station_pixel,
    station_embed,
    conv_fine,
    conv_mid,
    conv_coarse,
    norm_gains,
    film_table,
    horizon_step_list,
    out_proj,
    gauge_bin_projector,
):
    space_count = lax.axis_size("space")
    count, readings = station_obs.shape
    space_at = lax.axis_index("space")
    place = jnp.stack(
        [space_at // TILE_COLS, space_at % TILE_COLS, jnp.int32(space_count // TILE_COLS)]
    ).astype(jnp.int32)

    table_rows = film_table.shape[0]
    own_rows = lax.axis_index("lead") * table_rows + jnp.arange(table_rows, dtype=jnp.int32)
    lead_hot = (horizon_step_list[:, None] == own_rows[None, :]).astype(BF16)
    film_parts = lax.all_gather(dot(lead_hot, film_table).astype(BF16), "lead")
    film = jnp.sum(film_parts.astype(F32), axis=0)
    film = lax.dynamic_slice_in_dim(film, lax.axis_index("lead"), 1, 0).reshape(2, DEPTH)

    dest = station_tile[:, 0]
    dest_hot = (dest[None, :] == jnp.arange(space_count, dtype=jnp.int32)[:, None]).astype(BF16)
    order = jnp.arange(count, dtype=jnp.int32)
    earlier = (order[:, None] < order[None, :]).astype(BF16)
    prior = dot(dest_hot, earlier)
    position = jnp.sum(prior * dest_hot.astype(F32), axis=0).astype(jnp.int32)
    half, pair = position % 2, position // 2
    key = dest * 2 + half + 2 * space_count * pair
    slot_rows = jnp.arange(2 * space_count, dtype=jnp.int32)
    first = key[None, :] == slot_rows[:, None]
    second = key[None, :] == slot_rows[:, None] + 2 * space_count
    match = jnp.concatenate([first, second], axis=1).astype(BF16)
    high = (station_pixel // 16).astype(BF16)[:, None]
    low = (station_pixel % 16).astype(BF16)[:, None]
    blank = jnp.zeros((count, readings), BF16)
    zero_two = jnp.zeros((count, 2), BF16)
    rest = jnp.zeros((count, readings - 4), BF16)
    records = jnp.concatenate(
        [
            jnp.concatenate([station_obs, blank, high, low, zero_two, rest], axis=1),
            jnp.concatenate([blank, station_obs, zero_two, high, low, rest], axis=1),
        ],
        axis=0,
    )
    payload = dot(match, records).astype(BF16)
    arrived = lax.all_to_all(
        payload.reshape(space_count, 2, 3 * readings), "space", 0, 0, tiled=True
    ).reshape(2 * space_count, 3 * readings)
    embedded = dot(
        jnp.concatenate([arrived[:, :readings], arrived[:, readings : 2 * readings]], axis=0),
        station_embed,
    ).astype(BF16)
    places = arrived[:, 2 * readings : 2 * readings + 4].astype(F32)
    pixel = jnp.stack(
        [places[:, 0] * 16 + places[:, 1], places[:, 2] * 16 + places[:, 3]], axis=0
    ).astype(jnp.int32)
    cell = jnp.arange(CELLS, dtype=jnp.int32)
    pixel_hot = (pixel.reshape(-1)[:, None] == cell[None, :]).astype(BF16)
    inject = jnp.einsum("kp,kc->pc", pixel_hot, embedded, preferred_element_type=F32)
    fine_own = tiles[0].astype(F32) + inject.reshape(TILE_H, TILE_W, DEPTH)

    rim = fine_own.astype(BF16)
    west = shifted(rim[:, -SIDE:], 0, 1)
    east = shifted(rim[:, :SIDE], 0, -1)
    wide = jnp.concatenate([west, rim, east], axis=1)
    north = shifted(wide[-HALO:], 1, 0)
    south = shifted(wide[:HALO], -1, 0)

    back_hot = (pixel.T.reshape(-1)[:, None] == cell[None, :]).astype(BF16)
    partial, found, coarse_own = trunk(
        place, north, south, west, east, fine_own, conv_fine, conv_mid, norm_gains, back_hot
    )
    coarse_rows = coarse_own[:2].reshape(1, 4, DEPTH // 2)
    parcel = jnp.concatenate(
        [
            found.reshape(space_count, 4, DEPTH),
            jnp.broadcast_to(coarse_rows, (space_count, 4, DEPTH // 2)),
        ],
        axis=2,
    )
    returned = lax.all_to_all(parcel, "space", 0, 0, tiled=True)

    grid = 2 * space_count
    coarse_in = returned[:, :, DEPTH:].reshape(grid, DEPTH)
    slots = returned[:, :, :DEPTH].reshape(4 * space_count, DEPTH)
    slot = dest * 4 + half * 2 + pair
    coarse_at = (dest // TILE_COLS) * (TILE_COLS * 2) + (dest % TILE_COLS) * 2
    coarse_at = coarse_at + (station_pixel % TILE_W) // (TILE_W // 2)
    slot_hot = slot[:, None] == jnp.arange(4 * space_count, dtype=jnp.int32)[None, :]
    coarse_hot = coarse_at[:, None] == jnp.arange(grid, dtype=jnp.int32)[None, :]
    pick = jnp.concatenate([slot_hot, coarse_hot], axis=1).astype(BF16)
    maps, scores = tail(
        place, slots, coarse_in, conv_coarse, norm_gains, partial, film, pick,
        out_proj, gauge_bin_projector,
    )
    return maps.reshape(1, 1, TILE_H, TILE_W, DEPTH), scores.reshape(1, count, -1)


def solution(mesh):
    in_specs = (
        P("space", None, None, None),
        P("space", None),
        P("space", None),
        P("space"),
        P(),
        P(),
        P(),
        P(),
        P(),
        P("lead", None),
        P(),
        P(),
        P(),
    )
    out_specs = (P("lead", "space", None, None, None), P("lead", "space", None))
    return jax.shard_map(body, mesh=mesh, in_specs=in_specs, out_specs=out_specs, check_vma=False)
```

time: 118 us -> 114 us (0.966)
  Pallas kernels: 0 us -> 8.58 us
  matrix products: 8.78 us -> 1.99 us
  other arithmetic: 5.78 us -> 2.74 us
    pallas_call x0 -> x2, Pallas kernels: none -> 8.58 us  [call(): pl.pallas_call(kernel, out_shape=outs, in_specs=[smem] + [vmem] * (len(op...]
    conv_general_dilated x3 -> x0, matrix products: 3.83 us -> none  [conv3(): lax.conv_general_dilated(picture[None], weight, (1, 1), padding, dimensio...]
    dot_general x7 -> x3, matrix products: 4.4 us -> 1.44 us  [dot(): return jnp.dot(a, b, preferred_element_type=F32)]
    conv_general_dilated x7 -> x0, local copies, waits for them, and re-layouts: 1.34 us -> none  [conv3(): lax.conv_general_dilated(picture[None], weight, (1, 1), padding, dimensio...]
  transfers between devices with their start and end apart: 6 -> 6, of which waited for: 5 -> 5; matrix products, arithmetic and copies ran while one was open for 1% -> 2% of each run, Pallas kernels for 0% -> 0%
where the time goes in v2:
time: 114 us
  waiting for transfers between devices  41.8 us (37%)
  starting transfers between devices  40.6 us (36%)
  blocking collectives  9.71 us (9%)
  Pallas kernels  8.58 us (8%)
  local copies, waits for them, and re-layouts  6.95 us (6%)
  other arithmetic  2.74 us (2%)
  matrix products  1.99 us (2%)
    all_to_all x1, waiting for transfers between devices, body(): lax.all_to_all(payload.reshape(space_count, 2, 3 * readings), 'space', 0,...  19.8 us
    all_to_all x1, starting transfers between devices, body(): lax.all_to_all(payload.reshape(space_count, 2, 3 * readings), 'space', 0,...  19.5 us
    all_to_all x1, waiting for transfers between devices, body(): returned = lax.all_to_all(parcel, 'space', 0, 0, tiled=True)  17.8 us
    all_to_all x1, starting transfers between devices, body(): returned = lax.all_to_all(parcel, 'space', 0, 0, tiled=True)  11.4 us
    ppermute x4, starting transfers between devices, shifted(): return lax.ppermute(value, 'space', pairs)  9.76 us
    all_gather x1, blocking collectives, body(): film_parts = lax.all_gather(dot(lead_hot, film_table).astype(BF16), 'lead')  9.71 us
    pallas_call x2, Pallas kernels, call(): pl.pallas_call(kernel, out_shape=outs, in_specs=[smem] + [vmem] * (len(op...  8.58 us
    ppermute x4, waiting for transfers between devices, shifted(): return lax.ppermute(value, 'space', pairs)  4.27 us
  transfers between devices with their start and end apart: 6, of which 5 were waited for; matrix products, arithmetic and copies ran while one was open for 2% of the time, Pallas kernels for 0%

profile of v2, /device:TPU:35, one launch (start us, length us, event | category | flops | bytes accessed | tf_op | source)
XLA Modules:
  0.0 113.5 jit_solution(8706688767580587332)
XLA Ops:
  0.7 0.9 fusion.1
  1.6 0.7 fusion.28
  2.6 1.0 concatenate.25
  4.2 0.8 reshape.224
  5.0 19.5 %all-to-all-start = ((bf16[128,2,384]{2,1,0:T(2,128)(2,1)}), bf16[128,2,384]{2,1,0:T(2,128)(2,1)S(1)}, u32[]{:S(2)}, u32[]{:S(2)}) async-start(bf16[128,2,384]{2,1,0:T(2,128)(2,1)} %reshape.224), calls=%async_computation | async-start | bytes 393216 | tf_op jit(solution)/shard_map/all_to_all | solution.py:273
  24.5 19.8 %all-to-all-done = bf16[128,2,384]{2,1,0:T(2,128)(2,1)S(1)} async-done(((bf16[128,2,384]{2,1,0:T(2,128)(2,1)}), bf16[128,2,384]{2,1,0:T(2,128)(2,1)S(1)}, u32[]{:S(2)}, u32[]{:S(2)}) %all-to-all-start) | async-done | bytes 196640 | tf_op jit(solution)/shard_map/all_to_all | solution.py:273
  44.7 0.5 fusion
  45.4 0.6 fusion.41
  46.1 2.6 %collective-permute-start = (bf16[16,8,256]{2,1,0:T(8,128)(2,1)}, bf16[16,8,256]{2,1,0:T(8,128)(2,1)S(1)}, u32[]{:S(2)}, u32[]{:S(2)}) collective-permute-start(bf16[16,8,256]{2,1,0:T(8,128)(2,1)} %get-tuple-element.18), channel_id=1, source_target_pairs={{0,4},{4,8},{8,12},{12,16},{16,20},{20,24},{24,28},{32,36},{36,40}... | collective-permute-start | bytes 196616 | tf_op jit(solution)/shard_map/ppermute | solution.py:216
  48.6 1.9 %collective-permute-start.1 = (bf16[16,8,256]{2,1,0:T(8,128)(2,1)}, bf16[16,8,256]{2,1,0:T(8,128)(2,1)S(1)}, u32[]{:S(2)}, u32[]{:S(2)}) collective-permute-start(bf16[16,8,256]{2,1,0:T(8,128)(2,1)} %get-tuple-element.19), channel_id=1, source_target_pairs={{4,0},{8,4},{12,8},{16,12},{20,16},{24,20},{28,24},{36,32},{40,36}... | collective-permute-start | bytes 196616 | tf_op jit(solution)/shard_map/ppermute | solution.py:216
  50.6 0.8 copy.33
  51.4 1.0 eq.119
  52.5 1.9 %collective-permute-done.1.east = bf16[16,8,256]{2,1,0:T(8,128)(2,1)S(1)} collective-permute-done((bf16[16,8,256]{2,1,0:T(8,128)(2,1)}, bf16[16,8,256]{2,1,0:T(8,128)(2,1)S(1)}, u32[]{:S(2)}, u32[]{:S(2)}) %collective-permute-start.1) | collective-permute-done | bytes 65568 | tf_op jit(solution)/shard_map/ppermute | solution.py:216
  54.4 2.2 %collective-permute-start.2 = (bf16[5,48,256]{2,1,0:T(8,128)(2,1)S(1)}, bf16[5,48,256]{2,1,0:T(8,128)(2,1)S(1)}, u32[]{:S(2)}, u32[]{:S(2)}) collective-permute-start(bf16[5,48,256]{2,1,0:T(8,128)(2,1)S(1)} %get-tuple-element.17), channel_id=1, source_target_pairs={{0,32},{4,36},{8,40},{12,44},{16,48},{20,52},{24,56},{28,60},{32,6... | collective-permute-start | bytes 368648 | tf_op jit(solution)/shard_map/ppermute | solution.py:216
  56.6 3.1 %collective-permute-start.3 = (bf16[5,48,256]{2,1,0:T(8,128)(2,1)S(1)}, bf16[5,48,256]{2,1,0:T(8,128)(2,1)S(1)}, u32[]{:S(2)}, u32[]{:S(2)}) collective-permute-start(bf16[5,48,256]{2,1,0:T(8,128)(2,1)S(1)} %get-tuple-element.16), channel_id=1, source_target_pairs={{32,0},{36,4},{40,8},{44,12},{48,16},{52,20},{56,24},{60,28},{64,3... | collective-permute-start | bytes 368648 | tf_op jit(solution)/shard_map/ppermute | solution.py:216
  60.4 1.9 %collective-permute-done.3.south = bf16[5,48,256]{2,1,0:T(8,128)(2,1)S(1)} collective-permute-done((bf16[5,48,256]{2,1,0:T(8,128)(2,1)S(1)}, bf16[5,48,256]{2,1,0:T(8,128)(2,1)S(1)}, u32[]{:S(2)}, u32[]{:S(2)}) %collective-permute-start.3) | collective-permute-done | bytes 122912 | tf_op jit(solution)/shard_map/ppermute | solution.py:216
  62.3 0.9 copy-done.8
  63.2 5.2 %shard_map.167 = (f32[512,256]{1,0:T(8,128)S(1)}, bf16[512,256]{1,0:T(8,128)(2,1)S(1)}, bf16[16,256]{1,0:T(8,128)(2,1)S(1)}) custom-call(s32[3]{0:T(128)S(1)} %pad_add_fusion.place, bf16[5,48,256]{2,1,0:T(8,128)(2,1)S(1)} %collective-permute-done.2.north, bf16[5,48,256]{2,1,0:T(8,128)(2,1)S(1)} %collective-permute-done.3.south, ...), custom_call_target="tpu_custom_call" | custom-call | tf_op jit(solution)/shard_map/pallas_call | solution.py:158
  68.4 0.8 copy-done.4
  69.3 1.0 pad_maximum_fusion
  70.3 11.4 %all-to-all-start.1 = ((bf16[128,4,384]{2,1,0:T(4,128)(2,1)}), bf16[128,4,384]{2,1,0:T(4,128)(2,1)S(1)}, u32[]{:S(2)}, u32[]{:S(2)}) async-start(bf16[128,4,384]{2,1,0:T(4,128)(2,1)} %pad_maximum_fusion), calls=%async_computation.1 | async-start | bytes 786432 | tf_op jit(solution)/shard_map/all_to_all | solution.py:308
  81.9 9.7 %all-gather.1 = bf16[4,4,512]{2,1,0:T(4,128)(2,1)S(1)} all-gather(bf16[1,4,512]{2,1,0:T(4,128)(2,1)S(1)} %fusion.2), channel_id=2, replica_groups=mesh['space'=128,'lead'=4] {'lead'}, dimensions={0}, use_global_device_ids=true | all-gather | bytes 20480 | tf_op jit(solution)/shard_map/all_gather | solution.py:244
  92.0 17.8 %all-to-all-done.1 = bf16[128,4,384]{2,1,0:T(4,128)(2,1)S(1)} async-done(((bf16[128,4,384]{2,1,0:T(4,128)(2,1)}), bf16[128,4,384]{2,1,0:T(4,128)(2,1)S(1)}, u32[]{:S(2)}, u32[]{:S(2)}) %all-to-all-start.1) | async-done | bytes 393248 | tf_op jit(solution)/shard_map/all_to_all | solution.py:308
  110.2 3.4 %shard_map.168 = (bf16[512,256]{1,0:T(8,128)(2,1)}, bf16[256,256]{1,0:T(8,128)(2,1)}) custom-call(s32[3]{0:T(128)S(1)} %pad_add_fusion.place, bf16[512,256]{1,0:T(8,128)(2,1)S(1)} %reshape.230.slots, bf16[256,256]{1,0:T(8,128)(2,1)S(1)} %reshape.231.coarse_in, bf16[3,768,256]{2,1,0:T(8,128)(2,1)S(1)} %bitcast.28, bf16[4,256]{1,0:T(4,128)(2,1)S(1)} %copy-done.10, ...), custom_call_target="tpu_custom_call" | custom-call | tf_op jit(solution)/shard_map/pallas_call | solution.py:158
  (70 shorter events, 3.1 us)
Async XLA Ops:
  0.6 81.0 %copy-start = (bf16[180,512]{1,0:T(8,128)(2,1)S(1)}, bf16[180,512]{1,0:T(8,128)(2,1)}, u32[]{:S(2)}) copy-start(bf16[180,512]{1,0:T(8,128)(2,1)} %param.25) | copy-start | bytes 552964
  0.6 2.9 %copy-start.12 = (bf16[256,128]{1,0:T(8,128)(2,1)S(1)}, bf16[256,128]{1,0:T(8,128)(2,1)}, u32[]{:S(2)}) copy-start(bf16[256,128]{1,0:T(8,128)(2,1)} %param.17) | copy-start | bytes 196612
  4.2 40.5 %copy-start.15 = (bf16[128,256]{1,0:T(8,128)(2,1)S(1)}, bf16[128,256]{1,0:T(8,128)(2,1)}, u32[]{:S(2)}) copy-start(bf16[128,256]{1,0:T(8,128)(2,1)} %param.20) | copy-start | bytes 196612
  5.0 39.3 %all-to-all-start = ((bf16[128,2,384]{2,1,0:T(2,128)(2,1)}), bf16[128,2,384]{2,1,0:T(2,128)(2,1)S(1)}, u32[]{:S(2)}, u32[]{:S(2)}) async-start(bf16[128,2,384]{2,1,0:T(2,128)(2,1)} %reshape.224), calls=%async_computation | async-start | bytes 393216 | tf_op jit(solution)/shard_map/all_to_all | solution.py:273
  24.5 20.8 %copy-start.13 = (bf16[1,16,32,256]{3,2,1,0:T(8,128)(2,1)S(1)}, bf16[1,16,32,256]{3,2,1,0:T(8,128)(2,1)}, u32[]{:S(2)}) copy-start(bf16[1,16,32,256]{3,2,1,0:T(8,128)(2,1)} %param.16) | copy-start | bytes 786436
  45.3 17.0 %copy-start.2 = (bf16[3,3,256,256]{3,2,1,0:T(8,128)(2,1)S(1)}, bf16[3,3,256,256]{3,2,1,0:T(8,128)(2,1)}, u32[]{:S(2)}) copy-start(bf16[3,3,256,256]{3,2,1,0:T(8,128)(2,1)} %param.22) | copy-start | bytes 3538948
  45.4 16.9 %copy-start.1 = (bf16[3,3,256,256]{3,2,1,0:T(8,128)(2,1)S(1)}, bf16[3,3,256,256]{3,2,1,0:T(8,128)(2,1)}, u32[]{:S(2)}) copy-start(bf16[3,3,256,256]{3,2,1,0:T(8,128)(2,1)} %param.21) | copy-start | bytes 3538948
  45.4 16.9 %copy-start.9 = (bf16[32,384]{1,0:T(8,128)(2,1)S(1)}, bf16[32,384]{1,0:T(8,128)(2,1)}, u32[]{:S(2)}) copy-start(bf16[32,384]{1,0:T(8,128)(2,1)} %constant.145.pool_fine) | copy-start | bytes 73732
  45.4 16.9 %copy-start.10 = (bf16[4,256]{1,0:T(4,128)(2,1)S(1)}, bf16[4,256]{1,0:T(4,128)(2,1)}, u32[]{:S(2)}) copy-start(bf16[4,256]{1,0:T(4,128)(2,1)} %gains.3) | copy-start | bytes 6148
  45.4 16.9 %copy-start.11 = (bf16[16,64]{1,0:T(8,128)(2,1)S(1)}, bf16[16,64]{1,0:T(8,128)(2,1)}, u32[]{:S(2)}) copy-start(bf16[16,64]{1,0:T(8,128)(2,1)} %constant.146.pool_mid) | copy-start | bytes 6148
  46.1 6.4 %collective-permute-start = (bf16[16,8,256]{2,1,0:T(8,128)(2,1)}, bf16[16,8,256]{2,1,0:T(8,128)(2,1)S(1)}, u32[]{:S(2)}, u32[]{:S(2)}) collective-permute-start(bf16[16,8,256]{2,1,0:T(8,128)(2,1)} %get-tuple-element.18), channel_id=1, source_target_pairs={{0,4},{4,8},{8,12},{12,16},{16,20},{20,24},{24,28},{32,36},{36,40}... | collective-permute-start | bytes 196616 | tf_op jit(solution)/shard_map/ppermute | solution.py:216
  48.6 5.8 %collective-permute-start.1 = (bf16[16,8,256]{2,1,0:T(8,128)(2,1)}, bf16[16,8,256]{2,1,0:T(8,128)(2,1)S(1)}, u32[]{:S(2)}, u32[]{:S(2)}) collective-permute-start(bf16[16,8,256]{2,1,0:T(8,128)(2,1)} %get-tuple-element.19), channel_id=1, source_target_pairs={{4,0},{8,4},{12,8},{16,12},{20,16},{24,20},{28,24},{36,32},{40,36}... | collective-permute-start | bytes 196616 | tf_op jit(solution)/shard_map/ppermute | solution.py:216
  54.4 5.9 %collective-permute-start.2 = (bf16[5,48,256]{2,1,0:T(8,128)(2,1)S(1)}, bf16[5,48,256]{2,1,0:T(8,128)(2,1)S(1)}, u32[]{:S(2)}, u32[]{:S(2)}) collective-permute-start(bf16[5,48,256]{2,1,0:T(8,128)(2,1)S(1)} %get-tuple-element.17), channel_id=1, source_target_pairs={{0,32},{4,36},{8,40},{12,44},{16,48},{20,52},{24,56},{28,60},{32,6... | collective-permute-start | bytes 368648 | tf_op jit(solution)/shard_map/ppermute | solution.py:216
  56.6 5.6 %collective-permute-start.3 = (bf16[5,48,256]{2,1,0:T(8,128)(2,1)S(1)}, bf16[5,48,256]{2,1,0:T(8,128)(2,1)S(1)}, u32[]{:S(2)}, u32[]{:S(2)}) collective-permute-start(bf16[5,48,256]{2,1,0:T(8,128)(2,1)S(1)} %get-tuple-element.16), channel_id=1, source_target_pairs={{32,0},{36,4},{40,8},{44,12},{48,16},{52,20},{56,24},{60,28},{64,3... | collective-permute-start | bytes 368648 | tf_op jit(solution)/shard_map/ppermute | solution.py:216
  62.3 0.9 copy-start.8
  68.4 0.8 copy-start.4
  69.2 12.5 %copy-start.16 = (s32[4]{0:T(128)S(1)}, s32[4]{0:T(128)}, u32[]{:S(2)}) copy-start(s32[4]{0:T(128)} %param.26) | copy-start | bytes 52
  69.2 22.5 %copy-start.14 = (s32[256,1]{0,1:T(1,128)S(1)}, s32[256,1]{0,1:T(1,128)}, u32[]{:S(2)}) copy-start(s32[256,1]{0,1:T(1,128)} %param.18) | copy-start | bytes 3076
  70.3 39.5 %all-to-all-start.1 = ((bf16[128,4,384]{2,1,0:T(4,128)(2,1)}), bf16[128,4,384]{2,1,0:T(4,128)(2,1)S(1)}, u32[]{:S(2)}, u32[]{:S(2)}) async-start(bf16[128,4,384]{2,1,0:T(4,128)(2,1)} %pad_maximum_fusion), calls=%async_computation.1 | async-start | bytes 786432 | tf_op jit(solution)/shard_map/all_to_all | solution.py:308
  91.7 18.5 %copy-start.3 = (bf16[3,3,256,256]{3,2,1,0:T(8,128)(2,1)S(1)}, bf16[3,3,256,256]{3,2,1,0:T(8,128)(2,1)}, u32[]{:S(2)}) copy-start(bf16[3,3,256,256]{3,2,1,0:T(8,128)(2,1)} %param.23) | copy-start | bytes 3538948
  91.7 18.5 %copy-start.5 = (f32[512,256]{1,0:T(8,128)S(1)}, f32[512,256]{1,0:T(8,128)}, u32[]{:S(2)}) copy-start(f32[512,256]{1,0:T(8,128)} %copy-done.4) | copy-start | bytes 1572868
  91.7 18.5 %copy-start.6 = (bf16[256,256]{1,0:T(8,128)(2,1)S(1)}, bf16[256,256]{1,0:T(8,128)(2,1)}, u32[]{:S(2)}) copy-start(bf16[256,256]{1,0:T(8,128)(2,1)} %out_proj.1) | copy-start | bytes 393220
  91.7 18.5 %copy-start.7 = (bf16[256,256]{1,0:T(8,128)(2,1)S(1)}, bf16[256,256]{1,0:T(8,128)(2,1)}, u32[]{:S(2)}) copy-start(bf16[256,256]{1,0:T(8,128)(2,1)} %projector.1) | copy-start | bytes 393220

commit v3 on v2

v3 whole, which is shorter than its diff:
```python
import jax
import jax.numpy as jnp
import numpy as np
from jax import lax
from jax.experimental import pallas as pl
from jax.experimental.pallas import tpu as pltpu
from jax.sharding import PartitionSpec as P

TILE_COLS = 8
TILE_H, TILE_W, DEPTH = 16, 32, 256
CELLS = TILE_H * TILE_W
EPS = 1e-06
HALO = 5
SIDE = 8
FRAME_H, FRAME_W = TILE_H + 2 * HALO, TILE_W + 2 * SIDE
ENC_H = FRAME_H - 2
BAND = 24
MID_W = 16
F32 = jnp.float32
BF16 = jnp.bfloat16


def dot(a, b):
    return jnp.dot(a, b, preferred_element_type=F32)


def silu(v):
    return v / (1.0 + jnp.exp(-v))


def rms_scale(values, gain):
    mean_sq = jnp.mean(values * values, axis=-1, keepdims=True)
    return values * lax.rsqrt(mean_sq + EPS) * gain


def column(shape):
    return lax.broadcasted_iota(jnp.int32, shape, 1)


def line(shape):
    return lax.broadcasted_iota(jnp.int32, shape, 0)


def ones_where(condition):
    return condition.astype(F32).astype(BF16)


def pool_fine_matrix():
    q = np.arange(BAND * FRAME_W)
    y, x = q // FRAME_W, q % FRAME_W
    rows = np.arange(BAND // 4 * MID_W)[:, None]
    hit = (y // 4 == rows // MID_W) & (x // 4 - 1 == rows % MID_W) & (rows % MID_W < 10)
    return jnp.asarray(hit, BF16) / 16


def pack_kernel(dest_ref, pixel_ref, obs, payload, key_ref):
    count, readings = obs.shape
    pairs = payload.shape[0]
    dest = dest_ref[...]
    hot = (line((pairs // 2, count)) == dest).astype(F32)
    earlier = ones_where(line((count, count)) < column((count, count)))
    prior = dot(hot.astype(BF16), earlier)
    position = jnp.sum(prior * hot, axis=0, keepdims=True).astype(jnp.int32)
    key = dest * 2 + (position & 1) + pairs * (position >> 1)
    key_ref[...] = key
    pixel = pixel_ref[...]
    lane = column((pairs, readings))
    places = jnp.zeros((pairs, readings), jnp.int32)
    for half in range(2):
        match = line((pairs, count)) + half * pairs == key
        sent = dot(ones_where(match), obs[...])
        payload[:, half * readings : (half + 1) * readings] = sent.astype(BF16)
        at = jnp.sum(jnp.where(match, pixel, 0), axis=1, keepdims=True)
        places = jnp.where(lane == 2 * half, at >> 4, places)
        places = jnp.where(lane == 2 * half + 1, at & 15, places)
    payload[:, 2 * readings :] = places.astype(F32).astype(BF16)


def inject_kernel(arrived, embed, tiles, own, first_cols, last_cols, first_rows, last_rows):
    pairs = arrived.shape[0]
    readings = embed.shape[0]
    sort, lane = line((8, readings)), column((8, readings))
    weights = jnp.where(lane == 2 * sort, 16.0, jnp.where(lane == 2 * sort + 1, 1.0, 0.0))
    weights = jnp.where(sort < 2, weights, 0.0).astype(BF16)
    pixels = lax.dot_general(
        weights,
        arrived[:, 2 * readings :],
        (((1,), (1,)), ((), ())),
        preferred_element_type=F32,
    ).astype(jnp.int32)
    fine = tiles[...].astype(F32)
    for half in range(2):
        embedded = dot(arrived[:, half * readings : (half + 1) * readings], embed[...])
        hot = ones_where(line((CELLS, pairs)) == pixels[half : half + 1])
        fine += dot(hot, embedded.astype(BF16))
    fine = fine.reshape(TILE_H, TILE_W, DEPTH)
    own[...] = fine
    first_cols[...] = fine[:, :SIDE].astype(BF16)
    last_cols[...] = fine[:, -SIDE:].astype(BF16)
    first_rows[...] = fine[:HALO].astype(BF16)
    last_rows[...] = fine[-HALO:].astype(BF16)


def trunk_kernel(
    place, north, south, west, east, own, conv_fine, conv_mid, gains, pool_fine, arrived,
    partial_ref, parcel,
    frame, taps, enc, mid_in, mid_taps, held, sent,
):
    frame[:HALO] = north[...].astype(F32)
    frame[HALO + TILE_H :] = south[...].astype(F32)
    frame[HALO : HALO + TILE_H, :SIDE] = west[...].astype(F32)
    frame[HALO : HALO + TILE_H, SIDE : SIDE + TILE_W] = own[...]
    frame[HALO : HALO + TILE_H, SIDE + TILE_W :] = east[...].astype(F32)
    gain = gains[0:1].astype(F32)
    for y in range(FRAME_H):
        normed = rms_scale(frame[y], gain)
        rows = slice(y * FRAME_W, (y + 1) * FRAME_W)
        taps[rows, :DEPTH] = pltpu.roll(normed, 1, 0).astype(BF16)
        taps[rows, DEPTH : 2 * DEPTH] = normed.astype(BF16)
        taps[rows, 2 * DEPTH :] = pltpu.roll(normed, FRAME_W - 1, 0).astype(BF16)
    size = BAND * FRAME_W
    mid_size = BAND // 4 * MID_W
    for band in range(ENC_H // BAND):
        first = band * BAND
        conv = 0.0
        for dy in range(3):
            start = (first + dy) * FRAME_W
            conv += dot(taps[start : start + size], conv_fine[dy])
        rows = frame[first + 1 : first + 1 + BAND].reshape(size, DEPTH)
        done = (rows + silu(conv)).astype(BF16)
        enc[first : first + BAND] = done.astype(F32).reshape(BAND, FRAME_W, DEPTH)
        mid_in[band * mid_size : (band + 1) * mid_size] = dot(pool_fine[...], done)

    mid = mid_in[...]
    normed = rms_scale(mid, gains[1:2].astype(F32))
    at = line(mid.shape)
    row = place[0] * (TILE_H // 4) - 1 + at // MID_W
    col = place[1] * (TILE_W // 4) - 1 + at % MID_W
    inside = (row >= 0) & (row < place[2] * (TILE_H // 4))
    inside = inside & (col >= 0) & (col < TILE_COLS * (TILE_W // 4))
    normed = jnp.where(inside, normed, 0.0)
    mid_taps[:, :DEPTH] = pltpu.roll(normed, 1, 0).astype(BF16)
    mid_taps[:, DEPTH : 2 * DEPTH] = normed.astype(BF16)
    mid_taps[:, 2 * DEPTH :] = pltpu.roll(normed, mid.shape[0] - 1, 0).astype(BF16)
    conv = 0.0
    for dy in range(3):
        conv += dot(mid_taps[dy * MID_W : (dy + 4) * MID_W], conv_mid[dy])
    enc_mid = mid[MID_W : 5 * MID_W] + silu(conv)
    high = enc_mid.astype(BF16)
    low = (enc_mid - high.astype(F32)).astype(BF16)

    shape = (CELLS, 4 * MID_W)
    cell = line(shape)
    spread = (cell >> 7) * MID_W + ((cell & (TILE_W - 1)) >> 2) + 1
    spread = ones_where(column(shape) == spread)
    centre = enc[HALO - 1 : HALO - 1 + TILE_H, SIDE : SIDE + TILE_W]
    partial = centre.reshape(CELLS, DEPTH) + (dot(spread, high) + dot(spread, low))
    held[...] = partial
    copy = pltpu.make_async_copy(held, partial_ref, sent)
    copy.start()

    x = column((16, 4 * MID_W)) % MID_W - 1
    pool = (x >= 0) & (x < 8) & ((x >> 2) == line((16, 4 * MID_W)))
    pool = jnp.where(pool, 1.0 / 16, 0.0).astype(BF16)
    coarse = dot(pool, high) + dot(pool, low)
    pairs, readings = arrived.shape[0], arrived.shape[1] // 3
    partial = partial.astype(BF16)
    for half in range(2):
        at = 2 * readings + 2 * half
        pixel = arrived[:, at : at + 1].astype(F32) * 16 + arrived[:, at + 1 : at + 2].astype(F32)
        hot = ones_where(column((pairs, CELLS)) == pixel.astype(jnp.int32))
        parcel[:, half * DEPTH : (half + 1) * DEPTH] = dot(hot, partial).astype(BF16)
    even = line((pairs, DEPTH)) % 2 == 0
    parcel[:, 2 * DEPTH :] = jnp.where(even, coarse[0:1], coarse[1:2]).astype(BF16)
    copy.wait()


def tail_kernel(
    place, returned, conv_coarse, gains, partial_ref, film, pick, out_proj, projector,
    maps_ref, scores_ref,
    taps, partial, maps, scores, sems,
):
    fetch = pltpu.make_async_copy(partial_ref, partial, sems.at[0])
    fetch.start()
    cells, wide = returned.shape[0], TILE_COLS * 2
    coarse = returned[:, 2 * DEPTH :].astype(F32)
    normed = rms_scale(coarse, gains[2:3].astype(F32))
    col = line(coarse.shape) % wide
    taps[:wide] = jnp.zeros((wide, 3 * DEPTH), BF16)
    taps[wide + cells :] = jnp.zeros((wide, 3 * DEPTH), BF16)
    inner = slice(wide, wide + cells)
    left, right = pltpu.roll(normed, 1, 0), pltpu.roll(normed, cells - 1, 0)
    taps[inner, :DEPTH] = jnp.where(col == 0, 0.0, left).astype(BF16)
    taps[inner, DEPTH : 2 * DEPTH] = normed.astype(BF16)
    taps[inner, 2 * DEPTH :] = jnp.where(col == wide - 1, 0.0, right).astype(BF16)
    conv = 0.0
    for dy in range(3):
        conv += dot(taps[dy * wide : dy * wide + cells], conv_coarse[dy])
    context = coarse + silu(conv)
    high = context.astype(BF16)
    low = (context - high.astype(F32)).astype(BF16)

    gain = gains[3:4].astype(F32)
    scale, shift = 1.0 + film[0:1], film[1:2]

    def decode(values):
        hidden = rms_scale(values, gain) * scale + shift
        return (values + dot(silu(hidden).astype(BF16), out_proj[...])).astype(BF16)

    here = place[0] * wide + place[1] * 2 + ((line((CELLS, cells)) & (TILE_W - 1)) >> 4)
    mine = ones_where(column((CELLS, cells)) == here)
    spread = dot(mine, high) + dot(mine, low)
    fetch.wait()
    maps[...] = decode(partial[...] + spread)
    put_maps = pltpu.make_async_copy(maps, maps_ref, sems.at[1])
    put_maps.start()

    at_stations = dot(pick[:, 2 * cells :], high) + dot(pick[:, 2 * cells :], low)
    for half in range(2):
        found = returned[:, half * DEPTH : (half + 1) * DEPTH]
        at_stations += dot(pick[:, half * cells : (half + 1) * cells], found)
    scores[...] = dot(decode(at_stations), projector[...]).astype(BF16)
    put_scores = pltpu.make_async_copy(scores, scores_ref, sems.at[2])
    put_scores.start()
    put_maps.wait()
    put_scores.wait()


def call(kernel, outs, scratch, operands, anywhere=(), scalars=0):
    vmem = pl.BlockSpec(memory_space=pltpu.VMEM)
    smem = pl.BlockSpec(memory_space=pltpu.SMEM)
    hbm = pl.BlockSpec(memory_space=pl.ANY)
    ins = [smem if i < scalars else vmem for i in range(len(operands))]
    return pl.pallas_call(
        kernel,
        out_shape=[jax.ShapeDtypeStruct(shape, dtype) for shape, dtype in outs],
        in_specs=[hbm if ("in", i) in anywhere else spec for i, spec in enumerate(ins)],
        out_specs=[hbm if ("out", i) in anywhere else vmem for i in range(len(outs))],
        scratch_shapes=scratch,
        compiler_params=pltpu.CompilerParams(vmem_limit_bytes=32 * 2**20),
    )(*operands)


def pack(dest, pixel, obs, space_count):
    count, readings = obs.shape
    return call(
        pack_kernel,
        [((2 * space_count, 3 * readings), BF16), ((1, count), jnp.int32)],
        [],
        [dest, pixel, obs],
    )


def inject(arrived, embed, tiles):
    return call(
        inject_kernel,
        [
            ((TILE_H, TILE_W, DEPTH), F32),
            ((TILE_H, SIDE, DEPTH), BF16),
            ((TILE_H, SIDE, DEPTH), BF16),
            ((HALO, TILE_W, DEPTH), BF16),
            ((HALO, TILE_W, DEPTH), BF16),
        ],
        [],
        [arrived, embed, tiles],
    )


def trunk(place, north, south, west, east, own, conv_fine, conv_mid, gains, arrived):
    return call(
        trunk_kernel,
        [((CELLS, DEPTH), F32), ((arrived.shape[0], 3 * DEPTH), BF16)],
        [
            pltpu.VMEM((FRAME_H, FRAME_W, DEPTH), F32),
            pltpu.VMEM((FRAME_H * FRAME_W, 3 * DEPTH), BF16),
            pltpu.VMEM((ENC_H, FRAME_W, DEPTH), F32),
            pltpu.VMEM((ENC_H // 4 * MID_W, DEPTH), F32),
            pltpu.VMEM((ENC_H // 4 * MID_W, 3 * DEPTH), BF16),
            pltpu.VMEM((CELLS, DEPTH), F32),
            pltpu.SemaphoreType.DMA,
        ],
        [
            place, north, south, west, east, own,
            conv_fine.reshape(3, 3 * DEPTH, DEPTH),
            conv_mid.reshape(3, 3 * DEPTH, DEPTH),
            gains, pool_fine_matrix(), arrived,
        ],
        anywhere=[("out", 0)],
        scalars=1,
    )


def tail(place, returned, conv_coarse, gains, partial, film, pick, out_proj, projector):
    cells = returned.shape[0]
    outs = [((CELLS, DEPTH), BF16), ((pick.shape[0], projector.shape[1]), BF16)]
    return call(
        tail_kernel,
        outs,
        [
            pltpu.VMEM((cells + 4 * TILE_COLS, 3 * DEPTH), BF16),
            pltpu.VMEM((CELLS, DEPTH), F32),
            *[pltpu.VMEM(shape, dtype) for shape, dtype in outs],
            pltpu.SemaphoreType.DMA((3,)),
        ],
        [
            place, returned, conv_coarse.reshape(3, 3 * DEPTH, DEPTH), gains,
            partial, film, pick, out_proj, projector,
        ],
        anywhere=[("in", 4), ("out", 0), ("out", 1)],
        scalars=1,
    )


def shifted(value, row_step, col_step):
    count = lax.axis_size("space")
    pairs = []
    for source in range(count):
        row, col = source // TILE_COLS + row_step, source % TILE_COLS + col_step
        if 0 <= row < count // TILE_COLS and 0 <= col < TILE_COLS:
            pairs.append((source, row * TILE_COLS + col))
    return lax.ppermute(value, "space", pairs)


def body(
    tiles,
    station_obs,
    station_tile,
    station_pixel,
    station_embed,
    conv_fine,
    conv_mid,
    conv_coarse,
    norm_gains,
    film_table,
    horizon_step_list,
    out_proj,
    gauge_bin_projector,
):
    space_count = lax.axis_size("space")
    count, readings = station_obs.shape
    space_at = lax.axis_index("space")
    place = jnp.stack(
        [space_at // TILE_COLS, space_at % TILE_COLS, jnp.int32(space_count // TILE_COLS)]
    ).astype(jnp.int32)

    table_rows = film_table.shape[0]
    own_rows = lax.axis_index("lead") * table_rows + jnp.arange(table_rows, dtype=jnp.int32)
    lead_hot = (horizon_step_list[:, None] == own_rows[None, :]).astype(BF16)
    film_parts = lax.all_gather(dot(lead_hot, film_table).astype(BF16), "lead")
    film = jnp.sum(film_parts.astype(F32), axis=0)
    film = lax.dynamic_slice_in_dim(film, lax.axis_index("lead"), 1, 0).reshape(2, DEPTH)

    dest = station_tile.reshape(1, count)
    pixel = station_pixel.reshape(1, count)
    payload, key = pack(dest, pixel, station_obs, space_count)
    arrived = lax.all_to_all(
        payload.reshape(space_count, 2, 3 * readings), "space", 0, 0, tiled=True
    ).reshape(2 * space_count, 3 * readings)
    own, first_cols, last_cols, first_rows, last_rows = inject(
        arrived, station_embed, tiles.reshape(CELLS, DEPTH)
    )

    west = shifted(last_cols, 0, 1)
    east = shifted(first_cols, 0, -1)

    def widened(rows, side):
        return jnp.concatenate([west[side], rows, east[side]], axis=1)

    north = shifted(widened(last_rows, slice(-HALO, None)), 1, 0)
    south = shifted(widened(first_rows, slice(0, HALO)), -1, 0)

    partial, parcel = trunk(
        place, north, south, west, east, own, conv_fine, conv_mid, norm_gains, arrived
    )
    returned = lax.all_to_all(
        parcel.reshape(space_count, 2, 3 * DEPTH), "space", 0, 0, tiled=True
    ).reshape(2 * space_count, 3 * DEPTH)

    coarse_at = (dest // TILE_COLS) * (TILE_COLS * 2) + (dest % TILE_COLS) * 2
    coarse_at = coarse_at + (pixel % TILE_W) // (TILE_W // 2) + 4 * space_count
    rows = jnp.arange(6 * space_count, dtype=jnp.int32)[None, :]
    pick = ((key.reshape(count, 1) == rows) | (coarse_at.reshape(count, 1) == rows)).astype(BF16)
    maps, scores = tail(
        place, returned, conv_coarse, norm_gains, partial, film, pick,
        out_proj, gauge_bin_projector,
    )
    return maps.reshape(1, 1, TILE_H, TILE_W, DEPTH), scores.reshape(1, count, -1)


def solution(mesh):
    in_specs = (
        P("space", None, None, None),
        P("space", None),
        P("space", None),
        P("space"),
        P(),
        P(),
        P(),
        P(),
        P(),
        P("lead", None),
        P(),
        P(),
        P(),
    )
    out_specs = (P("lead", "space", None, None, None), P("lead", "space", None))
    return jax.shard_map(body, mesh=mesh, in_specs=in_specs, out_specs=out_specs, check_vma=False)
```

time: 114 us -> 115 us (level)
  the two profiles are of different devices: /device:TPU:35 before, /device:TPU:39 now
where the time goes in v3:
time: 115 us; the launch traced here: 114 us
  blocking collectives  48.9 us (43%)
  waiting for transfers between devices  24.3 us (21%)
  starting transfers between devices  20.9 us (18%)
  Pallas kernels  9.64 us (8%)
  local copies, waits for them, and re-layouts  8.02 us (7%)
  other arithmetic  1.6 us (1%)
    all_to_all x1, blocking collectives, body(): lax.all_to_all(payload.reshape(space_count, 2, 3 * readings), 'space', 0,...  39.2 us
    all_to_all x1, waiting for transfers between devices, body(): lax.all_to_all(parcel.reshape(space_count, 2, 3 * DEPTH), 'space', 0, 0,...  18 us
    all_to_all x1, starting transfers between devices, body(): lax.all_to_all(parcel.reshape(space_count, 2, 3 * DEPTH), 'space', 0, 0,...  11.3 us
    all_gather x1, blocking collectives, body(): film_parts = lax.all_gather(dot(lead_hot, film_table).astype(BF16), 'lead')  9.66 us
    pallas_call x4, Pallas kernels, call(): pl.pallas_call(kernel, out_shape=[jax.ShapeDtypeStruct(shape, dtype) for...  9.64 us
    ppermute x4, starting transfers between devices, shifted(): return lax.ppermute(value, 'space', pairs)  9.59 us
    ppermute x4, waiting for transfers between devices, shifted(): return lax.ppermute(value, 'space', pairs)  6.27 us
    unnamed x38, local copies, waits for them, and re-layouts  5.72 us
  transfers between devices with their start and end apart: 5, of which 4 were waited for; matrix products, arithmetic and copies ran while one was open for 1% of the time, Pallas kernels for 0%

profile of v3, /device:TPU:39, one launch (start us, length us, event | category | flops | bytes accessed | tf_op | source)
XLA Modules:
  0.0 114.4 jit_solution(4558473955094858450)
XLA Ops:
  0.7 0.9 copy-done.11
  1.5 0.7 copy-done.14
  2.2 0.7 copy-done.16
  2.9 0.4 shard_map.149
  3.4 39.2 %all_to_all.10 = bf16[128,2,384]{2,1,0:T(2,128)(2,1)S(1)} all-to-all(bf16[128,2,384]{2,1,0:T(2,128)(2,1)S(1)} %reshape.118), channel_id=1, replica_groups=mesh['space'=128,'lead'=4] {'space'}, dimensions={0} | all-to-all | bytes 393216 | tf_op jit(solution)/shard_map/all_to_all | solution.py:356
  42.8 0.9 copy-done.7
  43.7 0.8 shard_map.150
  44.5 2.4 %collective-permute-start = (bf16[16,8,256]{2,1,0:T(8,128)(2,1)S(1)}, bf16[16,8,256]{2,1,0:T(8,128)(2,1)S(1)}, u32[]{:S(2)}, u32[]{:S(2)}) collective-permute-start(bf16[16,8,256]{2,1,0:T(8,128)(2,1)S(1)} %get-tuple-element.14), channel_id=1, source_target_pairs={{0,4},{4,8},{8,12},{12,16},{16,20},{20,24},{24,28},{32,36},{36,40}... | collective-permute-start | bytes 196616 | tf_op jit(solution)/shard_map/ppermute | solution.py:321
  46.9 1.9 %collective-permute-start.1 = (bf16[16,8,256]{2,1,0:T(8,128)(2,1)S(1)}, bf16[16,8,256]{2,1,0:T(8,128)(2,1)S(1)}, u32[]{:S(2)}, u32[]{:S(2)}) collective-permute-start(bf16[16,8,256]{2,1,0:T(8,128)(2,1)S(1)} %get-tuple-element.16), channel_id=1, source_target_pairs={{4,0},{8,4},{12,8},{16,12},{20,16},{24,20},{28,24},{36,32},{40,36}... | collective-permute-start | bytes 196616 | tf_op jit(solution)/shard_map/ppermute | solution.py:321
  48.9 3.6 %collective-permute-done.1.east = bf16[16,8,256]{2,1,0:T(8,128)(2,1)S(1)} collective-permute-done((bf16[16,8,256]{2,1,0:T(8,128)(2,1)S(1)}, bf16[16,8,256]{2,1,0:T(8,128)(2,1)S(1)}, u32[]{:S(2)}, u32[]{:S(2)}) %collective-permute-start.1) | collective-permute-done | bytes 65568 | tf_op jit(solution)/shard_map/ppermute | solution.py:321
  52.5 0.7 pad_maximum_fusion.1
  53.1 2.1 %collective-permute-start.3 = (bf16[5,48,256]{2,1,0:T(8,128)(2,1)}, bf16[5,48,256]{2,1,0:T(8,128)(2,1)S(1)}, u32[]{:S(2)}, u32[]{:S(2)}) collective-permute-start(bf16[5,48,256]{2,1,0:T(8,128)(2,1)} %pad_maximum_fusion.1), channel_id=1, source_target_pairs={{32,0},{36,4},{40,8},{44,12},{48,16},{52,20},{56,24},{60,28},{64,3... | collective-permute-start | bytes 368648 | tf_op jit(solution)/shard_map/ppermute | solution.py:321
  55.2 0.7 pad_maximum_fusion
  55.9 3.2 %collective-permute-start.2 = (bf16[5,48,256]{2,1,0:T(8,128)(2,1)}, bf16[5,48,256]{2,1,0:T(8,128)(2,1)}, u32[]{:S(2)}, u32[]{:S(2)}) collective-permute-start(bf16[5,48,256]{2,1,0:T(8,128)(2,1)} %pad_maximum_fusion), channel_id=1, source_target_pairs={{0,32},{4,36},{8,40},{12,44},{16,48},{20,52},{24,56},{28,60},{32,6... | collective-permute-start | bytes 368648 | tf_op jit(solution)/shard_map/ppermute | solution.py:321
  59.4 2.5 %collective-permute-done.2.north = bf16[5,48,256]{2,1,0:T(8,128)(2,1)} collective-permute-done((bf16[5,48,256]{2,1,0:T(8,128)(2,1)}, bf16[5,48,256]{2,1,0:T(8,128)(2,1)}, u32[]{:S(2)}, u32[]{:S(2)}) %collective-permute-start.2) | collective-permute-done | bytes 122912 | tf_op jit(solution)/shard_map/ppermute | solution.py:321
  61.9 0.9 copy-done.8
  62.8 4.8 %shard_map.151 = (f32[512,256]{1,0:T(8,128)S(1)}, bf16[256,768]{1,0:T(8,128)(2,1)S(1)}) custom-call(s32[3]{0:T(128)S(1)} %pad_add_fusion.place, bf16[5,48,256]{2,1,0:T(8,128)(2,1)} %collective-permute-done.2.north, bf16[5,48,256]{2,1,0:T(8,128)(2,1)S(1)} %collective-permute-done.3.south, bf16[16,8,256]{2,1,0:T(8,128)(2,1)S(1)} %collective-permute-done.west, ...), custom_call_target="tpu_custom_call" | custom-call | tf_op jit(solution)/shard_map/pallas_call | solution.py:234
  67.6 0.8 copy-done.4
  68.4 0.8 copy-done.6
  69.2 1.9 %reshape.123 = bf16[128,2,768]{2,1,0:T(2,128)(2,1)} reshape(bf16[256,768]{1,0:T(8,128)(2,1)} %copy-done.6) | data formatting | bytes 786432 | tf_op jit(solution)/shard_map/reshape | solution.py:376
  71.2 11.3 %all-to-all-start.1 = ((bf16[128,2,768]{2,1,0:T(2,128)(2,1)}), bf16[128,2,768]{2,1,0:T(2,128)(2,1)S(1)}, u32[]{:S(2)}, u32[]{:S(2)}) async-start(bf16[128,2,768]{2,1,0:T(2,128)(2,1)} %reshape.123), calls=%async_computation.1 | async-start | bytes 786432 | tf_op jit(solution)/shard_map/all_to_all | solution.py:375
  82.7 9.7 %all-gather.1 = bf16[4,4,512]{2,1,0:T(4,128)(2,1)S(1)} all-gather(bf16[1,4,512]{2,1,0:T(4,128)(2,1)S(1)} %fusion), channel_id=2, replica_groups=mesh['space'=128,'lead'=4] {'lead'}, dimensions={0}, use_global_device_ids=true | all-gather | bytes 20480 | tf_op jit(solution)/shard_map/all_gather | solution.py:349
  92.7 18.0 %all-to-all-done.1 = bf16[128,2,768]{2,1,0:T(2,128)(2,1)S(1)} async-done(((bf16[128,2,768]{2,1,0:T(2,128)(2,1)}), bf16[128,2,768]{2,1,0:T(2,128)(2,1)S(1)}, u32[]{:S(2)}, u32[]{:S(2)}) %all-to-all-start.1) | async-done | bytes 393248 | tf_op jit(solution)/shard_map/all_to_all | solution.py:375
  110.9 3.6 %shard_map.152 = (bf16[512,256]{1,0:T(8,128)(2,1)}, bf16[256,256]{1,0:T(8,128)(2,1)}) custom-call(s32[3]{0:T(128)S(1)} %pad_add_fusion.place, bf16[256,768]{1,0:T(8,128)(2,1)S(1)} %reshape.124.returned, bf16[3,768,256]{2,1,0:T(8,128)(2,1)S(1)} %bitcast.17, bf16[4,256]{1,0:T(4,128)(2,1)S(1)} %copy-done.13, f32[512,256]{1,0:T(8,128)S(1)} %copy-done.5, ...), custom_call_target="tpu_custom_call" | custom-call | tf_op jit(solution)/shard_map/pallas_call | solution.py:234
  (46 shorter events, 1.1 us)
Async XLA Ops:
  0.6 81.9 %copy-start = (bf16[180,512]{1,0:T(8,128)(2,1)S(1)}, bf16[180,512]{1,0:T(8,128)(2,1)}, u32[]{:S(2)}) copy-start(bf16[180,512]{1,0:T(8,128)(2,1)} %param.23) | copy-start | bytes 552964
  0.6 0.9 copy-start.11
  1.5 0.7 copy-start.14
  2.2 0.7 copy-start.16
  2.9 39.9 %copy-start.12 = (bf16[128,256]{1,0:T(8,128)(2,1)S(1)}, bf16[128,256]{1,0:T(8,128)(2,1)}, u32[]{:S(2)}) copy-start(bf16[128,256]{1,0:T(8,128)(2,1)} %embed.1) | copy-start | bytes 196612
  2.9 59.0 %copy-start.13 = (bf16[4,256]{1,0:T(4,128)(2,1)S(1)}, bf16[4,256]{1,0:T(4,128)(2,1)}, u32[]{:S(2)}) copy-start(bf16[4,256]{1,0:T(4,128)(2,1)} %gains.3) | copy-start | bytes 6148
  3.3 58.5 %copy-start.1 = (bf16[3,3,256,256]{3,2,1,0:T(8,128)(2,1)S(1)}, bf16[3,3,256,256]{3,2,1,0:T(8,128)(2,1)}, u32[]{:S(2)}) copy-start(bf16[3,3,256,256]{3,2,1,0:T(8,128)(2,1)} %param.19) | copy-start | bytes 3538948
  3.3 58.5 %copy-start.2 = (bf16[3,3,256,256]{3,2,1,0:T(8,128)(2,1)S(1)}, bf16[3,3,256,256]{3,2,1,0:T(8,128)(2,1)}, u32[]{:S(2)}) copy-start(bf16[3,3,256,256]{3,2,1,0:T(8,128)(2,1)} %param.20) | copy-start | bytes 3538948
  42.8 1.0 copy-start.7
  44.5 4.3 %collective-permute-start = (bf16[16,8,256]{2,1,0:T(8,128)(2,1)S(1)}, bf16[16,8,256]{2,1,0:T(8,128)(2,1)S(1)}, u32[]{:S(2)}, u32[]{:S(2)}) collective-permute-start(bf16[16,8,256]{2,1,0:T(8,128)(2,1)S(1)} %get-tuple-element.14), channel_id=1, source_target_pairs={{0,4},{4,8},{8,12},{12,16},{16,20},{20,24},{24,28},{32,36},{36,40}... | collective-permute-start | bytes 196616 | tf_op jit(solution)/shard_map/ppermute | solution.py:321
  46.9 5.6 %collective-permute-start.1 = (bf16[16,8,256]{2,1,0:T(8,128)(2,1)S(1)}, bf16[16,8,256]{2,1,0:T(8,128)(2,1)S(1)}, u32[]{:S(2)}, u32[]{:S(2)}) collective-permute-start(bf16[16,8,256]{2,1,0:T(8,128)(2,1)S(1)} %get-tuple-element.16), channel_id=1, source_target_pairs={{4,0},{8,4},{12,8},{16,12},{20,16},{24,20},{28,24},{36,32},{40,36}... | collective-permute-start | bytes 196616 | tf_op jit(solution)/shard_map/ppermute | solution.py:321
  53.1 6.2 %collective-permute-start.3 = (bf16[5,48,256]{2,1,0:T(8,128)(2,1)}, bf16[5,48,256]{2,1,0:T(8,128)(2,1)S(1)}, u32[]{:S(2)}, u32[]{:S(2)}) collective-permute-start(bf16[5,48,256]{2,1,0:T(8,128)(2,1)} %pad_maximum_fusion.1), channel_id=1, source_target_pairs={{32,0},{36,4},{40,8},{44,12},{48,16},{52,20},{56,24},{60,28},{64,3... | collective-permute-start | bytes 368648 | tf_op jit(solution)/shard_map/ppermute | solution.py:321
  55.9 5.9 %collective-permute-start.2 = (bf16[5,48,256]{2,1,0:T(8,128)(2,1)}, bf16[5,48,256]{2,1,0:T(8,128)(2,1)}, u32[]{:S(2)}, u32[]{:S(2)}) collective-permute-start(bf16[5,48,256]{2,1,0:T(8,128)(2,1)} %pad_maximum_fusion), channel_id=1, source_target_pairs={{0,32},{4,36},{8,40},{12,44},{16,48},{20,52},{24,56},{28,60},{32,6... | collective-permute-start | bytes 368648 | tf_op jit(solution)/shard_map/ppermute | solution.py:321
  61.8 0.9 copy-start.8
  67.6 0.8 copy-start.4
  68.4 0.8 copy-start.6
  69.2 13.3 %copy-start.18 = (s32[4]{0:T(128)S(1)}, s32[4]{0:T(128)}, u32[]{:S(2)}) copy-start(s32[4]{0:T(128)} %param.24) | copy-start | bytes 52
  69.2 23.2 %copy-start.15 = (s32[256,1]{0,1:T(1,128)S(1)}, s32[256,1]{0,1:T(1,128)}, u32[]{:S(2)}) copy-start(s32[256,1]{0,1:T(1,128)} %param.16) | copy-start | bytes 3076
  69.2 23.2 %copy-start.17 = (s32[256]{0:T(256)S(1)}, s32[256]{0:T(256)}, u32[]{:S(2)}) copy-start(s32[256]{0:T(256)} %param.17) | copy-start | bytes 3076
  71.2 39.7 %copy-start.3 = (bf16[3,3,256,256]{3,2,1,0:T(8,128)(2,1)S(1)}, bf16[3,3,256,256]{3,2,1,0:T(8,128)(2,1)}, u32[]{:S(2)}) copy-start(bf16[3,3,256,256]{3,2,1,0:T(8,128)(2,1)} %param.21) | copy-start | bytes 3538948
  71.2 39.7 %copy-start.5 = (f32[512,256]{1,0:T(8,128)S(1)}, f32[512,256]{1,0:T(8,128)}, u32[]{:S(2)}) copy-start(f32[512,256]{1,0:T(8,128)} %copy-done.4) | copy-start | bytes 1572868
  71.2 39.7 %copy-start.9 = (bf16[256,256]{1,0:T(8,128)(2,1)S(1)}, bf16[256,256]{1,0:T(8,128)(2,1)}, u32[]{:S(2)}) copy-start(bf16[256,256]{1,0:T(8,128)(2,1)} %out_proj.1) | copy-start | bytes 393220
  71.2 39.7 %copy-start.10 = (bf16[256,256]{1,0:T(8,128)(2,1)S(1)}, bf16[256,256]{1,0:T(8,128)(2,1)}, u32[]{:S(2)}) copy-start(bf16[256,256]{1,0:T(8,128)(2,1)} %projector.1) | copy-start | bytes 393220
  71.2 39.5 %all-to-all-start.1 = ((bf16[128,2,768]{2,1,0:T(2,128)(2,1)}), bf16[128,2,768]{2,1,0:T(2,128)(2,1)S(1)}, u32[]{:S(2)}, u32[]{:S(2)}) async-start(bf16[128,2,768]{2,1,0:T(2,128)(2,1)} %reshape.123), calls=%async_computation.1 | async-start | bytes 786432 | tf_op jit(solution)/shard_map/all_to_all | solution.py:375

commit v4 on v3

v4 whole, which is shorter than its diff:
```python
import functools

import jax
import jax.numpy as jnp
from jax import lax
from jax.experimental import pallas as pl
from jax.experimental.pallas import tpu as pltpu
from jax.sharding import PartitionSpec as P

TILE_COLS = 8
TILE_H, TILE_W, DEPTH = 16, 32, 256
CELLS = TILE_H * TILE_W
EPS = 1e-06
HALO = 5
SIDE = 8
FRAME_H, FRAME_W = TILE_H + 2 * HALO, TILE_W + 2 * SIDE
ENC_H = FRAME_H - 2
MID_W = 16
F32 = jnp.float32
BF16 = jnp.bfloat16


def dot(a, b):
    return jnp.dot(a, b, preferred_element_type=F32)


def silu(v):
    return v / (1.0 + jnp.exp(-v))


def rms_scale(values, gain):
    mean_sq = jnp.mean(values * values, axis=-1, keepdims=True)
    return values * lax.rsqrt(mean_sq + EPS) * gain


def column(shape):
    return lax.broadcasted_iota(jnp.int32, shape, 1)


def line(shape):
    return lax.broadcasted_iota(jnp.int32, shape, 0)


def ones_where(condition):
    return condition.astype(F32).astype(BF16)


def grid_place():
    at = lax.axis_index("space")
    return lax.div(at, TILE_COLS), lax.rem(at, TILE_COLS)


def pack_kernel(ids, obs, payload, lookup):
    count, readings = obs.shape
    pairs = payload.shape[0]
    earlier = ones_where(line((count, count)) < column((count, count)))
    lane = column((pairs, readings))
    dest, pixel = ids[...] // CELLS, ids[...] % CELLS
    hot = (line((pairs // 2, count)) == dest).astype(F32)
    prior = dot(hot.astype(BF16), earlier)
    position = jnp.sum(prior * hot, axis=0, keepdims=True).astype(jnp.int32)
    key = dest * 2 + (position & 1) + pairs * (position >> 1)
    coarse = dest * 2 + ((pixel & (TILE_W - 1)) >> 4)
    sort = line((16, count))
    found = jnp.where(sort == 0, key >> 4, jnp.where(sort == 1, key & 15, 0))
    found = jnp.where(sort == 2, coarse >> 4, jnp.where(sort == 3, coarse & 15, found))
    lookup[...] = found.astype(F32).astype(BF16)
    places = jnp.zeros((pairs, readings), jnp.int32)
    for half in range(2):
        match = line((pairs, count)) + half * pairs == key
        sent = dot(ones_where(match), obs[...])
        payload[:, half * readings : (half + 1) * readings] = sent.astype(BF16)
        at = jnp.sum(jnp.where(match, pixel, 0), axis=1, keepdims=True)
        places = jnp.where(lane == 2 * half, at >> 4, places)
        places = jnp.where(lane == 2 * half + 1, at & 15, places)
    payload[:, 2 * readings :] = places.astype(F32).astype(BF16)


def inject_kernel(
    arrived, embed, tiles, own, first_cols, last_cols, first_rows, last_rows
):
    pairs = arrived.shape[0]
    readings = embed.shape[0]
    weight = embed[...].astype(BF16)
    sort, lane = line((8, readings)), column((8, readings))
    weights = jnp.where(lane == 2 * sort, 16.0, jnp.where(lane == 2 * sort + 1, 1.0, 0.0))
    weights = jnp.where(sort < 2, weights, 0.0).astype(BF16)
    pixels = lax.dot_general(
        weights,
        arrived[:, 2 * readings :],
        (((1,), (1,)), ((), ())),
        preferred_element_type=F32,
    ).astype(jnp.int32)
    fine = 0.0
    for half in range(2):
        embedded = dot(arrived[:, half * readings : (half + 1) * readings], weight)
        hot = ones_where(line((CELLS, pairs)) == pixels[half : half + 1])
        fine += dot(hot, embedded.astype(BF16))
    fine = (fine + tiles[...]).reshape(TILE_H, TILE_W, DEPTH)
    own[...] = fine
    first_cols[...] = fine[:, :SIDE].astype(BF16)
    last_cols[...] = fine[:, -SIDE:].astype(BF16)
    first_rows[...] = fine[:HALO].astype(BF16)
    last_rows[...] = fine[-HALO:].astype(BF16)


def widen_kernel(west, east, first_rows, last_rows, top, bottom):
    for rows, target, side in (
        (first_rows, top, slice(0, HALO)),
        (last_rows, bottom, slice(TILE_H - HALO, TILE_H)),
    ):
        parts = [west[side], rows[...], east[side]]
        whole = jnp.concatenate([part.astype(F32) for part in parts], axis=1)
        target[...] = whole.astype(BF16)


def trunk_kernel(
    image_rows,
    north, south, west, east, own, conv_fine, conv_mid, gains, arrived,
    partial_ref, parcel,
    frame, taps, enc, mid_in, mid_taps,
):
    frame[:HALO] = north[...].astype(F32)
    frame[HALO + TILE_H :] = south[...].astype(F32)
    frame[HALO : HALO + TILE_H, :SIDE] = west[...].astype(F32)
    frame[HALO : HALO + TILE_H, SIDE : SIDE + TILE_W] = own[...]
    frame[HALO : HALO + TILE_H, SIDE + TILE_W :] = east[...].astype(F32)
    gain = gains[0:1].astype(F32)
    for y in range(FRAME_H):
        normed = rms_scale(frame[y], gain)
        rows = slice(y * FRAME_W, (y + 1) * FRAME_W)
        taps[rows, :DEPTH] = pltpu.roll(normed, 1, 0).astype(BF16)
        taps[rows, DEPTH : 2 * DEPTH] = normed.astype(BF16)
        taps[rows, 2 * DEPTH :] = pltpu.roll(normed, FRAME_W - 1, 0).astype(BF16)
    size = ENC_H * FRAME_W
    conv = 0.0
    for dy in range(3):
        conv += dot(taps[dy * FRAME_W : dy * FRAME_W + size], conv_fine[dy])
    done = (frame[1 : 1 + ENC_H].reshape(size, DEPTH) + silu(conv)).astype(BF16)
    enc[...] = done.astype(F32).reshape(ENC_H, FRAME_W, DEPTH)
    group = 4 * FRAME_W
    at = column((MID_W, group))
    x = at - FRAME_W * sum((at >= FRAME_W * i).astype(jnp.int32) for i in range(1, 4))
    pool = ((x >> 2) - 1 == line((MID_W, group))) & (line((MID_W, group)) < 10)
    pool = jnp.where(pool, 1.0 / 16, 0.0).astype(BF16)
    for i in range(ENC_H // 4):
        mid_in[i * MID_W : (i + 1) * MID_W] = dot(pool, done[i * group : (i + 1) * group])

    mid = mid_in[...]
    normed = rms_scale(mid, gains[1:2].astype(F32))
    at = line(mid.shape)
    row_at, col_at = grid_place()
    row = row_at * (TILE_H // 4) - 1 + at // MID_W
    col = col_at * (TILE_W // 4) - 1 + at % MID_W
    inside = (row >= 0) & (row < image_rows * (TILE_H // 4))
    inside = inside & (col >= 0) & (col < TILE_COLS * (TILE_W // 4))
    normed = jnp.where(inside, normed, 0.0)
    mid_taps[:, :DEPTH] = pltpu.roll(normed, 1, 0).astype(BF16)
    mid_taps[:, DEPTH : 2 * DEPTH] = normed.astype(BF16)
    mid_taps[:, 2 * DEPTH :] = pltpu.roll(normed, mid.shape[0] - 1, 0).astype(BF16)
    conv = 0.0
    for dy in range(3):
        conv += dot(mid_taps[dy * MID_W : (dy + 4) * MID_W], conv_mid[dy])
    enc_mid = mid[MID_W : 5 * MID_W] + silu(conv)
    high = enc_mid.astype(BF16)
    low = (enc_mid - high.astype(F32)).astype(BF16)

    shape = (CELLS, 4 * MID_W)
    cell = line(shape)
    spread = (cell >> 7) * MID_W + ((cell & (TILE_W - 1)) >> 2) + 1
    spread = ones_where(column(shape) == spread)
    centre = enc[HALO - 1 : HALO - 1 + TILE_H, SIDE : SIDE + TILE_W]
    partial = centre.reshape(CELLS, DEPTH) + (dot(spread, high) + dot(spread, low))
    partial_ref[...] = partial

    x = column((16, 4 * MID_W)) % MID_W - 1
    pool = (x >= 0) & (x < 8) & ((x >> 2) == line((16, 4 * MID_W)))
    pool = jnp.where(pool, 1.0 / 16, 0.0).astype(BF16)
    coarse = dot(pool, high) + dot(pool, low)
    pairs, readings = arrived.shape[0], arrived.shape[1] // 3
    partial = partial.astype(BF16)
    for half in range(2):
        at = 2 * readings + 2 * half
        pixel = arrived[:, at : at + 1].astype(F32) * 16 + arrived[:, at + 1 : at + 2].astype(F32)
        hot = ones_where(column((pairs, CELLS)) == pixel.astype(jnp.int32))
        parcel[:, half * DEPTH : (half + 1) * DEPTH] = dot(hot, partial).astype(BF16)
    even = line((pairs, DEPTH)) % 2 == 0
    parcel[:, 2 * DEPTH :] = jnp.where(even, coarse[0:1], coarse[1:2]).astype(BF16)


def tail_kernel(
    returned, conv_coarse, gains, partial, film, lookup, out_proj, projector,
    maps_ref, scores_ref,
    taps, maps, scores, sems,
):
    cells, wide = returned.shape[0], TILE_COLS * 2
    coarse = returned[:, 2 * DEPTH :].astype(F32)
    normed = rms_scale(coarse, gains[2:3].astype(F32))
    col = line(coarse.shape) % wide
    taps[:wide] = jnp.zeros((wide, 3 * DEPTH), BF16)
    taps[wide + cells :] = jnp.zeros((wide, 3 * DEPTH), BF16)
    inner = slice(wide, wide + cells)
    left, right = pltpu.roll(normed, 1, 0), pltpu.roll(normed, cells - 1, 0)
    taps[inner, :DEPTH] = jnp.where(col == 0, 0.0, left).astype(BF16)
    taps[inner, DEPTH : 2 * DEPTH] = normed.astype(BF16)
    taps[inner, 2 * DEPTH :] = jnp.where(col == wide - 1, 0.0, right).astype(BF16)
    conv = 0.0
    for dy in range(3):
        conv += dot(taps[dy * wide : dy * wide + cells], conv_coarse[dy])
    context = coarse + silu(conv)
    high = context.astype(BF16)
    low = (context - high.astype(F32)).astype(BF16)

    gain = gains[3:4].astype(F32)
    scale, shift = 1.0 + film[0:1], film[1:2]

    def decode(values):
        hidden = rms_scale(values, gain) * scale + shift
        return (values + dot(silu(hidden).astype(BF16), out_proj[...])).astype(BF16)

    row_at, col_at = grid_place()
    here = row_at * wide + col_at * 2 + ((line((CELLS, cells)) & (TILE_W - 1)) >> 4)
    mine = ones_where(column((CELLS, cells)) == here)
    spread = dot(mine, high) + dot(mine, low)
    maps[...] = decode(partial[...] + spread)
    put_maps = pltpu.make_async_copy(maps, maps_ref, sems.at[0])
    put_maps.start()

    count = lookup.shape[1]
    same = ones_where(line((count, count)) == column((count, count)))
    where = lax.dot_general(
        same, lookup[...], (((1,), (1,)), ((), ())), preferred_element_type=F32
    )
    key = (where[:, 0:1] * 16 + where[:, 1:2]).astype(jnp.int32)
    area = (where[:, 2:3] * 16 + where[:, 3:4]).astype(jnp.int32)
    slot = column((count, cells))
    pick = ones_where(slot == area)
    at_stations = dot(pick, high) + dot(pick, low)
    for half in range(2):
        found = returned[:, half * DEPTH : (half + 1) * DEPTH]
        at_stations += dot(ones_where(slot + half * cells == key), found)
    scores[...] = dot(decode(at_stations), projector[...]).astype(BF16)
    put_scores = pltpu.make_async_copy(scores, scores_ref, sems.at[1])
    put_scores.start()
    put_maps.wait()
    put_scores.wait()


def call(kernel, outs, scratch, operands, hbm_outs=(), megabytes=4):
    vmem = pl.BlockSpec(memory_space=pltpu.VMEM)
    hbm = pl.BlockSpec(memory_space=pltpu.HBM)
    return pl.pallas_call(
        kernel,
        out_shape=[jax.ShapeDtypeStruct(shape, dtype) for shape, dtype in outs],
        in_specs=[vmem] * len(operands),
        out_specs=[hbm if i in hbm_outs else vmem for i in range(len(outs))],
        scratch_shapes=scratch,
        compiler_params=pltpu.CompilerParams(vmem_limit_bytes=megabytes * 2**20),
    )(*operands)


def pack(ids, obs, space_count):
    count, readings = obs.shape
    outs = [((2 * space_count, 3 * readings), BF16), ((16, count), BF16)]
    return call(pack_kernel, outs, [], [ids, obs], megabytes=8)


def inject(arrived, embed, tiles):
    return call(
        inject_kernel,
        [
            ((TILE_H, TILE_W, DEPTH), F32),
            ((TILE_H, SIDE, DEPTH), BF16),
            ((TILE_H, SIDE, DEPTH), BF16),
            ((HALO, TILE_W, DEPTH), BF16),
            ((HALO, TILE_W, DEPTH), BF16),
        ],
        [],
        [arrived, embed, tiles],
        megabytes=8,
    )


def widen(west, east, first_rows, last_rows):
    shape = (HALO, FRAME_W, DEPTH)
    return call(
        widen_kernel, [(shape, BF16), (shape, BF16)], [], [west, east, first_rows, last_rows]
    )


def trunk(image_rows, north, south, west, east, own, conv_fine, conv_mid, gains, arrived):
    return call(
        functools.partial(trunk_kernel, image_rows),
        [((CELLS, DEPTH), F32), ((arrived.shape[0], 3 * DEPTH), BF16)],
        [
            pltpu.VMEM((FRAME_H, FRAME_W, DEPTH), F32),
            pltpu.VMEM((FRAME_H * FRAME_W, 3 * DEPTH), BF16),
            pltpu.VMEM((ENC_H, FRAME_W, DEPTH), F32),
            pltpu.VMEM((ENC_H // 4 * MID_W, DEPTH), F32),
            pltpu.VMEM((ENC_H // 4 * MID_W, 3 * DEPTH), BF16),
        ],
        [
            north, south, west, east, own,
            conv_fine.reshape(3, 3 * DEPTH, DEPTH),
            conv_mid.reshape(3, 3 * DEPTH, DEPTH),
            gains, arrived,
        ],
        megabytes=16,
    )


def tail(returned, conv_coarse, gains, partial, film, lookup, out_proj, projector):
    cells = returned.shape[0]
    outs = [((CELLS, DEPTH), BF16), ((lookup.shape[1], projector.shape[1]), BF16)]
    return call(
        tail_kernel,
        outs,
        [
            pltpu.VMEM((cells + 4 * TILE_COLS, 3 * DEPTH), BF16),
            *[pltpu.VMEM(shape, dtype) for shape, dtype in outs],
            pltpu.SemaphoreType.DMA((2,)),
        ],
        [
            returned, conv_coarse.reshape(3, 3 * DEPTH, DEPTH), gains,
            partial, film, lookup, out_proj, projector,
        ],
        hbm_outs=(0, 1),
        megabytes=16,
    )


def shifted(value, row_step, col_step):
    count = lax.axis_size("space")
    pairs = []
    for source in range(count):
        row, col = source // TILE_COLS + row_step, source % TILE_COLS + col_step
        if 0 <= row < count // TILE_COLS and 0 <= col < TILE_COLS:
            pairs.append((source, row * TILE_COLS + col))
    return lax.ppermute(value, "space", pairs)


def body(
    tiles,
    station_obs,
    station_tile,
    station_pixel,
    station_embed,
    conv_fine,
    conv_mid,
    conv_coarse,
    norm_gains,
    film_table,
    horizon_step_list,
    out_proj,
    gauge_bin_projector,
):
    space_count = lax.axis_size("space")
    count, readings = station_obs.shape
    table_rows = film_table.shape[0]
    own_rows = lax.axis_index("lead") * table_rows + jnp.arange(table_rows, dtype=jnp.int32)
    lead_hot = (horizon_step_list[:, None] == own_rows[None, :]).astype(BF16)
    film_parts = lax.all_gather(dot(lead_hot, film_table).astype(BF16), "lead")
    film = jnp.sum(film_parts.astype(F32), axis=0)
    film = lax.dynamic_slice_in_dim(film, lax.axis_index("lead"), 1, 0).reshape(2, DEPTH)

    ids = (station_tile[:, 0] * CELLS + station_pixel).reshape(1, count)
    payload, lookup = pack(ids, station_obs, space_count)
    arrived = lax.all_to_all(
        payload.reshape(space_count, 2, 3 * readings), "space", 0, 0, tiled=True
    ).reshape(2 * space_count, 3 * readings)
    arrived, film, embed, fine = lax.optimization_barrier(
        (arrived, film, station_embed.astype(F32), tiles.reshape(CELLS, DEPTH).astype(F32))
    )
    own, first_cols, last_cols, first_rows, last_rows = inject(arrived, embed, fine)

    west = shifted(last_cols, 0, 1)
    east = shifted(first_cols, 0, -1)

    top, bottom = widen(west, east, first_rows, last_rows)
    north = shifted(bottom, 1, 0)
    south = shifted(top, -1, 0)

    partial, parcel = trunk(
        space_count // TILE_COLS,
        north, south, west, east, own, conv_fine, conv_mid, norm_gains, arrived,
    )
    returned = lax.all_to_all(
        parcel.reshape(space_count, 2, 3 * DEPTH), "space", 0, 0, tiled=True
    ).reshape(2 * space_count, 3 * DEPTH)

    maps, scores = tail(
        returned, conv_coarse, norm_gains, partial, film, lookup, out_proj, gauge_bin_projector
    )
    return maps.reshape(1, 1, TILE_H, TILE_W, DEPTH), scores.reshape(1, count, -1)


def solution(mesh):
    in_specs = (
        P("space", None, None, None),
        P("space", None),
        P("space", None),
        P("space"),
        P(),
        P(),
        P(),
        P(),
        P(),
        P("lead", None),
        P(),
        P(),
        P(),
    )
    out_specs = (P("lead", "space", None, None, None), P("lead", "space", None))
    return jax.shard_map(body, mesh=mesh, in_specs=in_specs, out_specs=out_specs, check_vma=False)
```

time: 115 us -> 112 us (0.974)
  the two profiles are of different devices: /device:TPU:39 before, /device:TPU:33 now
where the time goes in v4:
time: 112 us; the launch traced here: 111 us
  blocking collectives  52.8 us (47%)
  starting transfers between devices  29.5 us (26%)
  waiting for transfers between devices  13.2 us (12%)
  Pallas kernels  7.64 us (7%)
  local copies, waits for them, and re-layouts  3.77 us (3%)
  other arithmetic  2.57 us (2%)
    all_to_all x1, blocking collectives, body(): lax.all_to_all(parcel.reshape(space_count, 2, 3 * DEPTH), 'space', 0, 0,...  42.5 us
    all_to_all x1, starting transfers between devices, body(): lax.all_to_all(payload.reshape(space_count, 2, 3 * readings), 'space', 0,...  19.9 us
    all_gather x1, blocking collectives, body(): film_parts = lax.all_gather(dot(lead_hot, film_table).astype(BF16), 'lead')  10.3 us
    ppermute x4, starting transfers between devices, shifted(): return lax.ppermute(value, 'space', pairs)  9.61 us
    pallas_call x5, Pallas kernels, call(): pl.pallas_call(kernel, out_shape=[jax.ShapeDtypeStruct(shape, dtype) for...  7.64 us
    all_to_all x1, waiting for transfers between devices, body(): lax.all_to_all(payload.reshape(space_count, 2, 3 * readings), 'space', 0,...  7.07 us
    ppermute x4, waiting for transfers between devices, shifted(): return lax.ppermute(value, 'space', pairs)  6.14 us
  transfers between devices with their start and end apart: 5, of which 4 were waited for; matrix products, arithmetic and copies ran while one was open for 2% of the time, Pallas kernels for 0%

profile of v4, /device:TPU:33, one launch (start us, length us, event | category | flops | bytes accessed | tf_op | source)
XLA Modules:
  0.0 111.1 jit_solution(3826453014108034546)
XLA Ops:
  0.6 0.7 broadcast_multiply_fusion
  1.4 0.7 add.16
  2.0 0.8 copy-done.8
  2.9 0.4 shard_map.140
  3.3 0.8 reshape.48
  4.1 19.9 %all-to-all-start = ((bf16[128,2,384]{2,1,0:T(2,128)(2,1)}), bf16[128,2,384]{2,1,0:T(2,128)(2,1)}, u32[]{:S(2)}, u32[]{:S(2)}) async-start(bf16[128,2,384]{2,1,0:T(2,128)(2,1)} %reshape.48), calls=%async_computation | async-start | bytes 393216 | tf_op jit(solution)/shard_map/all_to_all | solution.py:368
  24.0 0.8 fusion
  24.9 10.3 %all-gather.1 = bf16[4,4,512]{2,1,0:T(4,128)(2,1)S(1)} all-gather(bf16[1,4,512]{2,1,0:T(4,128)(2,1)S(1)} %fusion), channel_id=2, replica_groups=mesh['space'=128,'lead'=4] {'lead'}, dimensions={0}, use_global_device_ids=true | all-gather | bytes 20480 | tf_op jit(solution)/shard_map/all_gather | solution.py:362
  35.3 1.1 %bitcast_convert_fusion.tiles = f32[512,256]{1,0:T(8,128)S(1)} fusion(bf16[1,16,32,256]{3,2,1,0:T(8,128)(2,1)} %param.13), kind=kLoop, calls=%fused_computation.2 | loop fusion | flops 131072 | bytes 786432 | tf_op jit(solution)/shard_map/convert_element_type | solution.py:372
  36.4 7.1 %all-to-all-done = bf16[128,2,384]{2,1,0:T(2,128)(2,1)} async-done(((bf16[128,2,384]{2,1,0:T(2,128)(2,1)}), bf16[128,2,384]{2,1,0:T(2,128)(2,1)}, u32[]{:S(2)}, u32[]{:S(2)}) %all-to-all-start) | async-done | bytes 196640 | tf_op jit(solution)/shard_map/all_to_all | solution.py:368
  43.5 1.0 reshape.49.arrived
  44.5 0.5 shard_map.141
  45.1 2.4 %collective-permute-start = (bf16[16,8,256]{2,1,0:T(8,128)(2,1)S(1)}, bf16[16,8,256]{2,1,0:T(8,128)(2,1)S(1)}, u32[]{:S(2)}, u32[]{:S(2)}) collective-permute-start(bf16[16,8,256]{2,1,0:T(8,128)(2,1)S(1)} %get-tuple-element.23), channel_id=1, source_target_pairs={{0,4},{4,8},{8,12},{12,16},{16,20},{20,24},{24,28},{32,36},{36,40}... | collective-permute-start | bytes 196616 | tf_op jit(solution)/shard_map/ppermute | solution.py:339
  47.4 1.9 %collective-permute-start.1 = (bf16[16,8,256]{2,1,0:T(8,128)(2,1)S(1)}, bf16[16,8,256]{2,1,0:T(8,128)(2,1)S(1)}, u32[]{:S(2)}, u32[]{:S(2)}) collective-permute-start(bf16[16,8,256]{2,1,0:T(8,128)(2,1)S(1)} %get-tuple-element.24), channel_id=1, source_target_pairs={{4,0},{8,4},{12,8},{16,12},{20,16},{24,20},{28,24},{36,32},{40,36}... | collective-permute-start | bytes 196616 | tf_op jit(solution)/shard_map/ppermute | solution.py:339
  49.4 3.6 %collective-permute-done.1.east = bf16[16,8,256]{2,1,0:T(8,128)(2,1)S(1)} collective-permute-done((bf16[16,8,256]{2,1,0:T(8,128)(2,1)S(1)}, bf16[16,8,256]{2,1,0:T(8,128)(2,1)S(1)}, u32[]{:S(2)}, u32[]{:S(2)}) %collective-permute-start.1) | collective-permute-done | bytes 65568 | tf_op jit(solution)/shard_map/ppermute | solution.py:339
  53.0 2.2 %collective-permute-start.2 = (bf16[5,48,256]{2,1,0:T(8,128)(2,1)S(1)}, bf16[5,48,256]{2,1,0:T(8,128)(2,1)S(1)}, u32[]{:S(2)}, u32[]{:S(2)}) collective-permute-start(bf16[5,48,256]{2,1,0:T(8,128)(2,1)S(1)} %get-tuple-element.27), channel_id=1, source_target_pairs={{0,32},{4,36},{8,40},{12,44},{16,48},{20,52},{24,56},{28,60},{32,6... | collective-permute-start | bytes 368648 | tf_op jit(solution)/shard_map/ppermute | solution.py:339
  55.2 3.1 %collective-permute-start.3 = (bf16[5,48,256]{2,1,0:T(8,128)(2,1)S(1)}, bf16[5,48,256]{2,1,0:T(8,128)(2,1)S(1)}, u32[]{:S(2)}, u32[]{:S(2)}) collective-permute-start(bf16[5,48,256]{2,1,0:T(8,128)(2,1)S(1)} %get-tuple-element.28), channel_id=1, source_target_pairs={{32,0},{36,4},{40,8},{44,12},{48,16},{52,20},{56,24},{60,28},{64,3... | collective-permute-start | bytes 368648 | tf_op jit(solution)/shard_map/ppermute | solution.py:339
  58.3 0.6 collective-permute-done.2.north
  59.0 1.9 %collective-permute-done.3.south = bf16[5,48,256]{2,1,0:T(8,128)(2,1)S(1)} collective-permute-done((bf16[5,48,256]{2,1,0:T(8,128)(2,1)S(1)}, bf16[5,48,256]{2,1,0:T(8,128)(2,1)S(1)}, u32[]{:S(2)}, u32[]{:S(2)}) %collective-permute-start.3) | collective-permute-done | bytes 122912 | tf_op jit(solution)/shard_map/ppermute | solution.py:339
  60.9 3.5 %shard_map.143 = (f32[512,256]{1,0:T(8,128)S(1)}, bf16[256,768]{1,0:T(8,128)(2,1)S(1)}) custom-call(bf16[5,48,256]{2,1,0:T(8,128)(2,1)S(1)} %collective-permute-done.2.north, bf16[5,48,256]{2,1,0:T(8,128)(2,1)S(1)} %collective-permute-done.3.south, bf16[16,8,256]{2,1,0:T(8,128)(2,1)S(1)} %collective-permute-done.west, ...), custom_call_target="tpu_custom_call" | custom-call | tf_op jit(solution)/shard_map/pallas_call | solution.py:252
  64.4 0.8 copy-done.4
  65.2 0.1 reshape.53
  65.3 42.5 %all_to_all.10 = bf16[128,2,768]{2,1,0:T(2,128)(2,1)S(1)} all-to-all(bf16[128,2,768]{2,1,0:T(2,128)(2,1)S(1)} %reshape.53), channel_id=1, replica_groups=mesh['space'=128,'lead'=4] {'space'}, dimensions={0} | all-to-all | bytes 786432 | tf_op jit(solution)/shard_map/all_to_all | solution.py:387
  108.0 3.2 %shard_map.144 = (bf16[512,256]{1,0:T(8,128)(2,1)}, bf16[256,256]{1,0:T(8,128)(2,1)}) custom-call(bf16[256,768]{1,0:T(8,128)(2,1)S(1)} %reshape.54.returned, bf16[3,768,256]{2,1,0:T(8,128)(2,1)S(1)} %bitcast.15, bf16[4,256]{1,0:T(4,128)(2,1)S(1)} %copy-done.9, f32[512,256]{1,0:T(8,128)S(1)} %copy-done.5, f32[2,256]{1,0:T(2,128)S(1)} %reshape.50.film, ...), custom_call_target="tpu_custom_call" | custom-call | tf_op jit(solution)/shard_map/pallas_call | solution.py:252
  (28 shorter events, 0.3 us)
Async XLA Ops:
  0.6 23.4 %copy-start = (bf16[180,512]{1,0:T(8,128)(2,1)S(1)}, bf16[180,512]{1,0:T(8,128)(2,1)}, u32[]{:S(2)}) copy-start(bf16[180,512]{1,0:T(8,128)(2,1)} %param.22) | copy-start | bytes 552964
  2.0 0.8 copy-start.8
  2.9 32.4 %copy-start.10 = (bf16[128,256]{1,0:T(8,128)(2,1)S(1)}, bf16[128,256]{1,0:T(8,128)(2,1)}, u32[]{:S(2)}) copy-start(bf16[128,256]{1,0:T(8,128)(2,1)} %param.17) | copy-start | bytes 196612
  4.1 39.4 %all-to-all-start = ((bf16[128,2,384]{2,1,0:T(2,128)(2,1)}), bf16[128,2,384]{2,1,0:T(2,128)(2,1)}, u32[]{:S(2)}, u32[]{:S(2)}) async-start(bf16[128,2,384]{2,1,0:T(2,128)(2,1)} %reshape.48), calls=%async_computation | async-start | bytes 393216 | tf_op jit(solution)/shard_map/all_to_all | solution.py:368
  35.2 25.6 %copy-start.2 = (bf16[3,3,256,256]{3,2,1,0:T(8,128)(2,1)S(1)}, bf16[3,3,256,256]{3,2,1,0:T(8,128)(2,1)}, u32[]{:S(2)}) copy-start(bf16[3,3,256,256]{3,2,1,0:T(8,128)(2,1)} %param.19) | copy-start | bytes 3538948
  35.3 25.6 %copy-start.1 = (bf16[3,3,256,256]{3,2,1,0:T(8,128)(2,1)S(1)}, bf16[3,3,256,256]{3,2,1,0:T(8,128)(2,1)}, u32[]{:S(2)}) copy-start(bf16[3,3,256,256]{3,2,1,0:T(8,128)(2,1)} %param.18) | copy-start | bytes 3538948
  35.3 25.6 %copy-start.9 = (bf16[4,256]{1,0:T(4,128)(2,1)S(1)}, bf16[4,256]{1,0:T(4,128)(2,1)}, u32[]{:S(2)}) copy-start(bf16[4,256]{1,0:T(4,128)(2,1)} %gains.3) | copy-start | bytes 6148
  45.1 4.3 %collective-permute-start = (bf16[16,8,256]{2,1,0:T(8,128)(2,1)S(1)}, bf16[16,8,256]{2,1,0:T(8,128)(2,1)S(1)}, u32[]{:S(2)}, u32[]{:S(2)}) collective-permute-start(bf16[16,8,256]{2,1,0:T(8,128)(2,1)S(1)} %get-tuple-element.23), channel_id=1, source_target_pairs={{0,4},{4,8},{8,12},{12,16},{16,20},{20,24},{24,28},{32,36},{36,40}... | collective-permute-start | bytes 196616 | tf_op jit(solution)/shard_map/ppermute | solution.py:339
  47.4 5.6 %collective-permute-start.1 = (bf16[16,8,256]{2,1,0:T(8,128)(2,1)S(1)}, bf16[16,8,256]{2,1,0:T(8,128)(2,1)S(1)}, u32[]{:S(2)}, u32[]{:S(2)}) collective-permute-start(bf16[16,8,256]{2,1,0:T(8,128)(2,1)S(1)} %get-tuple-element.24), channel_id=1, source_target_pairs={{4,0},{8,4},{12,8},{16,12},{20,16},{24,20},{28,24},{36,32},{40,36}... | collective-permute-start | bytes 196616 | tf_op jit(solution)/shard_map/ppermute | solution.py:339
  53.0 5.9 %collective-permute-start.2 = (bf16[5,48,256]{2,1,0:T(8,128)(2,1)S(1)}, bf16[5,48,256]{2,1,0:T(8,128)(2,1)S(1)}, u32[]{:S(2)}, u32[]{:S(2)}) collective-permute-start(bf16[5,48,256]{2,1,0:T(8,128)(2,1)S(1)} %get-tuple-element.27), channel_id=1, source_target_pairs={{0,32},{4,36},{8,40},{12,44},{16,48},{20,52},{24,56},{28,60},{32,6... | collective-permute-start | bytes 368648 | tf_op jit(solution)/shard_map/ppermute | solution.py:339
  55.2 5.6 %collective-permute-start.3 = (bf16[5,48,256]{2,1,0:T(8,128)(2,1)S(1)}, bf16[5,48,256]{2,1,0:T(8,128)(2,1)S(1)}, u32[]{:S(2)}, u32[]{:S(2)}) collective-permute-start(bf16[5,48,256]{2,1,0:T(8,128)(2,1)S(1)} %get-tuple-element.28), channel_id=1, source_target_pairs={{32,0},{36,4},{40,8},{44,12},{48,16},{52,20},{56,24},{60,28},{64,3... | collective-permute-start | bytes 368648 | tf_op jit(solution)/shard_map/ppermute | solution.py:339
  64.4 0.8 copy-start.4
  65.2 42.8 %copy-start.3 = (bf16[3,3,256,256]{3,2,1,0:T(8,128)(2,1)S(1)}, bf16[3,3,256,256]{3,2,1,0:T(8,128)(2,1)}, u32[]{:S(2)}) copy-start(bf16[3,3,256,256]{3,2,1,0:T(8,128)(2,1)} %param.20) | copy-start | bytes 3538948
  65.2 42.8 %copy-start.5 = (f32[512,256]{1,0:T(8,128)S(1)}, f32[512,256]{1,0:T(8,128)}, u32[]{:S(2)}) copy-start(f32[512,256]{1,0:T(8,128)} %copy-done.4) | copy-start | bytes 1572868
  65.2 42.8 %copy-start.6 = (bf16[256,256]{1,0:T(8,128)(2,1)S(1)}, bf16[256,256]{1,0:T(8,128)(2,1)}, u32[]{:S(2)}) copy-start(bf16[256,256]{1,0:T(8,128)(2,1)} %out_proj.1) | copy-start | bytes 393220
  65.2 42.8 %copy-start.7 = (bf16[256,256]{1,0:T(8,128)(2,1)S(1)}, bf16[256,256]{1,0:T(8,128)(2,1)}, u32[]{:S(2)}) copy-start(bf16[256,256]{1,0:T(8,128)(2,1)} %projector.1) | copy-start | bytes 393220

commit v5 on v4

--- a/solution.py
+++ b/solution.py
@@ -24,6 +24,10 @@
     return jnp.dot(a, b, preferred_element_type=F32)
 
 
+def dot_rows(a, b):
+    return lax.dot_general(a, b, (((1,), (1,)), ((), ())), preferred_element_type=F32)
+
+
 def silu(v):
     return v / (1.0 + jnp.exp(-v))
 
@@ -50,12 +54,17 @@
     return lax.div(at, TILE_COLS), lax.rem(at, TILE_COLS)
 
 
-def pack_kernel(ids, obs, payload, lookup):
-    count, readings = obs.shape
+def pack_kernel(records, payload, lookup):
+    count, readings = records.shape[0], records.shape[1] // 2
     pairs = payload.shape[0]
+    obs = records[:, :readings]
     earlier = ones_where(line((count, count)) < column((count, count)))
+    sort, lane = line((16, readings)), column((16, readings))
+    weights = jnp.where((sort == 1) & (lane == 1), 16.0, 0.0)
+    weights = jnp.where((sort == 0) & (lane == 0) | (sort == 1) & (lane == 2), 1.0, weights)
+    ids = dot_rows(weights.astype(BF16), records[:, readings:]).astype(jnp.int32)
+    dest, pixel = ids[0:1], ids[1:2]
     lane = column((pairs, readings))
-    dest, pixel = ids[...] // CELLS, ids[...] % CELLS
     hot = (line((pairs // 2, count)) == dest).astype(F32)
     prior = dot(hot.astype(BF16), earlier)
     position = jnp.sum(prior * hot, axis=0, keepdims=True).astype(jnp.int32)
@@ -68,7 +77,7 @@
     places = jnp.zeros((pairs, readings), jnp.int32)
     for half in range(2):
         match = line((pairs, count)) + half * pairs == key
-        sent = dot(ones_where(match), obs[...])
+        sent = dot(ones_where(match), obs)
         payload[:, half * readings : (half + 1) * readings] = sent.astype(BF16)
         at = jnp.sum(jnp.where(match, pixel, 0), axis=1, keepdims=True)
         places = jnp.where(lane == 2 * half, at >> 4, places)
@@ -77,54 +86,81 @@
 
 
 def inject_kernel(
-    arrived, embed, tiles, own, first_cols, last_cols, first_rows, last_rows
+    steps, arrived, embed, tiles, film_table,
+    own, first_cols, last_cols, first_rows, last_rows, film,
 ):
     pairs = arrived.shape[0]
     readings = embed.shape[0]
-    weight = embed[...].astype(BF16)
+    weight = embed[...]
     sort, lane = line((8, readings)), column((8, readings))
     weights = jnp.where(lane == 2 * sort, 16.0, jnp.where(lane == 2 * sort + 1, 1.0, 0.0))
     weights = jnp.where(sort < 2, weights, 0.0).astype(BF16)
-    pixels = lax.dot_general(
-        weights,
-        arrived[:, 2 * readings :],
-        (((1,), (1,)), ((), ())),
-        preferred_element_type=F32,
-    ).astype(jnp.int32)
+    pixels = dot_rows(weights, arrived[:, 2 * readings :]).astype(jnp.int32)
     fine = 0.0
     for half in range(2):
         embedded = dot(arrived[:, half * readings : (half + 1) * readings], weight)
         hot = ones_where(line((CELLS, pairs)) == pixels[half : half + 1])
         fine += dot(hot, embedded.astype(BF16))
-    fine = (fine + tiles[...]).reshape(TILE_H, TILE_W, DEPTH)
+    fine = (fine + tiles[...].astype(F32)).reshape(TILE_H, TILE_W, DEPTH)
     own[...] = fine
-    first_cols[...] = fine[:, :SIDE].astype(BF16)
-    last_cols[...] = fine[:, -SIDE:].astype(BF16)
+    table_rows = film_table.shape[0]
+    offset = lax.axis_index("lead") * table_rows
+    sort = line((8, table_rows))
+    at = jnp.full((8, table_rows), -1, jnp.int32)
+    for i in range(4):
+        at = jnp.where((sort & 3) == i, steps[i] - offset, at)
+    hot = ones_where(column((8, table_rows)) == at)
+    both = dot(hot, film_table[...])
+    rows = jnp.where(line((8, DEPTH)) < 4, both[:, :DEPTH], both[:, DEPTH:])
+    film[...] = rows
+    at = line((SIDE, DEPTH))
+    for y in range(TILE_H):
+        first, last = fine[y, :SIDE], fine[y, -SIDE:]
+        if y < 8:
+            first = jnp.where(at == SIDE - 1, rows[y : y + 1], first)
+            last = jnp.where(at == 0, rows[y : y + 1], last)
+        first_cols[y] = first.astype(BF16)
+        last_cols[y] = last.astype(BF16)
     first_rows[...] = fine[:HALO].astype(BF16)
     last_rows[...] = fine[-HALO:].astype(BF16)
 
 
 def widen_kernel(west, east, first_rows, last_rows, top, bottom):
-    for rows, target, side in (
-        (first_rows, top, slice(0, HALO)),
-        (last_rows, bottom, slice(TILE_H - HALO, TILE_H)),
-    ):
-        parts = [west[side], rows[...], east[side]]
-        whole = jnp.concatenate([part.astype(F32) for part in parts], axis=1)
-        target[...] = whole.astype(BF16)
+    _, col_at = grid_place()
+    at = line((FRAME_W, DEPTH))
+    for rows, target, offset in ((first_rows, top, 0), (last_rows, bottom, TILE_H - HALO)):
+        for y in range(HALO):
+            left = jnp.where(col_at > 0, west[offset + y].astype(F32), 0.0)
+            right = jnp.where(col_at < TILE_COLS - 1, east[offset + y].astype(F32), 0.0)
+            whole = jnp.concatenate([left, rows[y].astype(F32), right], axis=0)
+            if offset:
+                whole = jnp.where(at == 0, west[y, 0:1].astype(F32), whole)
+                if y + HALO < 8:
+                    whole = jnp.where(at == 1, west[y + HALO, 0:1].astype(F32), whole)
+            target[y] = whole.astype(BF16)
 
 
 def trunk_kernel(
     image_rows,
-    north, south, west, east, own, conv_fine, conv_mid, gains, arrived,
-    partial_ref, parcel,
+    north, south, west, east, own, film, conv_fine, conv_mid, gains, arrived,
+    partial_ref, parcel, film_ref,
     frame, taps, enc, mid_in, mid_taps,
 ):
-    frame[:HALO] = north[...].astype(F32)
-    frame[HALO + TILE_H :] = south[...].astype(F32)
-    frame[HALO : HALO + TILE_H, :SIDE] = west[...].astype(F32)
+    row_at, col_at = grid_place()
+    left = west[...].astype(F32)
+    right = east[...].astype(F32)
+    above = north[...].astype(F32)
+    at = line((8, DEPTH))
+    rows = film[...]
+    for y in range(8):
+        extra = above[y, 0:1] if y < HALO else above[y - HALO, 1:2]
+        rows += jnp.where(at == y, left[y, 0:1] + right[y, SIDE - 1 : SIDE] + extra, 0.0)
+    film_ref[...] = rows
+    frame[:HALO] = jnp.where(row_at > 0, above, 0.0)
+    frame[HALO + TILE_H :] = jnp.where(row_at < image_rows - 1, south[...].astype(F32), 0.0)
+    frame[HALO : HALO + TILE_H, :SIDE] = jnp.where(col_at > 0, left, 0.0)
     frame[HALO : HALO + TILE_H, SIDE : SIDE + TILE_W] = own[...]
-    frame[HALO : HALO + TILE_H, SIDE + TILE_W :] = east[...].astype(F32)
+    frame[HALO : HALO + TILE_H, SIDE + TILE_W :] = jnp.where(col_at < TILE_COLS - 1, right, 0.0)
     gain = gains[0:1].astype(F32)
     for y in range(FRAME_H):
         normed = rms_scale(frame[y], gain)
@@ -149,7 +185,6 @@
     mid = mid_in[...]
     normed = rms_scale(mid, gains[1:2].astype(F32))
     at = line(mid.shape)
-    row_at, col_at = grid_place()
     row = row_at * (TILE_H // 4) - 1 + at // MID_W
     col = col_at * (TILE_W // 4) - 1 + at % MID_W
     inside = (row >= 0) & (row < image_rows * (TILE_H // 4))
@@ -212,7 +247,9 @@
     low = (context - high.astype(F32)).astype(BF16)
 
     gain = gains[3:4].astype(F32)
-    scale, shift = 1.0 + film[0:1], film[1:2]
+    lead, at = lax.axis_index("lead"), line((8, DEPTH))
+    scale = 1.0 + jnp.sum(jnp.where(at == lead, film[...], 0.0), axis=0, keepdims=True)
+    shift = jnp.sum(jnp.where(at == lead + 4, film[...], 0.0), axis=0, keepdims=True)
 
     def decode(values):
         hidden = rms_scale(values, gain) * scale + shift
@@ -228,9 +265,7 @@
 
     count = lookup.shape[1]
     same = ones_where(line((count, count)) == column((count, count)))
-    where = lax.dot_general(
-        same, lookup[...], (((1,), (1,)), ((), ())), preferred_element_type=F32
-    )
+    where = dot_rows(same, lookup[...])
     key = (where[:, 0:1] * 16 + where[:, 1:2]).astype(jnp.int32)
     area = (where[:, 2:3] * 16 + where[:, 3:4]).astype(jnp.int32)
     slot = column((count, cells))
@@ -246,26 +281,27 @@
     put_scores.wait()
 
 
-def call(kernel, outs, scratch, operands, hbm_outs=(), megabytes=4):
+def call(kernel, outs, scratch, operands, hbm_outs=(), scalars=0, megabytes=4):
     vmem = pl.BlockSpec(memory_space=pltpu.VMEM)
     hbm = pl.BlockSpec(memory_space=pltpu.HBM)
+    smem = pl.BlockSpec(memory_space=pltpu.SMEM)
     return pl.pallas_call(
         kernel,
         out_shape=[jax.ShapeDtypeStruct(shape, dtype) for shape, dtype in outs],
-        in_specs=[vmem] * len(operands),
+        in_specs=[smem] * scalars + [vmem] * (len(operands) - scalars),
         out_specs=[hbm if i in hbm_outs else vmem for i in range(len(outs))],
         scratch_shapes=scratch,
         compiler_params=pltpu.CompilerParams(vmem_limit_bytes=megabytes * 2**20),
     )(*operands)
 
 
-def pack(ids, obs, space_count):
-    count, readings = obs.shape
-    outs = [((2 * space_count, 3 * readings), BF16), ((16, count), BF16)]
-    return call(pack_kernel, outs, [], [ids, obs], megabytes=8)
-
-
-def inject(arrived, embed, tiles):
+def pack(records, space_count):
+    count, width = records.shape
+    outs = [((2 * space_count, width // 2 * 3), BF16), ((16, count), BF16)]
+    return call(pack_kernel, outs, [], [records], megabytes=8)
+
+
+def inject(steps, arrived, embed, tiles, film_table):
     return call(
         inject_kernel,
         [
@@ -274,9 +310,11 @@
             ((TILE_H, SIDE, DEPTH), BF16),
             ((HALO, TILE_W, DEPTH), BF16),
             ((HALO, TILE_W, DEPTH), BF16),
+            ((8, DEPTH), F32),
         ],
         [],
-        [arrived, embed, tiles],
+        [steps, arrived, embed, tiles, film_table],
+        scalars=1,
         megabytes=8,
     )
 
@@ -288,10 +326,10 @@
     )
 
 
-def trunk(image_rows, north, south, west, east, own, conv_fine, conv_mid, gains, arrived):
+def trunk(image_rows, north, south, west, east, own, film, conv_fine, conv_mid, gains, arrived):
     return call(
         functools.partial(trunk_kernel, image_rows),
-        [((CELLS, DEPTH), F32), ((arrived.shape[0], 3 * DEPTH), BF16)],
+        [((CELLS, DEPTH), F32), ((arrived.shape[0], 3 * DEPTH), BF16), ((8, DEPTH), F32)],
         [
             pltpu.VMEM((FRAME_H, FRAME_W, DEPTH), F32),
             pltpu.VMEM((FRAME_H * FRAME_W, 3 * DEPTH), BF16),
@@ -300,7 +338,7 @@
             pltpu.VMEM((ENC_H // 4 * MID_W, 3 * DEPTH), BF16),
         ],
         [
-            north, south, west, east, own,
+            north, south, west, east, own, film,
             conv_fine.reshape(3, 3 * DEPTH, DEPTH),
             conv_mid.reshape(3, 3 * DEPTH, DEPTH),
             gains, arrived,
@@ -329,14 +367,16 @@
     )
 
 
-def shifted(value, row_step, col_step):
-    count = lax.axis_size("space")
+def shifted(value, row_step, col_step, lead_step):
+    rows, leads = lax.axis_size("space") // TILE_COLS, lax.axis_size("lead")
     pairs = []
-    for source in range(count):
-        row, col = source // TILE_COLS + row_step, source % TILE_COLS + col_step
-        if 0 <= row < count // TILE_COLS and 0 <= col < TILE_COLS:
-            pairs.append((source, row * TILE_COLS + col))
-    return lax.ppermute(value, "space", pairs)
+    for row in range(rows):
+        for col in range(TILE_COLS):
+            for lead in range(leads):
+                source = (row * TILE_COLS + col) * leads + lead
+                there = (row + row_step) % rows * TILE_COLS + (col + col_step) % TILE_COLS
+                pairs.append((source, there * leads + (lead - lead_step) % leads))
+    return lax.ppermute(value, ("space", "lead"), pairs)
 
 
 def body(
@@ -356,33 +396,33 @@
 ):
     space_count = lax.axis_size("space")
     count, readings = station_obs.shape
-    table_rows = film_table.shape[0]
-    own_rows = lax.axis_index("lead") * table_rows + jnp.arange(table_rows, dtype=jnp.int32)
-    lead_hot = (horizon_step_list[:, None] == own_rows[None, :]).astype(BF16)
-    film_parts = lax.all_gather(dot(lead_hot, film_table).astype(BF16), "lead")
-    film = jnp.sum(film_parts.astype(F32), axis=0)
-    film = lax.dynamic_slice_in_dim(film, lax.axis_index("lead"), 1, 0).reshape(2, DEPTH)
-
-    ids = (station_tile[:, 0] * CELLS + station_pixel).reshape(1, count)
-    payload, lookup = pack(ids, station_obs, space_count)
+    records = jnp.concatenate(
+        [
+            station_obs,
+            station_tile.astype(BF16),
+            (station_pixel // 16).astype(BF16)[:, None],
+            (station_pixel % 16).astype(BF16)[:, None],
+            jnp.zeros((count, readings - 3), BF16),
+        ],
+        axis=1,
+    )
+    payload, lookup = pack(records, space_count)
     arrived = lax.all_to_all(
         payload.reshape(space_count, 2, 3 * readings), "space", 0, 0, tiled=True
     ).reshape(2 * space_count, 3 * readings)
-    arrived, film, embed, fine = lax.optimization_barrier(
-        (arrived, film, station_embed.astype(F32), tiles.reshape(CELLS, DEPTH).astype(F32))
-    )
-    own, first_cols, last_cols, first_rows, last_rows = inject(arrived, embed, fine)
-
-    west = shifted(last_cols, 0, 1)
-    east = shifted(first_cols, 0, -1)
-
+    own, first_cols, last_cols, first_rows, last_rows, film = inject(
+        horizon_step_list, arrived, station_embed, tiles.reshape(CELLS, DEPTH), film_table
+    )
+
+    west = shifted(last_cols, 0, 1, 1)
+    east = shifted(first_cols, 0, -1, -1)
     top, bottom = widen(west, east, first_rows, last_rows)
-    north = shifted(bottom, 1, 0)
-    south = shifted(top, -1, 0)
-
-    partial, parcel = trunk(
+    north = shifted(bottom, 1, 0, 1)
+    south = shifted(top, -1, 0, 0)
+
+    partial, parcel, film = trunk(
         space_count // TILE_COLS,
-        north, south, west, east, own, conv_fine, conv_mid, norm_gains, arrived,
+        north, south, west, east, own, film, conv_fine, conv_mid, norm_gains, arrived,
     )
     returned = lax.all_to_all(
         parcel.reshape(space_count, 2, 3 * DEPTH), "space", 0, 0, tiled=True

time: 112 us -> 112 us (level)
  the two profiles are of different devices: /device:TPU:33 before, /device:TPU:35 now
where the time goes in v5:
time: 112 us; the launch traced here: 111 us
  blocking collectives  77.4 us (69%)
  starting transfers between devices  14.1 us (13%)
  Pallas kernels  8.38 us (7%)
  waiting for transfers between devices  7.16 us (6%)
  local copies, waits for them, and re-layouts  1.92 us (2%)
  other arithmetic  1.43 us (1%)
    all_to_all x1, blocking collectives, body(): lax.all_to_all(payload.reshape(space_count, 2, 3 * readings), 'space', 0,...  39.1 us
    all_to_all x1, blocking collectives, body(): lax.all_to_all(parcel.reshape(space_count, 2, 3 * DEPTH), 'space', 0, 0,...  38.3 us
    ppermute x4, starting transfers between devices, shifted(): return lax.ppermute(value, ('space', 'lead'), pairs)  14.1 us
    pallas_call x5, Pallas kernels, call(): pl.pallas_call(kernel, out_shape=[jax.ShapeDtypeStruct(shape, dtype) for...  8.38 us
    ppermute x4, waiting for transfers between devices, shifted(): return lax.ppermute(value, ('space', 'lead'), pairs)  7.16 us
  transfers between devices with their start and end apart: 4, of which 3 were waited for; matrix products, arithmetic and copies ran while one was open for 0% of the time, Pallas kernels for 0%

profile of v5, /device:TPU:35, one launch (start us, length us, event | category | flops | bytes accessed | tf_op | source)
XLA Modules:
  0.0 111.3 jit_solution(4223666577758675907)
XLA Ops:
  0.7 0.7 convert_element_type.9
  1.4 0.7 fusion
  2.1 0.1 copy.16
  2.2 0.1 broadcast_in_dim.13
  2.3 0.1 broadcast_in_dim.12
  2.5 1.1 concatenate.3.records
  3.6 0.6 shard_map.140
  4.2 0.1 reshape.34
  4.2 39.1 %all_to_all.10 = bf16[128,2,384]{2,1,0:T(2,128)(2,1)S(1)} all-to-all(bf16[128,2,384]{2,1,0:T(2,128)(2,1)S(1)} %reshape.34), channel_id=1, replica_groups=mesh['space'=128,'lead'=4] {'space'}, dimensions={0} | all-to-all | bytes 393216 | tf_op jit(solution)/shard_map/all_to_all | solution.py:410
  43.3 0.1 reshape.35.arrived
  43.5 1.1 shard_map.141
  44.6 2.3 %collective-permute-start = (bf16[16,8,256]{2,1,0:T(8,128)(2,1)S(1)}, bf16[16,8,256]{2,1,0:T(8,128)(2,1)S(1)}, u32[]{:S(2)}, u32[]{:S(2)}) collective-permute-start(bf16[16,8,256]{2,1,0:T(8,128)(2,1)S(1)} %get-tuple-element.18), channel_id=1, source_target_pairs={{0,7},{1,4},{2,5},{3,6},{4,11},{5,8},{6,9},{7,10},{8,15},{9,12},{1... | collective-permute-start | bytes 196616 | tf_op jit(solution)/shard_map/ppermute | solution.py:379
  46.9 3.2 %collective-permute-start.1 = (bf16[16,8,256]{2,1,0:T(8,128)(2,1)S(1)}, bf16[16,8,256]{2,1,0:T(8,128)(2,1)S(1)}, u32[]{:S(2)}, u32[]{:S(2)}) collective-permute-start(bf16[16,8,256]{2,1,0:T(8,128)(2,1)S(1)} %get-tuple-element.19), channel_id=1, source_target_pairs={{0,29},{1,30},{2,31},{3,28},{4,1},{5,2},{6,3},{7,0},{8,5},{9,6},{1... | collective-permute-start | bytes 196616 | tf_op jit(solution)/shard_map/ppermute | solution.py:379
  50.2 0.3 collective-permute-done.west
  50.5 3.0 %collective-permute-done.1.east = bf16[16,8,256]{2,1,0:T(8,128)(2,1)S(1)} collective-permute-done((bf16[16,8,256]{2,1,0:T(8,128)(2,1)S(1)}, bf16[16,8,256]{2,1,0:T(8,128)(2,1)S(1)}, u32[]{:S(2)}, u32[]{:S(2)}) %collective-permute-start.1) | collective-permute-done | bytes 65568 | tf_op jit(solution)/shard_map/ppermute | solution.py:379
  53.6 5.5 %collective-permute-start.2 = (bf16[5,48,256]{2,1,0:T(8,128)(2,1)S(1)}, bf16[5,48,256]{2,1,0:T(8,128)(2,1)S(1)}, u32[]{:S(2)}, u32[]{:S(2)}) collective-permute-start(bf16[5,48,256]{2,1,0:T(8,128)(2,1)S(1)} %get-tuple-element.22), channel_id=1, source_target_pairs={{0,35},{1,32},{2,33},{3,34},{4,39},{5,36},{6,37},{7,38},{8,43},{9,... | collective-permute-start | bytes 368648 | tf_op jit(solution)/shard_map/ppermute | solution.py:379
  59.0 3.1 %collective-permute-start.3 = (bf16[5,48,256]{2,1,0:T(8,128)(2,1)S(1)}, bf16[5,48,256]{2,1,0:T(8,128)(2,1)S(1)}, u32[]{:S(2)}, u32[]{:S(2)}) collective-permute-start(bf16[5,48,256]{2,1,0:T(8,128)(2,1)S(1)} %get-tuple-element.23), channel_id=1, source_target_pairs={{0,480},{1,481},{2,482},{3,483},{4,484},{5,485},{6,486},{7,487},{8... | collective-permute-start | bytes 368648 | tf_op jit(solution)/shard_map/ppermute | solution.py:379
  62.2 3.8 %collective-permute-done.3.south = bf16[5,48,256]{2,1,0:T(8,128)(2,1)S(1)} collective-permute-done((bf16[5,48,256]{2,1,0:T(8,128)(2,1)S(1)}, bf16[5,48,256]{2,1,0:T(8,128)(2,1)S(1)}, u32[]{:S(2)}, u32[]{:S(2)}) %collective-permute-start.3) | collective-permute-done | bytes 122912 | tf_op jit(solution)/shard_map/ppermute | solution.py:379
  66.0 3.5 %shard_map.143 = (f32[512,256]{1,0:T(8,128)S(1)}, bf16[256,768]{1,0:T(8,128)(2,1)S(1)}, f32[8,256]{1,0:T(8,128)S(1)}) custom-call(bf16[5,48,256]{2,1,0:T(8,128)(2,1)S(1)} %collective-permute-done.2.north, bf16[5,48,256]{2,1,0:T(8,128)(2,1)S(1)} %collective-permute-done.3.south, bf16[16,8,256]{2,1,0:T(8,128)(2,1)S(1)} %collective-permute-done.west, ...), custom_call_target="tpu_custom_call" | custom-call | tf_op jit(solution)/shard_map/pallas_call | solution.py:288
  69.5 0.0 copy-start.5
  69.5 0.1 reshape.39
  69.7 38.3 %all_to_all.11 = bf16[128,2,768]{2,1,0:T(2,128)(2,1)S(1)} all-to-all(bf16[128,2,768]{2,1,0:T(2,128)(2,1)S(1)} %reshape.39), channel_id=1, replica_groups=mesh['space'=128,'lead'=4] {'space'}, dimensions={0} | all-to-all | bytes 786432 | tf_op jit(solution)/shard_map/all_to_all | solution.py:427
  108.0 0.1 reshape.40.returned
  108.2 3.2 %shard_map.144 = (bf16[512,256]{1,0:T(8,128)(2,1)}, bf16[256,256]{1,0:T(8,128)(2,1)}) custom-call(bf16[256,768]{1,0:T(8,128)(2,1)S(1)} %reshape.40.returned, bf16[3,768,256]{2,1,0:T(8,128)(2,1)S(1)} %bitcast.8, bf16[4,256]{1,0:T(4,128)(2,1)S(1)} %copy-done.8, f32[512,256]{1,0:T(8,128)S(1)} %get-tuple-element.27.partial, ...), custom_call_target="tpu_custom_call" | custom-call | tf_op jit(solution)/shard_map/pallas_call | solution.py:288
  (22 shorter events, 0.1 us)
Async XLA Ops:
  0.6 42.8 %copy-start.9 = (s32[4]{0:T(128)S(1)}, s32[4]{0:T(128)}, u32[]{:S(2)}) copy-start(s32[4]{0:T(128)} %steps.1) | copy-start | bytes 52
  0.6 42.8 %copy-start.4 = (bf16[180,512]{1,0:T(8,128)(2,1)S(1)}, bf16[180,512]{1,0:T(8,128)(2,1)}, u32[]{:S(2)}) copy-start(bf16[180,512]{1,0:T(8,128)(2,1)} %film_table.1) | copy-start | bytes 552964
  0.7 42.8 %copy-start.7 = (bf16[128,256]{1,0:T(8,128)(2,1)S(1)}, bf16[128,256]{1,0:T(8,128)(2,1)}, u32[]{:S(2)}) copy-start(bf16[128,256]{1,0:T(8,128)(2,1)} %embed.1) | copy-start | bytes 196612
  0.7 42.8 %copy-start.3 = (bf16[1,16,32,256]{3,2,1,0:T(8,128)(2,1)S(1)}, bf16[1,16,32,256]{3,2,1,0:T(8,128)(2,1)}, u32[]{:S(2)}) copy-start(bf16[1,16,32,256]{3,2,1,0:T(8,128)(2,1)} %param.13) | copy-start | bytes 786436
  2.5 63.5 %copy-start.1 = (bf16[3,3,256,256]{3,2,1,0:T(8,128)(2,1)S(1)}, bf16[3,3,256,256]{3,2,1,0:T(8,128)(2,1)}, u32[]{:S(2)}) copy-start(bf16[3,3,256,256]{3,2,1,0:T(8,128)(2,1)} %param.19) | copy-start | bytes 3538948
  3.6 62.4 %copy-start = (bf16[3,3,256,256]{3,2,1,0:T(8,128)(2,1)S(1)}, bf16[3,3,256,256]{3,2,1,0:T(8,128)(2,1)}, u32[]{:S(2)}) copy-start(bf16[3,3,256,256]{3,2,1,0:T(8,128)(2,1)} %param.18) | copy-start | bytes 3538948
  3.6 62.4 %copy-start.8 = (bf16[4,256]{1,0:T(4,128)(2,1)S(1)}, bf16[4,256]{1,0:T(4,128)(2,1)}, u32[]{:S(2)}) copy-start(bf16[4,256]{1,0:T(4,128)(2,1)} %gains.3) | copy-start | bytes 6148
  44.6 5.9 %collective-permute-start = (bf16[16,8,256]{2,1,0:T(8,128)(2,1)S(1)}, bf16[16,8,256]{2,1,0:T(8,128)(2,1)S(1)}, u32[]{:S(2)}, u32[]{:S(2)}) collective-permute-start(bf16[16,8,256]{2,1,0:T(8,128)(2,1)S(1)} %get-tuple-element.18), channel_id=1, source_target_pairs={{0,7},{1,4},{2,5},{3,6},{4,11},{5,8},{6,9},{7,10},{8,15},{9,12},{1... | collective-permute-start | bytes 196616 | tf_op jit(solution)/shard_map/ppermute | solution.py:379
  46.9 6.6 %collective-permute-start.1 = (bf16[16,8,256]{2,1,0:T(8,128)(2,1)S(1)}, bf16[16,8,256]{2,1,0:T(8,128)(2,1)S(1)}, u32[]{:S(2)}, u32[]{:S(2)}) collective-permute-start(bf16[16,8,256]{2,1,0:T(8,128)(2,1)S(1)} %get-tuple-element.19), channel_id=1, source_target_pairs={{0,29},{1,30},{2,31},{3,28},{4,1},{5,2},{6,3},{7,0},{8,5},{9,6},{1... | collective-permute-start | bytes 196616 | tf_op jit(solution)/shard_map/ppermute | solution.py:379
  53.6 8.6 %collective-permute-start.2 = (bf16[5,48,256]{2,1,0:T(8,128)(2,1)S(1)}, bf16[5,48,256]{2,1,0:T(8,128)(2,1)S(1)}, u32[]{:S(2)}, u32[]{:S(2)}) collective-permute-start(bf16[5,48,256]{2,1,0:T(8,128)(2,1)S(1)} %get-tuple-element.22), channel_id=1, source_target_pairs={{0,35},{1,32},{2,33},{3,34},{4,39},{5,36},{6,37},{7,38},{8,43},{9,... | collective-permute-start | bytes 368648 | tf_op jit(solution)/shard_map/ppermute | solution.py:379
  59.0 6.9 %collective-permute-start.3 = (bf16[5,48,256]{2,1,0:T(8,128)(2,1)S(1)}, bf16[5,48,256]{2,1,0:T(8,128)(2,1)S(1)}, u32[]{:S(2)}, u32[]{:S(2)}) collective-permute-start(bf16[5,48,256]{2,1,0:T(8,128)(2,1)S(1)} %get-tuple-element.23), channel_id=1, source_target_pairs={{0,480},{1,481},{2,482},{3,483},{4,484},{5,485},{6,486},{7,487},{8... | collective-permute-start | bytes 368648 | tf_op jit(solution)/shard_map/ppermute | solution.py:379
  69.5 38.7 %copy-start.2 = (bf16[3,3,256,256]{3,2,1,0:T(8,128)(2,1)S(1)}, bf16[3,3,256,256]{3,2,1,0:T(8,128)(2,1)}, u32[]{:S(2)}) copy-start(bf16[3,3,256,256]{3,2,1,0:T(8,128)(2,1)} %param.20) | copy-start | bytes 3538948
  69.5 38.7 %copy-start.5 = (bf16[256,256]{1,0:T(8,128)(2,1)S(1)}, bf16[256,256]{1,0:T(8,128)(2,1)}, u32[]{:S(2)}) copy-start(bf16[256,256]{1,0:T(8,128)(2,1)} %out_proj.1) | copy-start | bytes 393220
  69.5 38.7 %copy-start.6 = (bf16[256,256]{1,0:T(8,128)(2,1)S(1)}, bf16[256,256]{1,0:T(8,128)(2,1)}, u32[]{:S(2)}) copy-start(bf16[256,256]{1,0:T(8,128)(2,1)} %projector.1) | copy-start | bytes 393220

commit v6 on v5

--- a/solution.py
+++ b/solution.py
@@ -87,7 +87,7 @@
 
 def inject_kernel(
     steps, arrived, embed, tiles, film_table,
-    own, first_cols, last_cols, first_rows, last_rows, film,
+    own, first_rows, last_rows, film,
 ):
     pairs = arrived.shape[0]
     readings = embed.shape[0]
@@ -113,31 +113,36 @@
     both = dot(hot, film_table[...])
     rows = jnp.where(line((8, DEPTH)) < 4, both[:, :DEPTH], both[:, DEPTH:])
     film[...] = rows
+    extra = jnp.concatenate([rows, jnp.zeros((TILE_W - 8, DEPTH), F32)], axis=0).astype(BF16)
+    for target, start in ((first_rows, 0), (last_rows, TILE_H - HALO)):
+        target[:HALO] = fine[start : start + HALO].astype(BF16)
+        target[HALO] = extra
+
+
+def brought_film(north, south, col_at):
+    rows = north[HALO, :8].astype(F32)
+    return rows + jnp.where(lax.rem(col_at, 2) == 0, south[HALO, :8].astype(F32), 0.0)
+
+
+def widen_kernel(image_rows, north, south, own, first_cols, last_cols):
+    row_at, col_at = grid_place()
+    film = brought_film(north, south, col_at)
     at = line((SIDE, DEPTH))
-    for y in range(TILE_H):
-        first, last = fine[y, :SIDE], fine[y, -SIDE:]
-        if y < 8:
-            first = jnp.where(at == SIDE - 1, rows[y : y + 1], first)
-            last = jnp.where(at == 0, rows[y : y + 1], last)
-        first_cols[y] = first.astype(BF16)
-        last_cols[y] = last.astype(BF16)
-    first_rows[...] = fine[:HALO].astype(BF16)
-    last_rows[...] = fine[-HALO:].astype(BF16)
-
-
-def widen_kernel(west, east, first_rows, last_rows, top, bottom):
-    _, col_at = grid_place()
-    at = line((FRAME_W, DEPTH))
-    for rows, target, offset in ((first_rows, top, 0), (last_rows, bottom, TILE_H - HALO)):
-        for y in range(HALO):
-            left = jnp.where(col_at > 0, west[offset + y].astype(F32), 0.0)
-            right = jnp.where(col_at < TILE_COLS - 1, east[offset + y].astype(F32), 0.0)
-            whole = jnp.concatenate([left, rows[y].astype(F32), right], axis=0)
-            if offset:
-                whole = jnp.where(at == 0, west[y, 0:1].astype(F32), whole)
-                if y + HALO < 8:
-                    whole = jnp.where(at == 1, west[y + HALO, 0:1].astype(F32), whole)
-            target[y] = whole.astype(BF16)
+    for y in range(FRAME_H):
+        for target, cols in (
+            (first_cols, slice(0, SIDE)),
+            (last_cols, slice(TILE_W - SIDE, TILE_W)),
+        ):
+            if y < HALO:
+                rows = jnp.where(row_at > 0, north[y, cols].astype(F32), 0.0)
+            elif y < HALO + TILE_H:
+                rows = own[y - HALO, cols]
+            else:
+                rows = south[y - HALO - TILE_H, cols].astype(F32)
+                rows = jnp.where(row_at < image_rows - 1, rows, 0.0)
+            if y < 8 and target is last_cols:
+                rows = jnp.where(at == 0, film[y : y + 1], rows)
+            target[y] = rows.astype(BF16)
 
 
 def trunk_kernel(
@@ -148,19 +153,18 @@
 ):
     row_at, col_at = grid_place()
     left = west[...].astype(F32)
-    right = east[...].astype(F32)
-    above = north[...].astype(F32)
     at = line((8, DEPTH))
-    rows = film[...]
+    rows = film[...] + brought_film(north, south, col_at)
     for y in range(8):
-        extra = above[y, 0:1] if y < HALO else above[y - HALO, 1:2]
-        rows += jnp.where(at == y, left[y, 0:1] + right[y, SIDE - 1 : SIDE] + extra, 0.0)
+        rows += jnp.where(at == y, left[y, 0:1], 0.0)
     film_ref[...] = rows
-    frame[:HALO] = jnp.where(row_at > 0, above, 0.0)
-    frame[HALO + TILE_H :] = jnp.where(row_at < image_rows - 1, south[...].astype(F32), 0.0)
-    frame[HALO : HALO + TILE_H, :SIDE] = jnp.where(col_at > 0, left, 0.0)
-    frame[HALO : HALO + TILE_H, SIDE : SIDE + TILE_W] = own[...]
-    frame[HALO : HALO + TILE_H, SIDE + TILE_W :] = jnp.where(col_at < TILE_COLS - 1, right, 0.0)
+    above, below = north[:HALO].astype(F32), south[:HALO].astype(F32)
+    inner = slice(SIDE, SIDE + TILE_W)
+    frame[:HALO, inner] = jnp.where(row_at > 0, above, 0.0)
+    frame[HALO : HALO + TILE_H, inner] = own[...]
+    frame[HALO + TILE_H :, inner] = jnp.where(row_at < image_rows - 1, below, 0.0)
+    frame[:, :SIDE] = jnp.where(col_at > 0, left, 0.0)
+    frame[:, SIDE + TILE_W :] = jnp.where(col_at < TILE_COLS - 1, east[...].astype(F32), 0.0)
     gain = gains[0:1].astype(F32)
     for y in range(FRAME_H):
         normed = rms_scale(frame[y], gain)
@@ -306,10 +310,8 @@
         inject_kernel,
         [
             ((TILE_H, TILE_W, DEPTH), F32),
-            ((TILE_H, SIDE, DEPTH), BF16),
-            ((TILE_H, SIDE, DEPTH), BF16),
-            ((HALO, TILE_W, DEPTH), BF16),
-            ((HALO, TILE_W, DEPTH), BF16),
+            ((HALO + 1, TILE_W, DEPTH), BF16),
+            ((HALO + 1, TILE_W, DEPTH), BF16),
             ((8, DEPTH), F32),
         ],
         [],
@@ -319,10 +321,13 @@
     )
 
 
-def widen(west, east, first_rows, last_rows):
-    shape = (HALO, FRAME_W, DEPTH)
+def widen(image_rows, north, south, own):
+    shape = (FRAME_H, SIDE, DEPTH)
     return call(
-        widen_kernel, [(shape, BF16), (shape, BF16)], [], [west, east, first_rows, last_rows]
+        functools.partial(widen_kernel, image_rows),
+        [(shape, BF16), (shape, BF16)],
+        [],
+        [north, south, own],
     )
 
 
@@ -367,7 +372,7 @@
     )
 
 
-def shifted(value, row_step, col_step, lead_step):
+def shifted(value, row_step, col_step, lead_steps=(0, 0)):
     rows, leads = lax.axis_size("space") // TILE_COLS, lax.axis_size("lead")
     pairs = []
     for row in range(rows):
@@ -375,7 +380,7 @@
             for lead in range(leads):
                 source = (row * TILE_COLS + col) * leads + lead
                 there = (row + row_step) % rows * TILE_COLS + (col + col_step) % TILE_COLS
-                pairs.append((source, there * leads + (lead - lead_step) % leads))
+                pairs.append((source, there * leads + (lead - lead_steps[col % 2]) % leads))
     return lax.ppermute(value, ("space", "lead"), pairs)
 
 
@@ -410,18 +415,19 @@
     arrived = lax.all_to_all(
         payload.reshape(space_count, 2, 3 * readings), "space", 0, 0, tiled=True
     ).reshape(2 * space_count, 3 * readings)
-    own, first_cols, last_cols, first_rows, last_rows, film = inject(
+    own, first_rows, last_rows, film = inject(
         horizon_step_list, arrived, station_embed, tiles.reshape(CELLS, DEPTH), film_table
     )
 
-    west = shifted(last_cols, 0, 1, 1)
-    east = shifted(first_cols, 0, -1, -1)
-    top, bottom = widen(west, east, first_rows, last_rows)
-    north = shifted(bottom, 1, 0, 1)
-    south = shifted(top, -1, 0, 0)
+    image_rows = space_count // TILE_COLS
+    north = shifted(last_rows, 1, 0, (1, 2))
+    south = shifted(first_rows, -1, 0, (-1, 0))
+    first_cols, last_cols = widen(image_rows, north, south, own)
+    west = shifted(last_cols, 0, 1)
+    east = shifted(first_cols, 0, -1)
 
     partial, parcel, film = trunk(
-        space_count // TILE_COLS,
+        image_rows,
         north, south, west, east, own, film, conv_fine, conv_mid, norm_gains, arrived,
     )
     returned = lax.all_to_all(

time: 112 us -> 110 us (0.982)
  the two profiles are of different devices: /device:TPU:35 before, /device:TPU:33 now
where the time goes in v6:
time: 110 us; the launch traced here: 109 us
  blocking collectives  78.5 us (71%)
  starting transfers between devices  10.9 us (10%)
  Pallas kernels  8.39 us (8%)
  waiting for transfers between devices  7.31 us (7%)
  local copies, waits for them, and re-layouts  1.83 us (2%)
  other arithmetic  1.43 us (1%)
    all_to_all x1, blocking collectives, body(): lax.all_to_all(parcel.reshape(space_count, 2, 3 * DEPTH), 'space', 0, 0,...  39.3 us
    all_to_all x1, blocking collectives, body(): lax.all_to_all(payload.reshape(space_count, 2, 3 * readings), 'space', 0,...  39.2 us
    ppermute x4, starting transfers between devices, shifted(): return lax.ppermute(value, ('space', 'lead'), pairs)  10.9 us
    pallas_call x5, Pallas kernels, call(): pl.pallas_call(kernel, out_shape=[jax.ShapeDtypeStruct(shape, dtype) for...  8.39 us
    ppermute x4, waiting for transfers between devices, shifted(): return lax.ppermute(value, ('space', 'lead'), pairs)  7.31 us
  transfers between devices with their start and end apart: 4, of which 4 were waited for; matrix products, arithmetic and copies ran while one was open for 0% of the time, Pallas kernels for 0%

profile of v6, /device:TPU:33, one launch (start us, length us, event | category | flops | bytes accessed | tf_op | source)
XLA Modules:
  0.0 109.2 jit_solution(9811272807814004371)
XLA Ops:
  0.7 0.7 convert_element_type.9
  1.4 0.7 fusion
  2.1 0.1 copy.16
  2.2 0.1 broadcast_in_dim.13
  2.4 0.1 broadcast_in_dim.12
  2.5 1.0 concatenate.3.records
  3.5 0.6 shard_map.140
  4.0 0.1 reshape.34
  4.1 0.0 copy-start
  4.1 39.2 %all_to_all.10 = bf16[128,2,384]{2,1,0:T(2,128)(2,1)S(1)} all-to-all(bf16[128,2,384]{2,1,0:T(2,128)(2,1)S(1)} %reshape.34), channel_id=1, replica_groups=mesh['space'=128,'lead'=4] {'space'}, dimensions={0} | all-to-all | bytes 393216 | tf_op jit(solution)/shard_map/all_to_all | solution.py:415
  43.4 0.1 reshape.35.arrived
  43.5 1.1 %shard_map.141 = (f32[16,32,256]{2,1,0:T(8,128)S(1)}, bf16[6,32,256]{2,1,0:T(8,128)(2,1)S(1)}, bf16[6,32,256]{2,1,0:T(8,128)(2,1)S(1)}, f32[8,256]{1,0:T(8,128)S(1)}) custom-call(s32[4]{0:T(128)S(1)} %copy-done.9, bf16[256,384]{1,0:T(8,128)(2,1)S(1)} %reshape.35.arrived, bf16[128,256]{1,0:T(8,128)(2,1)S(1)} %copy-done.7, bf16[512,256]{1,0:T(8,128)(2,1)S(1)} %bitcast.9, ...), custom_call_target="tpu_custom_call" | custom-call | tf_op jit(solution)/shard_map/pallas_call | solution.py:292
  44.6 4.9 %collective-permute-start = (bf16[6,32,256]{2,1,0:T(8,128)(2,1)S(1)}, bf16[6,32,256]{2,1,0:T(8,128)(2,1)S(1)}, u32[]{:S(2)}, u32[]{:S(2)}) collective-permute-start(bf16[6,32,256]{2,1,0:T(8,128)(2,1)S(1)} %get-tuple-element.16), channel_id=1, source_target_pairs={{0,35},{1,32},{2,33},{3,34},{4,38},{5,39},{6,36},{7,37},{8,43},{9,... | collective-permute-start | bytes 294920 | tf_op jit(solution)/shard_map/ppermute | solution.py:384
  49.5 2.8 %collective-permute-start.1 = (bf16[6,32,256]{2,1,0:T(8,128)(2,1)S(1)}, bf16[6,32,256]{2,1,0:T(8,128)(2,1)S(1)}, u32[]{:S(2)}, u32[]{:S(2)}) collective-permute-start(bf16[6,32,256]{2,1,0:T(8,128)(2,1)S(1)} %get-tuple-element.17), channel_id=1, source_target_pairs={{0,481},{1,482},{2,483},{3,480},{4,484},{5,485},{6,486},{7,487},{8... | collective-permute-start | bytes 294920 | tf_op jit(solution)/shard_map/ppermute | solution.py:384
  52.4 0.2 collective-permute-done.north
  52.6 2.7 %collective-permute-done.1.south = bf16[6,32,256]{2,1,0:T(8,128)(2,1)S(1)} collective-permute-done((bf16[6,32,256]{2,1,0:T(8,128)(2,1)S(1)}, bf16[6,32,256]{2,1,0:T(8,128)(2,1)S(1)}, u32[]{:S(2)}, u32[]{:S(2)}) %collective-permute-start.1) | collective-permute-done | bytes 98336 | tf_op jit(solution)/shard_map/ppermute | solution.py:384
  55.3 3.1 %collective-permute-start.2 = (bf16[26,8,256]{2,1,0:T(8,128)(2,1)S(1)}, bf16[26,8,256]{2,1,0:T(8,128)(2,1)S(1)}, u32[]{:S(2)}, u32[]{:S(2)}) collective-permute-start(bf16[26,8,256]{2,1,0:T(8,128)(2,1)S(1)} %get-tuple-element.19), channel_id=1, source_target_pairs={{0,4},{1,5},{2,6},{3,7},{4,8},{5,9},{6,10},{7,11},{8,12},{9,13},{1... | collective-permute-start | bytes 319496 | tf_op jit(solution)/shard_map/ppermute | solution.py:384
  58.4 1.7 %collective-permute-done.2.west = bf16[26,8,256]{2,1,0:T(8,128)(2,1)S(1)} collective-permute-done((bf16[26,8,256]{2,1,0:T(8,128)(2,1)S(1)}, bf16[26,8,256]{2,1,0:T(8,128)(2,1)S(1)}, u32[]{:S(2)}, u32[]{:S(2)}) %collective-permute-start.2) | collective-permute-done | bytes 106528 | tf_op jit(solution)/shard_map/ppermute | solution.py:384
  60.1 2.7 %collective-permute-done.3.east = bf16[26,8,256]{2,1,0:T(8,128)(2,1)S(1)} collective-permute-done((bf16[26,8,256]{2,1,0:T(8,128)(2,1)S(1)}, bf16[26,8,256]{2,1,0:T(8,128)(2,1)S(1)}, u32[]{:S(2)}, u32[]{:S(2)}) %collective-permute-start.3) | collective-permute-done | bytes 106528 | tf_op jit(solution)/shard_map/ppermute | solution.py:384
  62.8 3.5 %shard_map.143 = (f32[512,256]{1,0:T(8,128)S(1)}, bf16[256,768]{1,0:T(8,128)(2,1)S(1)}, f32[8,256]{1,0:T(8,128)S(1)}) custom-call(bf16[6,32,256]{2,1,0:T(8,128)(2,1)S(1)} %collective-permute-done.north, bf16[6,32,256]{2,1,0:T(8,128)(2,1)S(1)} %collective-permute-done.1.south, bf16[26,8,256]{2,1,0:T(8,128)(2,1)S(1)} %collective-permute-done.2.west, ...), custom_call_target="tpu_custom_call" | custom-call | tf_op jit(solution)/shard_map/pallas_call | solution.py:292
  66.4 0.1 reshape.39
  66.6 39.3 %all_to_all.11 = bf16[128,2,768]{2,1,0:T(2,128)(2,1)S(1)} all-to-all(bf16[128,2,768]{2,1,0:T(2,128)(2,1)S(1)} %reshape.39), channel_id=1, replica_groups=mesh['space'=128,'lead'=4] {'space'}, dimensions={0} | all-to-all | bytes 786432 | tf_op jit(solution)/shard_map/all_to_all | solution.py:433
  105.9 0.1 reshape.40.returned
  106.0 3.2 %shard_map.144 = (bf16[512,256]{1,0:T(8,128)(2,1)}, bf16[256,256]{1,0:T(8,128)(2,1)}) custom-call(bf16[256,768]{1,0:T(8,128)(2,1)S(1)} %reshape.40.returned, bf16[3,768,256]{2,1,0:T(8,128)(2,1)S(1)} %bitcast.8, bf16[4,256]{1,0:T(4,128)(2,1)S(1)} %copy-done.8, f32[512,256]{1,0:T(8,128)S(1)} %get-tuple-element.23.partial, ...), custom_call_target="tpu_custom_call" | custom-call | tf_op jit(solution)/shard_map/pallas_call | solution.py:292
  (22 shorter events, 0.1 us)
Async XLA Ops:
  0.6 42.8 %copy-start.9 = (s32[4]{0:T(128)S(1)}, s32[4]{0:T(128)}, u32[]{:S(2)}) copy-start(s32[4]{0:T(128)} %steps.1) | copy-start | bytes 52
  0.6 42.8 %copy-start.4 = (bf16[180,512]{1,0:T(8,128)(2,1)S(1)}, bf16[180,512]{1,0:T(8,128)(2,1)}, u32[]{:S(2)}) copy-start(bf16[180,512]{1,0:T(8,128)(2,1)} %film_table.1) | copy-start | bytes 552964
  0.7 42.8 %copy-start.7 = (bf16[128,256]{1,0:T(8,128)(2,1)S(1)}, bf16[128,256]{1,0:T(8,128)(2,1)}, u32[]{:S(2)}) copy-start(bf16[128,256]{1,0:T(8,128)(2,1)} %embed.1) | copy-start | bytes 196612
  0.7 42.8 %copy-start.3 = (bf16[1,16,32,256]{3,2,1,0:T(8,128)(2,1)S(1)}, bf16[1,16,32,256]{3,2,1,0:T(8,128)(2,1)}, u32[]{:S(2)}) copy-start(bf16[1,16,32,256]{3,2,1,0:T(8,128)(2,1)} %param.13) | copy-start | bytes 786436
  4.0 58.8 %copy-start.1 = (bf16[3,3,256,256]{3,2,1,0:T(8,128)(2,1)S(1)}, bf16[3,3,256,256]{3,2,1,0:T(8,128)(2,1)}, u32[]{:S(2)}) copy-start(bf16[3,3,256,256]{3,2,1,0:T(8,128)(2,1)} %param.19) | copy-start | bytes 3538948
  4.1 58.7 %copy-start = (bf16[3,3,256,256]{3,2,1,0:T(8,128)(2,1)S(1)}, bf16[3,3,256,256]{3,2,1,0:T(8,128)(2,1)}, u32[]{:S(2)}) copy-start(bf16[3,3,256,256]{3,2,1,0:T(8,128)(2,1)} %param.18) | copy-start | bytes 3538948
  4.1 58.7 %copy-start.8 = (bf16[4,256]{1,0:T(4,128)(2,1)S(1)}, bf16[4,256]{1,0:T(4,128)(2,1)}, u32[]{:S(2)}) copy-start(bf16[4,256]{1,0:T(4,128)(2,1)} %gains.3) | copy-start | bytes 6148
  44.6 8.0 %collective-permute-start = (bf16[6,32,256]{2,1,0:T(8,128)(2,1)S(1)}, bf16[6,32,256]{2,1,0:T(8,128)(2,1)S(1)}, u32[]{:S(2)}, u32[]{:S(2)}) collective-permute-start(bf16[6,32,256]{2,1,0:T(8,128)(2,1)S(1)} %get-tuple-element.16), channel_id=1, source_target_pairs={{0,35},{1,32},{2,33},{3,34},{4,38},{5,39},{6,36},{7,37},{8,43},{9,... | collective-permute-start | bytes 294920 | tf_op jit(solution)/shard_map/ppermute | solution.py:384
  49.5 5.7 %collective-permute-start.1 = (bf16[6,32,256]{2,1,0:T(8,128)(2,1)S(1)}, bf16[6,32,256]{2,1,0:T(8,128)(2,1)S(1)}, u32[]{:S(2)}, u32[]{:S(2)}) collective-permute-start(bf16[6,32,256]{2,1,0:T(8,128)(2,1)S(1)} %get-tuple-element.17), channel_id=1, source_target_pairs={{0,481},{1,482},{2,483},{3,480},{4,484},{5,485},{6,486},{7,487},{8... | collective-permute-start | bytes 294920 | tf_op jit(solution)/shard_map/ppermute | solution.py:384
  55.3 4.8 %collective-permute-start.2 = (bf16[26,8,256]{2,1,0:T(8,128)(2,1)S(1)}, bf16[26,8,256]{2,1,0:T(8,128)(2,1)S(1)}, u32[]{:S(2)}, u32[]{:S(2)}) collective-permute-start(bf16[26,8,256]{2,1,0:T(8,128)(2,1)S(1)} %get-tuple-element.19), channel_id=1, source_target_pairs={{0,4},{1,5},{2,6},{3,7},{4,8},{5,9},{6,10},{7,11},{8,12},{9,13},{1... | collective-permute-start | bytes 319496 | tf_op jit(solution)/shard_map/ppermute | solution.py:384
  58.4 4.4 %collective-permute-start.3 = (bf16[26,8,256]{2,1,0:T(8,128)(2,1)S(1)}, bf16[26,8,256]{2,1,0:T(8,128)(2,1)S(1)}, u32[]{:S(2)}, u32[]{:S(2)}) collective-permute-start(bf16[26,8,256]{2,1,0:T(8,128)(2,1)S(1)} %get-tuple-element.20), channel_id=1, source_target_pairs={{0,28},{1,29},{2,30},{3,31},{4,0},{5,1},{6,2},{7,3},{8,4},{9,5},{1... | collective-permute-start | bytes 319496 | tf_op jit(solution)/shard_map/ppermute | solution.py:384
  66.4 39.6 %copy-start.2 = (bf16[3,3,256,256]{3,2,1,0:T(8,128)(2,1)S(1)}, bf16[3,3,256,256]{3,2,1,0:T(8,128)(2,1)}, u32[]{:S(2)}) copy-start(bf16[3,3,256,256]{3,2,1,0:T(8,128)(2,1)} %param.20) | copy-start | bytes 3538948
  66.4 39.6 %copy-start.5 = (bf16[256,256]{1,0:T(8,128)(2,1)S(1)}, bf16[256,256]{1,0:T(8,128)(2,1)}, u32[]{:S(2)}) copy-start(bf16[256,256]{1,0:T(8,128)(2,1)} %out_proj.1) | copy-start | bytes 393220
  66.4 39.6 %copy-start.6 = (bf16[256,256]{1,0:T(8,128)(2,1)S(1)}, bf16[256,256]{1,0:T(8,128)(2,1)}, u32[]{:S(2)}) copy-start(bf16[256,256]{1,0:T(8,128)(2,1)} %projector.1) | copy-start | bytes 393220

commit v7 on v6

--- a/solution.py
+++ b/solution.py
@@ -108,20 +108,19 @@
     sort = line((8, table_rows))
     at = jnp.full((8, table_rows), -1, jnp.int32)
     for i in range(4):
-        at = jnp.where((sort & 3) == i, steps[i] - offset, at)
+        at = jnp.where((sort & 3) == i, steps[0:1, i : i + 1] - offset, at)
     hot = ones_where(column((8, table_rows)) == at)
     both = dot(hot, film_table[...])
     rows = jnp.where(line((8, DEPTH)) < 4, both[:, :DEPTH], both[:, DEPTH:])
     film[...] = rows
-    extra = jnp.concatenate([rows, jnp.zeros((TILE_W - 8, DEPTH), F32)], axis=0).astype(BF16)
     for target, start in ((first_rows, 0), (last_rows, TILE_H - HALO)):
-        target[:HALO] = fine[start : start + HALO].astype(BF16)
-        target[HALO] = extra
+        edge = fine[start : start + HALO].reshape(HALO * TILE_W, DEPTH)
+        target[...] = jnp.concatenate([edge, rows], axis=0).astype(BF16)
 
 
 def brought_film(north, south, col_at):
-    rows = north[HALO, :8].astype(F32)
-    return rows + jnp.where(lax.rem(col_at, 2) == 0, south[HALO, :8].astype(F32), 0.0)
+    above, below = (rows[HALO * TILE_W :].astype(F32) for rows in (north, south))
+    return above + jnp.where(lax.rem(col_at, 2) == 0, below, 0.0)
 
 
 def widen_kernel(image_rows, north, south, own, first_cols, last_cols):
@@ -133,12 +132,14 @@
             (first_cols, slice(0, SIDE)),
             (last_cols, slice(TILE_W - SIDE, TILE_W)),
         ):
+            start = y % (HALO + TILE_H) * TILE_W + cols.start
             if y < HALO:
-                rows = jnp.where(row_at > 0, north[y, cols].astype(F32), 0.0)
+                rows = north[start : start + SIDE].astype(F32)
+                rows = jnp.where(row_at > 0, rows, 0.0)
             elif y < HALO + TILE_H:
                 rows = own[y - HALO, cols]
             else:
-                rows = south[y - HALO - TILE_H, cols].astype(F32)
+                rows = south[start : start + SIDE].astype(F32)
                 rows = jnp.where(row_at < image_rows - 1, rows, 0.0)
             if y < 8 and target is last_cols:
                 rows = jnp.where(at == 0, film[y : y + 1], rows)
@@ -158,7 +159,9 @@
     for y in range(8):
         rows += jnp.where(at == y, left[y, 0:1], 0.0)
     film_ref[...] = rows
-    above, below = north[:HALO].astype(F32), south[:HALO].astype(F32)
+    above, below = (
+        rows[: HALO * TILE_W].astype(F32).reshape(HALO, TILE_W, DEPTH) for rows in (north, south)
+    )
     inner = slice(SIDE, SIDE + TILE_W)
     frame[:HALO, inner] = jnp.where(row_at > 0, above, 0.0)
     frame[HALO : HALO + TILE_H, inner] = own[...]
@@ -285,14 +288,13 @@
     put_scores.wait()
 
 
-def call(kernel, outs, scratch, operands, hbm_outs=(), scalars=0, megabytes=4):
+def call(kernel, outs, scratch, operands, hbm_outs=(), megabytes=4):
     vmem = pl.BlockSpec(memory_space=pltpu.VMEM)
     hbm = pl.BlockSpec(memory_space=pltpu.HBM)
-    smem = pl.BlockSpec(memory_space=pltpu.SMEM)
     return pl.pallas_call(
         kernel,
         out_shape=[jax.ShapeDtypeStruct(shape, dtype) for shape, dtype in outs],
-        in_specs=[smem] * scalars + [vmem] * (len(operands) - scalars),
+        in_specs=[vmem] * len(operands),
         out_specs=[hbm if i in hbm_outs else vmem for i in range(len(outs))],
         scratch_shapes=scratch,
         compiler_params=pltpu.CompilerParams(vmem_limit_bytes=megabytes * 2**20),
@@ -310,13 +312,12 @@
         inject_kernel,
         [
             ((TILE_H, TILE_W, DEPTH), F32),
-            ((HALO + 1, TILE_W, DEPTH), BF16),
-            ((HALO + 1, TILE_W, DEPTH), BF16),
+            ((HALO * TILE_W + 8, DEPTH), BF16),
+            ((HALO * TILE_W + 8, DEPTH), BF16),
             ((8, DEPTH), F32),
         ],
         [],
         [steps, arrived, embed, tiles, film_table],
-        scalars=1,
         megabytes=8,
     )
 
@@ -401,22 +402,17 @@
 ):
     space_count = lax.axis_size("space")
     count, readings = station_obs.shape
-    records = jnp.concatenate(
-        [
-            station_obs,
-            station_tile.astype(BF16),
-            (station_pixel // 16).astype(BF16)[:, None],
-            (station_pixel % 16).astype(BF16)[:, None],
-            jnp.zeros((count, readings - 3), BF16),
-        ],
-        axis=1,
-    )
+    col = column((count, readings))
+    ids = jnp.where(col == 2, station_pixel[:, None] & 15, 0)
+    ids = jnp.where(col == 1, station_pixel[:, None] >> 4, ids)
+    ids = jnp.where(col == 0, station_tile, ids)
+    records = jnp.concatenate([station_obs, ids.astype(BF16)], axis=1)
     payload, lookup = pack(records, space_count)
     arrived = lax.all_to_all(
         payload.reshape(space_count, 2, 3 * readings), "space", 0, 0, tiled=True
     ).reshape(2 * space_count, 3 * readings)
     own, first_rows, last_rows, film = inject(
-        horizon_step_list, arrived, station_embed, tiles.reshape(CELLS, DEPTH), film_table
+        horizon_step_list.reshape(1, -1), arrived, station_embed, tiles.reshape(CELLS, DEPTH), film_table
     )
 
     image_rows = space_count // TILE_COLS

time: 110 us -> 109 us (level)
  local copies, waits for them, and re-layouts: 1.83 us -> 0.5 us
  transfers between devices with their start and end apart: 4 -> 4, of which waited for: 4 -> 3; matrix products, arithmetic and copies ran while one was open for 0% -> 0% of each run, Pallas kernels for 0% -> 0%
where the time goes in v7:
time: 109 us; the launch traced here: 108 us
  blocking collectives  78.5 us (72%)
  starting transfers between devices  11 us (10%)
  Pallas kernels  7.85 us (7%)
  waiting for transfers between devices  7.04 us (6%)
  other arithmetic  2.48 us (2%)
    all_to_all x1, blocking collectives, body(): lax.all_to_all(parcel.reshape(space_count, 2, 3 * DEPTH), 'space', 0, 0,...  39.3 us
    all_to_all x1, blocking collectives, body(): lax.all_to_all(payload.reshape(space_count, 2, 3 * readings), 'space', 0,...  39.2 us
    ppermute x4, starting transfers between devices, shifted(): return lax.ppermute(value, ('space', 'lead'), pairs)  11 us
    pallas_call x5, Pallas kernels, call(): pl.pallas_call(kernel, out_shape=[jax.ShapeDtypeStruct(shape, dtype) for...  7.85 us
    ppermute x4, waiting for transfers between devices, shifted(): return lax.ppermute(value, ('space', 'lead'), pairs)  7.04 us
  transfers between devices with their start and end apart: 4, of which 3 were waited for; matrix products, arithmetic and copies ran while one was open for 0% of the time, Pallas kernels for 0%

profile of v7, /device:TPU:33, one launch (start us, length us, event | category | flops | bytes accessed | tf_op | source)
XLA Modules:
  0.0 108.3 jit_solution(9152429239232603135)
XLA Ops:
  0.7 0.8 broadcast_shift-right-arithmetic_fusion
  1.5 0.8 select_convert_fusion
  2.3 0.9 pad_maximum_fusion.records
  3.2 0.6 shard_map.140
  3.7 0.0 copy-start.1
  3.8 0.1 reshape.42
  3.8 0.0 copy-start
  3.8 0.0 copy-start.8
  3.9 39.2 %all_to_all.10 = bf16[128,2,384]{2,1,0:T(2,128)(2,1)S(1)} all-to-all(bf16[128,2,384]{2,1,0:T(2,128)(2,1)S(1)} %reshape.42), channel_id=1, replica_groups=mesh['space'=128,'lead'=4] {'space'}, dimensions={0} | all-to-all | bytes 393216 | tf_op jit(solution)/shard_map/all_to_all | solution.py:411
  43.1 0.1 reshape.43.arrived
  43.2 0.6 shard_map.141
  43.8 4.9 %collective-permute-start = (bf16[168,256]{1,0:T(8,128)(2,1)S(1)}, bf16[168,256]{1,0:T(8,128)(2,1)S(1)}, u32[]{:S(2)}, u32[]{:S(2)}) collective-permute-start(bf16[168,256]{1,0:T(8,128)(2,1)S(1)} %get-tuple-element.16), channel_id=1, source_target_pairs={{0,35},{1,32},{2,33},{3,34},{4,38},{5,39},{6,36},{7,37},{8,43},{9,... | collective-permute-start | bytes 258056 | tf_op jit(solution)/shard_map/ppermute | solution.py:385
  48.7 2.8 %collective-permute-start.1 = (bf16[168,256]{1,0:T(8,128)(2,1)S(1)}, bf16[168,256]{1,0:T(8,128)(2,1)S(1)}, u32[]{:S(2)}, u32[]{:S(2)}) collective-permute-start(bf16[168,256]{1,0:T(8,128)(2,1)S(1)} %get-tuple-element.17), channel_id=1, source_target_pairs={{0,481},{1,482},{2,483},{3,480},{4,484},{5,485},{6,486},{7,487},{8... | collective-permute-start | bytes 258056 | tf_op jit(solution)/shard_map/ppermute | solution.py:385
  51.5 2.6 %collective-permute-done.1.south = bf16[168,256]{1,0:T(8,128)(2,1)S(1)} collective-permute-done((bf16[168,256]{1,0:T(8,128)(2,1)S(1)}, bf16[168,256]{1,0:T(8,128)(2,1)S(1)}, u32[]{:S(2)}, u32[]{:S(2)}) %collective-permute-start.1) | collective-permute-done | bytes 86048 | tf_op jit(solution)/shard_map/ppermute | solution.py:385
  54.2 3.2 %collective-permute-start.2 = (bf16[26,8,256]{2,1,0:T(8,128)(2,1)S(1)}, bf16[26,8,256]{2,1,0:T(8,128)(2,1)S(1)}, u32[]{:S(2)}, u32[]{:S(2)}) collective-permute-start(bf16[26,8,256]{2,1,0:T(8,128)(2,1)S(1)} %get-tuple-element.19), channel_id=1, source_target_pairs={{0,4},{1,5},{2,6},{3,7},{4,8},{5,9},{6,10},{7,11},{8,12},{9,13},{1... | collective-permute-start | bytes 319496 | tf_op jit(solution)/shard_map/ppermute | solution.py:385
  57.4 1.7 %collective-permute-done.2.west = bf16[26,8,256]{2,1,0:T(8,128)(2,1)S(1)} collective-permute-done((bf16[26,8,256]{2,1,0:T(8,128)(2,1)S(1)}, bf16[26,8,256]{2,1,0:T(8,128)(2,1)S(1)}, u32[]{:S(2)}, u32[]{:S(2)}) %collective-permute-start.2) | collective-permute-done | bytes 106528 | tf_op jit(solution)/shard_map/ppermute | solution.py:385
  59.2 2.7 %collective-permute-done.3.east = bf16[26,8,256]{2,1,0:T(8,128)(2,1)S(1)} collective-permute-done((bf16[26,8,256]{2,1,0:T(8,128)(2,1)S(1)}, bf16[26,8,256]{2,1,0:T(8,128)(2,1)S(1)}, u32[]{:S(2)}, u32[]{:S(2)}) %collective-permute-start.3) | collective-permute-done | bytes 106528 | tf_op jit(solution)/shard_map/ppermute | solution.py:385
  61.9 3.5 %shard_map.143 = (f32[512,256]{1,0:T(8,128)S(1)}, bf16[256,768]{1,0:T(8,128)(2,1)S(1)}, f32[8,256]{1,0:T(8,128)S(1)}) custom-call(bf16[168,256]{1,0:T(8,128)(2,1)S(1)} %collective-permute-done.north, bf16[168,256]{1,0:T(8,128)(2,1)S(1)} %collective-permute-done.1.south, bf16[26,8,256]{2,1,0:T(8,128)(2,1)S(1)} %collective-permute-done.2.west, ...), custom_call_target="tpu_custom_call" | custom-call | tf_op jit(solution)/shard_map/pallas_call | solution.py:294
  65.4 0.0 copy-start.5
  65.4 0.0 copy-start.6
  65.4 0.1 reshape.47
  65.6 39.3 %all_to_all.11 = bf16[128,2,768]{2,1,0:T(2,128)(2,1)S(1)} all-to-all(bf16[128,2,768]{2,1,0:T(2,128)(2,1)S(1)} %reshape.47), channel_id=1, replica_groups=mesh['space'=128,'lead'=4] {'space'}, dimensions={0} | all-to-all | bytes 786432 | tf_op jit(solution)/shard_map/all_to_all | solution.py:429
  104.9 0.1 reshape.48.returned
  105.1 3.2 %shard_map.144 = (bf16[512,256]{1,0:T(8,128)(2,1)}, bf16[256,256]{1,0:T(8,128)(2,1)}) custom-call(bf16[256,768]{1,0:T(8,128)(2,1)S(1)} %reshape.48.returned, bf16[3,768,256]{2,1,0:T(8,128)(2,1)S(1)} %bitcast.10, bf16[4,256]{1,0:T(4,128)(2,1)S(1)} %copy-done.8, f32[512,256]{1,0:T(8,128)S(1)} %get-tuple-element.23.partial, ...), custom_call_target="tpu_custom_call" | custom-call | tf_op jit(solution)/shard_map/pallas_call | solution.py:294
  (20 shorter events, 0.1 us)
Async XLA Ops:
  0.6 42.5 %copy-start.9 = (s32[4]{0:T(128)S(1)}, s32[4]{0:T(128)}, u32[]{:S(2)}) copy-start(s32[4]{0:T(128)} %param.23) | copy-start | bytes 52
  0.6 42.5 %copy-start.4 = (bf16[180,512]{1,0:T(8,128)(2,1)S(1)}, bf16[180,512]{1,0:T(8,128)(2,1)}, u32[]{:S(2)}) copy-start(bf16[180,512]{1,0:T(8,128)(2,1)} %film_table.1) | copy-start | bytes 552964
  0.7 42.5 %copy-start.7 = (bf16[128,256]{1,0:T(8,128)(2,1)S(1)}, bf16[128,256]{1,0:T(8,128)(2,1)}, u32[]{:S(2)}) copy-start(bf16[128,256]{1,0:T(8,128)(2,1)} %embed.1) | copy-start | bytes 196612
  0.7 42.5 %copy-start.3 = (bf16[1,16,32,256]{3,2,1,0:T(8,128)(2,1)S(1)}, bf16[1,16,32,256]{3,2,1,0:T(8,128)(2,1)}, u32[]{:S(2)}) copy-start(bf16[1,16,32,256]{3,2,1,0:T(8,128)(2,1)} %param.13) | copy-start | bytes 786436
  3.7 58.1 %copy-start.1 = (bf16[3,3,256,256]{3,2,1,0:T(8,128)(2,1)S(1)}, bf16[3,3,256,256]{3,2,1,0:T(8,128)(2,1)}, u32[]{:S(2)}) copy-start(bf16[3,3,256,256]{3,2,1,0:T(8,128)(2,1)} %param.19) | copy-start | bytes 3538948
  3.8 58.0 %copy-start = (bf16[3,3,256,256]{3,2,1,0:T(8,128)(2,1)S(1)}, bf16[3,3,256,256]{3,2,1,0:T(8,128)(2,1)}, u32[]{:S(2)}) copy-start(bf16[3,3,256,256]{3,2,1,0:T(8,128)(2,1)} %param.18) | copy-start | bytes 3538948
  3.8 58.0 %copy-start.8 = (bf16[4,256]{1,0:T(4,128)(2,1)S(1)}, bf16[4,256]{1,0:T(4,128)(2,1)}, u32[]{:S(2)}) copy-start(bf16[4,256]{1,0:T(4,128)(2,1)} %gains.3) | copy-start | bytes 6148
  43.8 7.8 %collective-permute-start = (bf16[168,256]{1,0:T(8,128)(2,1)S(1)}, bf16[168,256]{1,0:T(8,128)(2,1)S(1)}, u32[]{:S(2)}, u32[]{:S(2)}) collective-permute-start(bf16[168,256]{1,0:T(8,128)(2,1)S(1)} %get-tuple-element.16), channel_id=1, source_target_pairs={{0,35},{1,32},{2,33},{3,34},{4,38},{5,39},{6,36},{7,37},{8,43},{9,... | collective-permute-start | bytes 258056 | tf_op jit(solution)/shard_map/ppermute | solution.py:385
  48.7 5.5 %collective-permute-start.1 = (bf16[168,256]{1,0:T(8,128)(2,1)S(1)}, bf16[168,256]{1,0:T(8,128)(2,1)S(1)}, u32[]{:S(2)}, u32[]{:S(2)}) collective-permute-start(bf16[168,256]{1,0:T(8,128)(2,1)S(1)} %get-tuple-element.17), channel_id=1, source_target_pairs={{0,481},{1,482},{2,483},{3,480},{4,484},{5,485},{6,486},{7,487},{8... | collective-permute-start | bytes 258056 | tf_op jit(solution)/shard_map/ppermute | solution.py:385
  54.2 5.0 %collective-permute-start.2 = (bf16[26,8,256]{2,1,0:T(8,128)(2,1)S(1)}, bf16[26,8,256]{2,1,0:T(8,128)(2,1)S(1)}, u32[]{:S(2)}, u32[]{:S(2)}) collective-permute-start(bf16[26,8,256]{2,1,0:T(8,128)(2,1)S(1)} %get-tuple-element.19), channel_id=1, source_target_pairs={{0,4},{1,5},{2,6},{3,7},{4,8},{5,9},{6,10},{7,11},{8,12},{9,13},{1... | collective-permute-start | bytes 319496 | tf_op jit(solution)/shard_map/ppermute | solution.py:385
  57.4 4.4 %collective-permute-start.3 = (bf16[26,8,256]{2,1,0:T(8,128)(2,1)S(1)}, bf16[26,8,256]{2,1,0:T(8,128)(2,1)S(1)}, u32[]{:S(2)}, u32[]{:S(2)}) collective-permute-start(bf16[26,8,256]{2,1,0:T(8,128)(2,1)S(1)} %get-tuple-element.20), channel_id=1, source_target_pairs={{0,28},{1,29},{2,30},{3,31},{4,0},{5,1},{6,2},{7,3},{8,4},{9,5},{1... | collective-permute-start | bytes 319496 | tf_op jit(solution)/shard_map/ppermute | solution.py:385
  65.4 39.7 %copy-start.2 = (bf16[3,3,256,256]{3,2,1,0:T(8,128)(2,1)S(1)}, bf16[3,3,256,256]{3,2,1,0:T(8,128)(2,1)}, u32[]{:S(2)}) copy-start(bf16[3,3,256,256]{3,2,1,0:T(8,128)(2,1)} %param.20) | copy-start | bytes 3538948
  65.4 39.7 %copy-start.5 = (bf16[256,256]{1,0:T(8,128)(2,1)S(1)}, bf16[256,256]{1,0:T(8,128)(2,1)}, u32[]{:S(2)}) copy-start(bf16[256,256]{1,0:T(8,128)(2,1)} %out_proj.1) | copy-start | bytes 393220
  65.4 39.6 %copy-start.6 = (bf16[256,256]{1,0:T(8,128)(2,1)S(1)}, bf16[256,256]{1,0:T(8,128)(2,1)}, u32[]{:S(2)}) copy-start(bf16[256,256]{1,0:T(8,128)(2,1)} %projector.1) | copy-start | bytes 393220

commit v8 on v7

--- a/solution.py
+++ b/solution.py
@@ -118,14 +118,15 @@
         target[...] = jnp.concatenate([edge, rows], axis=0).astype(BF16)
 
 
-def brought_film(north, south, col_at):
+def brought_film(north, south, row_at, col_at):
     above, below = (rows[HALO * TILE_W :].astype(F32) for rows in (north, south))
-    return above + jnp.where(lax.rem(col_at, 2) == 0, below, 0.0)
-
-
-def widen_kernel(image_rows, north, south, own, first_cols, last_cols):
+    return above + jnp.where((lax.rem(col_at, 2) == 0) | (row_at == 0), below, 0.0)
+
+
+def widen_kernel(image_rows, north, south, own, film_ref, first_cols, last_cols):
     row_at, col_at = grid_place()
-    film = brought_film(north, south, col_at)
+    edge = (row_at == 0) | (row_at == image_rows - 1)
+    film = brought_film(north, south, row_at, col_at) + jnp.where(edge, film_ref[...], 0.0)
     at = line((SIDE, DEPTH))
     for y in range(FRAME_H):
         for target, cols in (
@@ -135,12 +136,10 @@
             start = y % (HALO + TILE_H) * TILE_W + cols.start
             if y < HALO:
                 rows = north[start : start + SIDE].astype(F32)
-                rows = jnp.where(row_at > 0, rows, 0.0)
             elif y < HALO + TILE_H:
                 rows = own[y - HALO, cols]
             else:
                 rows = south[start : start + SIDE].astype(F32)
-                rows = jnp.where(row_at < image_rows - 1, rows, 0.0)
             if y < 8 and target is last_cols:
                 rows = jnp.where(at == 0, film[y : y + 1], rows)
             target[y] = rows.astype(BF16)
@@ -155,7 +154,7 @@
     row_at, col_at = grid_place()
     left = west[...].astype(F32)
     at = line((8, DEPTH))
-    rows = film[...] + brought_film(north, south, col_at)
+    rows = film[...] + brought_film(north, south, row_at, col_at)
     for y in range(8):
         rows += jnp.where(at == y, left[y, 0:1], 0.0)
     film_ref[...] = rows
@@ -163,9 +162,9 @@
         rows[: HALO * TILE_W].astype(F32).reshape(HALO, TILE_W, DEPTH) for rows in (north, south)
     )
     inner = slice(SIDE, SIDE + TILE_W)
-    frame[:HALO, inner] = jnp.where(row_at > 0, above, 0.0)
+    frame[:HALO, inner] = above
     frame[HALO : HALO + TILE_H, inner] = own[...]
-    frame[HALO + TILE_H :, inner] = jnp.where(row_at < image_rows - 1, below, 0.0)
+    frame[HALO + TILE_H :, inner] = below
     frame[:, :SIDE] = jnp.where(col_at > 0, left, 0.0)
     frame[:, SIDE + TILE_W :] = jnp.where(col_at < TILE_COLS - 1, east[...].astype(F32), 0.0)
     gain = gains[0:1].astype(F32)
@@ -322,13 +321,13 @@
     )
 
 
-def widen(image_rows, north, south, own):
+def widen(image_rows, north, south, own, film):
     shape = (FRAME_H, SIDE, DEPTH)
     return call(
         functools.partial(widen_kernel, image_rows),
         [(shape, BF16), (shape, BF16)],
         [],
-        [north, south, own],
+        [north, south, own, film],
     )
 
 
@@ -373,15 +372,15 @@
     )
 
 
-def shifted(value, row_step, col_step, lead_steps=(0, 0)):
+def shifted(value, row_step, col_step, lead_step):
     rows, leads = lax.axis_size("space") // TILE_COLS, lax.axis_size("lead")
     pairs = []
-    for row in range(rows):
+    for row in range(max(0, row_step), min(rows, rows + row_step)):
         for col in range(TILE_COLS):
+            source = (row - row_step) * TILE_COLS + (col - col_step) % TILE_COLS
             for lead in range(leads):
-                source = (row * TILE_COLS + col) * leads + lead
-                there = (row + row_step) % rows * TILE_COLS + (col + col_step) % TILE_COLS
-                pairs.append((source, there * leads + (lead - lead_steps[col % 2]) % leads))
+                other = (lead + lead_step(row, col)) % leads
+                pairs.append((source * leads + other, (row * TILE_COLS + col) * leads + lead))
     return lax.ppermute(value, ("space", "lead"), pairs)
 
 
@@ -416,11 +415,19 @@
     )
 
     image_rows = space_count // TILE_COLS
-    north = shifted(last_rows, 1, 0, (1, 2))
-    south = shifted(first_rows, -1, 0, (-1, 0))
-    first_cols, last_cols = widen(image_rows, north, south, own)
-    west = shifted(last_cols, 0, 1)
-    east = shifted(first_cols, 0, -1)
+    last = image_rows - 1
+
+    def from_above(row, col):
+        return 1 if row == last else 1 + col % 2
+
+    def from_below(row, col):
+        return 1 if row == 0 else col % 2 - 1
+
+    north = shifted(last_rows, 1, 0, from_above)
+    south = shifted(first_rows, -1, 0, from_below)
+    first_cols, last_cols = widen(image_rows, north, south, own, film)
+    west = shifted(last_cols, 0, 1, lambda row, col: 2 if row in (0, last) else 0)
+    east = shifted(first_cols, 0, -1, lambda row, col: 0)
 
     partial, parcel, film = trunk(
         image_rows,

time: 109 us -> 111 us (1.018)
  starting transfers between devices: 11 us -> 13.5 us
    ppermute x4, starting transfers between devices: 11 us -> 13.5 us  [shifted(): return lax.ppermute(value, ('space', 'lead'), pairs)]
where the time goes in v8:
time: 111 us; the launch traced here: 110 us
  blocking collectives  78.5 us (71%)
  starting transfers between devices  13.5 us (12%)
  Pallas kernels  7.84 us (7%)
  waiting for transfers between devices  6.44 us (6%)
  other arithmetic  2.48 us (2%)
    all_to_all x1, blocking collectives, body(): lax.all_to_all(parcel.reshape(space_count, 2, 3 * DEPTH), 'space', 0, 0,...  39.3 us
    all_to_all x1, blocking collectives, body(): lax.all_to_all(payload.reshape(space_count, 2, 3 * readings), 'space', 0,...  39.2 us
    ppermute x4, starting transfers between devices, shifted(): return lax.ppermute(value, ('space', 'lead'), pairs)  13.5 us
    pallas_call x5, Pallas kernels, call(): pl.pallas_call(kernel, out_shape=[jax.ShapeDtypeStruct(shape, dtype) for...  7.84 us
    ppermute x4, waiting for transfers between devices, shifted(): return lax.ppermute(value, ('space', 'lead'), pairs)  6.44 us
  transfers between devices with their start and end apart: 4, of which 3 were waited for; matrix products, arithmetic and copies ran while one was open for 0% of the time, Pallas kernels for 0%

profile of v8, /device:TPU:33, one launch (start us, length us, event | category | flops | bytes accessed | tf_op | source)
XLA Modules:
  0.0 110.2 jit_solution(6936779157656791932)
XLA Ops:
  0.7 0.8 broadcast_shift-right-arithmetic_fusion
  1.5 0.8 select_convert_fusion
  2.3 0.9 pad_maximum_fusion.records
  3.2 0.6 shard_map.140
  3.8 0.1 reshape.42
  3.8 0.0 copy-start
  3.8 0.0 copy-start.8
  3.9 39.2 %all_to_all.10 = bf16[128,2,384]{2,1,0:T(2,128)(2,1)S(1)} all-to-all(bf16[128,2,384]{2,1,0:T(2,128)(2,1)S(1)} %reshape.42), channel_id=1, replica_groups=mesh['space'=128,'lead'=4] {'space'}, dimensions={0} | all-to-all | bytes 393216 | tf_op jit(solution)/shard_map/all_to_all | solution.py:410
  43.1 0.1 reshape.43.arrived
  43.2 0.6 shard_map.141
  43.8 4.9 %collective-permute-start = (bf16[168,256]{1,0:T(8,128)(2,1)S(1)}, bf16[168,256]{1,0:T(8,128)(2,1)S(1)}, u32[]{:S(2)}, u32[]{:S(2)}) collective-permute-start(bf16[168,256]{1,0:T(8,128)(2,1)S(1)} %get-tuple-element.16), channel_id=1, source_target_pairs={{1,32},{2,33},{3,34},{0,35},{6,36},{7,37},{4,38},{5,39},{9,40},{10... | collective-permute-start | bytes 258056 | tf_op jit(solution)/shard_map/ppermute | solution.py:384
  48.7 3.4 %collective-permute-start.1 = (bf16[168,256]{1,0:T(8,128)(2,1)S(1)}, bf16[168,256]{1,0:T(8,128)(2,1)S(1)}, u32[]{:S(2)}, u32[]{:S(2)}) collective-permute-start(bf16[168,256]{1,0:T(8,128)(2,1)S(1)} %get-tuple-element.17), channel_id=1, source_target_pairs={{33,0},{34,1},{35,2},{32,3},{37,4},{38,5},{39,6},{36,7},{41,8},{42... | collective-permute-start | bytes 258056 | tf_op jit(solution)/shard_map/ppermute | solution.py:384
  52.1 2.0 %collective-permute-done.1.south = bf16[168,256]{1,0:T(8,128)(2,1)S(1)} collective-permute-done((bf16[168,256]{1,0:T(8,128)(2,1)S(1)}, bf16[168,256]{1,0:T(8,128)(2,1)S(1)}, u32[]{:S(2)}, u32[]{:S(2)}) %collective-permute-start.1) | collective-permute-done | bytes 86048 | tf_op jit(solution)/shard_map/ppermute | solution.py:384
  54.2 5.1 %collective-permute-start.2 = (bf16[26,8,256]{2,1,0:T(8,128)(2,1)S(1)}, bf16[26,8,256]{2,1,0:T(8,128)(2,1)S(1)}, u32[]{:S(2)}, u32[]{:S(2)}) collective-permute-start(bf16[26,8,256]{2,1,0:T(8,128)(2,1)S(1)} %get-tuple-element.20), channel_id=1, source_target_pairs={{30,0},{31,1},{28,2},{29,3},{2,4},{3,5},{0,6},{1,7},{6,8},{7,9},{4... | collective-permute-start | bytes 319496 | tf_op jit(solution)/shard_map/ppermute | solution.py:384
  59.3 0.0 collective-permute-start.3
  59.4 1.7 %collective-permute-done.2.west = bf16[26,8,256]{2,1,0:T(8,128)(2,1)S(1)} collective-permute-done((bf16[26,8,256]{2,1,0:T(8,128)(2,1)S(1)}, bf16[26,8,256]{2,1,0:T(8,128)(2,1)S(1)}, u32[]{:S(2)}, u32[]{:S(2)}) %collective-permute-start.2) | collective-permute-done | bytes 106528 | tf_op jit(solution)/shard_map/ppermute | solution.py:384
  61.0 2.7 %collective-permute-done.3.east = bf16[26,8,256]{2,1,0:T(8,128)(2,1)S(1)} collective-permute-done((bf16[26,8,256]{2,1,0:T(8,128)(2,1)S(1)}, bf16[26,8,256]{2,1,0:T(8,128)(2,1)S(1)}, u32[]{:S(2)}, u32[]{:S(2)}) %collective-permute-start.3) | collective-permute-done | bytes 106528 | tf_op jit(solution)/shard_map/ppermute | solution.py:384
  63.8 3.5 %shard_map.143 = (f32[512,256]{1,0:T(8,128)S(1)}, bf16[256,768]{1,0:T(8,128)(2,1)S(1)}, f32[8,256]{1,0:T(8,128)S(1)}) custom-call(bf16[168,256]{1,0:T(8,128)(2,1)S(1)} %collective-permute-done.north, bf16[168,256]{1,0:T(8,128)(2,1)S(1)} %collective-permute-done.1.south, bf16[26,8,256]{2,1,0:T(8,128)(2,1)S(1)} %collective-permute-done.2.west, ...), custom_call_target="tpu_custom_call" | custom-call | tf_op jit(solution)/shard_map/pallas_call | solution.py:293
  67.3 0.0 copy-start.5
  67.3 0.0 copy-start.6
  67.3 0.1 reshape.47
  67.5 39.3 %all_to_all.11 = bf16[128,2,768]{2,1,0:T(2,128)(2,1)S(1)} all-to-all(bf16[128,2,768]{2,1,0:T(2,128)(2,1)S(1)} %reshape.47), channel_id=1, replica_groups=mesh['space'=128,'lead'=4] {'space'}, dimensions={0} | all-to-all | bytes 786432 | tf_op jit(solution)/shard_map/all_to_all | solution.py:436
  106.8 0.1 reshape.48.returned
  107.0 3.2 %shard_map.144 = (bf16[512,256]{1,0:T(8,128)(2,1)}, bf16[256,256]{1,0:T(8,128)(2,1)}) custom-call(bf16[256,768]{1,0:T(8,128)(2,1)S(1)} %reshape.48.returned, bf16[3,768,256]{2,1,0:T(8,128)(2,1)S(1)} %bitcast.10, bf16[4,256]{1,0:T(4,128)(2,1)S(1)} %copy-done.8, f32[512,256]{1,0:T(8,128)S(1)} %get-tuple-element.23.partial, ...), custom_call_target="tpu_custom_call" | custom-call | tf_op jit(solution)/shard_map/pallas_call | solution.py:293
  (20 shorter events, 0.1 us)
Async XLA Ops:
  0.6 42.5 %copy-start.9 = (s32[4]{0:T(128)S(1)}, s32[4]{0:T(128)}, u32[]{:S(2)}) copy-start(s32[4]{0:T(128)} %param.23) | copy-start | bytes 52
  0.6 42.5 %copy-start.4 = (bf16[180,512]{1,0:T(8,128)(2,1)S(1)}, bf16[180,512]{1,0:T(8,128)(2,1)}, u32[]{:S(2)}) copy-start(bf16[180,512]{1,0:T(8,128)(2,1)} %film_table.1) | copy-start | bytes 552964
  0.7 42.5 %copy-start.7 = (bf16[128,256]{1,0:T(8,128)(2,1)S(1)}, bf16[128,256]{1,0:T(8,128)(2,1)}, u32[]{:S(2)}) copy-start(bf16[128,256]{1,0:T(8,128)(2,1)} %embed.1) | copy-start | bytes 196612
  0.7 42.5 %copy-start.3 = (bf16[1,16,32,256]{3,2,1,0:T(8,128)(2,1)S(1)}, bf16[1,16,32,256]{3,2,1,0:T(8,128)(2,1)}, u32[]{:S(2)}) copy-start(bf16[1,16,32,256]{3,2,1,0:T(8,128)(2,1)} %param.13) | copy-start | bytes 786436
  3.7 60.0 %copy-start.1 = (bf16[3,3,256,256]{3,2,1,0:T(8,128)(2,1)S(1)}, bf16[3,3,256,256]{3,2,1,0:T(8,128)(2,1)}, u32[]{:S(2)}) copy-start(bf16[3,3,256,256]{3,2,1,0:T(8,128)(2,1)} %param.19) | copy-start | bytes 3538948
  3.8 59.9 %copy-start = (bf16[3,3,256,256]{3,2,1,0:T(8,128)(2,1)S(1)}, bf16[3,3,256,256]{3,2,1,0:T(8,128)(2,1)}, u32[]{:S(2)}) copy-start(bf16[3,3,256,256]{3,2,1,0:T(8,128)(2,1)} %param.18) | copy-start | bytes 3538948
  3.8 59.9 %copy-start.8 = (bf16[4,256]{1,0:T(4,128)(2,1)S(1)}, bf16[4,256]{1,0:T(4,128)(2,1)}, u32[]{:S(2)}) copy-start(bf16[4,256]{1,0:T(4,128)(2,1)} %gains.3) | copy-start | bytes 6148
  43.8 8.4 %collective-permute-start = (bf16[168,256]{1,0:T(8,128)(2,1)S(1)}, bf16[168,256]{1,0:T(8,128)(2,1)S(1)}, u32[]{:S(2)}, u32[]{:S(2)}) collective-permute-start(bf16[168,256]{1,0:T(8,128)(2,1)S(1)} %get-tuple-element.16), channel_id=1, source_target_pairs={{1,32},{2,33},{3,34},{0,35},{6,36},{7,37},{4,38},{5,39},{9,40},{10... | collective-permute-start | bytes 258056 | tf_op jit(solution)/shard_map/ppermute | solution.py:384
  48.7 5.5 %collective-permute-start.1 = (bf16[168,256]{1,0:T(8,128)(2,1)S(1)}, bf16[168,256]{1,0:T(8,128)(2,1)S(1)}, u32[]{:S(2)}, u32[]{:S(2)}) collective-permute-start(bf16[168,256]{1,0:T(8,128)(2,1)S(1)} %get-tuple-element.17), channel_id=1, source_target_pairs={{33,0},{34,1},{35,2},{32,3},{37,4},{38,5},{39,6},{36,7},{41,8},{42... | collective-permute-start | bytes 258056 | tf_op jit(solution)/shard_map/ppermute | solution.py:384
  54.2 6.8 %collective-permute-start.2 = (bf16[26,8,256]{2,1,0:T(8,128)(2,1)S(1)}, bf16[26,8,256]{2,1,0:T(8,128)(2,1)S(1)}, u32[]{:S(2)}, u32[]{:S(2)}) collective-permute-start(bf16[26,8,256]{2,1,0:T(8,128)(2,1)S(1)} %get-tuple-element.20), channel_id=1, source_target_pairs={{30,0},{31,1},{28,2},{29,3},{2,4},{3,5},{0,6},{1,7},{6,8},{7,9},{4... | collective-permute-start | bytes 319496 | tf_op jit(solution)/shard_map/ppermute | solution.py:384
  59.3 4.4 %collective-permute-start.3 = (bf16[26,8,256]{2,1,0:T(8,128)(2,1)S(1)}, bf16[26,8,256]{2,1,0:T(8,128)(2,1)S(1)}, u32[]{:S(2)}, u32[]{:S(2)}) collective-permute-start(bf16[26,8,256]{2,1,0:T(8,128)(2,1)S(1)} %get-tuple-element.21), channel_id=1, source_target_pairs={{4,0},{5,1},{6,2},{7,3},{8,4},{9,5},{10,6},{11,7},{12,8},{13,9},{1... | collective-permute-start | bytes 319496 | tf_op jit(solution)/shard_map/ppermute | solution.py:384
  67.3 39.7 %copy-start.2 = (bf16[3,3,256,256]{3,2,1,0:T(8,128)(2,1)S(1)}, bf16[3,3,256,256]{3,2,1,0:T(8,128)(2,1)}, u32[]{:S(2)}) copy-start(bf16[3,3,256,256]{3,2,1,0:T(8,128)(2,1)} %param.20) | copy-start | bytes 3538948
  67.3 39.7 %copy-start.5 = (bf16[256,256]{1,0:T(8,128)(2,1)S(1)}, bf16[256,256]{1,0:T(8,128)(2,1)}, u32[]{:S(2)}) copy-start(bf16[256,256]{1,0:T(8,128)(2,1)} %out_proj.1) | copy-start | bytes 393220
  67.3 39.7 %copy-start.6 = (bf16[256,256]{1,0:T(8,128)(2,1)S(1)}, bf16[256,256]{1,0:T(8,128)(2,1)}, u32[]{:S(2)}) copy-start(bf16[256,256]{1,0:T(8,128)(2,1)} %projector.1) | copy-start | bytes 393220

commit v9 on v7

--- a/solution.py
+++ b/solution.py
@@ -11,6 +11,7 @@
 TILE_H, TILE_W, DEPTH = 16, 32, 256
 CELLS = TILE_H * TILE_W
 EPS = 1e-06
+FILM_ROWS = 256
 HALO = 5
 SIDE = 8
 FRAME_H, FRAME_W = TILE_H + 2 * HALO, TILE_W + 2 * SIDE
@@ -86,8 +87,7 @@
 
 
 def inject_kernel(
-    steps, arrived, embed, tiles, film_table,
-    own, first_rows, last_rows, film,
+    arrived, embed, tiles, own, first_rows, last_rows
 ):
     pairs = arrived.shape[0]
     readings = embed.shape[0]
@@ -103,30 +103,24 @@
         fine += dot(hot, embedded.astype(BF16))
     fine = (fine + tiles[...].astype(F32)).reshape(TILE_H, TILE_W, DEPTH)
     own[...] = fine
+    first_rows[...] = fine[:HALO].reshape(HALO * TILE_W, DEPTH).astype(BF16)
+    last_rows[...] = fine[-HALO:].reshape(HALO * TILE_W, DEPTH).astype(BF16)
+
+
+def film_kernel(steps, film_table, out):
     table_rows = film_table.shape[0]
     offset = lax.axis_index("lead") * table_rows
     sort = line((8, table_rows))
     at = jnp.full((8, table_rows), -1, jnp.int32)
     for i in range(4):
         at = jnp.where((sort & 3) == i, steps[0:1, i : i + 1] - offset, at)
-    hot = ones_where(column((8, table_rows)) == at)
-    both = dot(hot, film_table[...])
+    both = dot(ones_where(column((8, table_rows)) == at), film_table[...])
     rows = jnp.where(line((8, DEPTH)) < 4, both[:, :DEPTH], both[:, DEPTH:])
-    film[...] = rows
-    for target, start in ((first_rows, 0), (last_rows, TILE_H - HALO)):
-        edge = fine[start : start + HALO].reshape(HALO * TILE_W, DEPTH)
-        target[...] = jnp.concatenate([edge, rows], axis=0).astype(BF16)
-
-
-def brought_film(north, south, col_at):
-    above, below = (rows[HALO * TILE_W :].astype(F32) for rows in (north, south))
-    return above + jnp.where(lax.rem(col_at, 2) == 0, below, 0.0)
-
-
-def widen_kernel(image_rows, north, south, own, first_cols, last_cols):
-    row_at, col_at = grid_place()
-    film = brought_film(north, south, col_at)
-    at = line((SIDE, DEPTH))
+    out[...] = jnp.zeros(out.shape, BF16)
+    out[:16] = jnp.concatenate([rows, jnp.zeros((8, DEPTH), F32)], axis=0).astype(BF16)
+
+
+def widen_kernel(north, south, own, first_cols, last_cols):
     for y in range(FRAME_H):
         for target, cols in (
             (first_cols, slice(0, SIDE)),
@@ -135,39 +129,29 @@
             start = y % (HALO + TILE_H) * TILE_W + cols.start
             if y < HALO:
                 rows = north[start : start + SIDE].astype(F32)
-                rows = jnp.where(row_at > 0, rows, 0.0)
             elif y < HALO + TILE_H:
                 rows = own[y - HALO, cols]
             else:
                 rows = south[start : start + SIDE].astype(F32)
-                rows = jnp.where(row_at < image_rows - 1, rows, 0.0)
-            if y < 8 and target is last_cols:
-                rows = jnp.where(at == 0, film[y : y + 1], rows)
             target[y] = rows.astype(BF16)
 
 
 def trunk_kernel(
     image_rows,
-    north, south, west, east, own, film, conv_fine, conv_mid, gains, arrived,
-    partial_ref, parcel, film_ref,
+    north, south, west, east, own, conv_fine, conv_mid, gains, arrived,
+    partial_ref, parcel,
     frame, taps, enc, mid_in, mid_taps,
 ):
     row_at, col_at = grid_place()
-    left = west[...].astype(F32)
-    at = line((8, DEPTH))
-    rows = film[...] + brought_film(north, south, col_at)
-    for y in range(8):
-        rows += jnp.where(at == y, left[y, 0:1], 0.0)
-    film_ref[...] = rows
     above, below = (
         rows[: HALO * TILE_W].astype(F32).reshape(HALO, TILE_W, DEPTH) for rows in (north, south)
     )
     inner = slice(SIDE, SIDE + TILE_W)
-    frame[:HALO, inner] = jnp.where(row_at > 0, above, 0.0)
+    frame[:HALO, inner] = above
     frame[HALO : HALO + TILE_H, inner] = own[...]
-    frame[HALO + TILE_H :, inner] = jnp.where(row_at < image_rows - 1, below, 0.0)
-    frame[:, :SIDE] = jnp.where(col_at > 0, left, 0.0)
-    frame[:, SIDE + TILE_W :] = jnp.where(col_at < TILE_COLS - 1, east[...].astype(F32), 0.0)
+    frame[HALO + TILE_H :, inner] = below
+    frame[:, :SIDE] = west[...].astype(F32)
+    frame[:, SIDE + TILE_W :] = east[...].astype(F32)
     gain = gains[0:1].astype(F32)
     for y in range(FRAME_H):
         normed = rms_scale(frame[y], gain)
@@ -254,9 +238,10 @@
     low = (context - high.astype(F32)).astype(BF16)
 
     gain = gains[3:4].astype(F32)
-    lead, at = lax.axis_index("lead"), line((8, DEPTH))
-    scale = 1.0 + jnp.sum(jnp.where(at == lead, film[...], 0.0), axis=0, keepdims=True)
-    shift = jnp.sum(jnp.where(at == lead + 4, film[...], 0.0), axis=0, keepdims=True)
+    lead, at = lax.axis_index("lead"), line((16, DEPTH))
+    rows = film[:16].astype(F32)
+    scale = 1.0 + jnp.sum(jnp.where(at == lead, rows, 0.0), axis=0, keepdims=True)
+    shift = jnp.sum(jnp.where(at == lead + 4, rows, 0.0), axis=0, keepdims=True)
 
     def decode(values):
         hidden = rms_scale(values, gain) * scale + shift
@@ -307,35 +292,33 @@
     return call(pack_kernel, outs, [], [records], megabytes=8)
 
 
-def inject(steps, arrived, embed, tiles, film_table):
+def film_rows(steps, film_table):
+    return call(film_kernel, [((FILM_ROWS, DEPTH), BF16)], [], [steps, film_table])[0]
+
+
+def inject(arrived, embed, tiles):
     return call(
         inject_kernel,
         [
             ((TILE_H, TILE_W, DEPTH), F32),
-            ((HALO * TILE_W + 8, DEPTH), BF16),
-            ((HALO * TILE_W + 8, DEPTH), BF16),
-            ((8, DEPTH), F32),
+            ((HALO * TILE_W, DEPTH), BF16),
+            ((HALO * TILE_W, DEPTH), BF16),
         ],
         [],
-        [steps, arrived, embed, tiles, film_table],
+        [arrived, embed, tiles],
         megabytes=8,
     )
 
 
-def widen(image_rows, north, south, own):
+def widen(north, south, own):
     shape = (FRAME_H, SIDE, DEPTH)
-    return call(
-        functools.partial(widen_kernel, image_rows),
-        [(shape, BF16), (shape, BF16)],
-        [],
-        [north, south, own],
-    )
-
-
-def trunk(image_rows, north, south, west, east, own, film, conv_fine, conv_mid, gains, arrived):
+    return call(widen_kernel, [(shape, BF16), (shape, BF16)], [], [north, south, own])
+
+
+def trunk(image_rows, north, south, west, east, own, conv_fine, conv_mid, gains, arrived):
     return call(
         functools.partial(trunk_kernel, image_rows),
-        [((CELLS, DEPTH), F32), ((arrived.shape[0], 3 * DEPTH), BF16), ((8, DEPTH), F32)],
+        [((CELLS, DEPTH), F32), ((arrived.shape[0], 3 * DEPTH), BF16)],
         [
             pltpu.VMEM((FRAME_H, FRAME_W, DEPTH), F32),
             pltpu.VMEM((FRAME_H * FRAME_W, 3 * DEPTH), BF16),
@@ -344,7 +327,7 @@
             pltpu.VMEM((ENC_H // 4 * MID_W, 3 * DEPTH), BF16),
         ],
         [
-            north, south, west, east, own, film,
+            north, south, west, east, own,
             conv_fine.reshape(3, 3 * DEPTH, DEPTH),
             conv_mid.reshape(3, 3 * DEPTH, DEPTH),
             gains, arrived,
@@ -373,16 +356,14 @@
     )
 
 
-def shifted(value, row_step, col_step, lead_steps=(0, 0)):
-    rows, leads = lax.axis_size("space") // TILE_COLS, lax.axis_size("lead")
+def shifted(value, row_step, col_step):
+    count = lax.axis_size("space")
     pairs = []
-    for row in range(rows):
-        for col in range(TILE_COLS):
-            for lead in range(leads):
-                source = (row * TILE_COLS + col) * leads + lead
-                there = (row + row_step) % rows * TILE_COLS + (col + col_step) % TILE_COLS
-                pairs.append((source, there * leads + (lead - lead_steps[col % 2]) % leads))
-    return lax.ppermute(value, ("space", "lead"), pairs)
+    for source in range(count):
+        row, col = source // TILE_COLS + row_step, source % TILE_COLS + col_step
+        if 0 <= row < count // TILE_COLS and 0 <= col < TILE_COLS:
+            pairs.append((source, row * TILE_COLS + col))
+    return lax.ppermute(value, "space", pairs)
 
 
 def body(
@@ -411,20 +392,19 @@
     arrived = lax.all_to_all(
         payload.reshape(space_count, 2, 3 * readings), "space", 0, 0, tiled=True
     ).reshape(2 * space_count, 3 * readings)
-    own, first_rows, last_rows, film = inject(
-        horizon_step_list.reshape(1, -1), arrived, station_embed, tiles.reshape(CELLS, DEPTH), film_table
-    )
-
-    image_rows = space_count // TILE_COLS
-    north = shifted(last_rows, 1, 0, (1, 2))
-    south = shifted(first_rows, -1, 0, (-1, 0))
-    first_cols, last_cols = widen(image_rows, north, south, own)
+    own, first_rows, last_rows = inject(arrived, station_embed, tiles.reshape(CELLS, DEPTH))
+
+    north = shifted(last_rows, 1, 0)
+    south = shifted(first_rows, -1, 0)
+    steps, last_rows = lax.optimization_barrier((horizon_step_list.reshape(1, -1), last_rows))
+    film = lax.psum(film_rows(steps, film_table), "lead")
+    first_cols, last_cols = widen(north, south, own)
     west = shifted(last_cols, 0, 1)
     east = shifted(first_cols, 0, -1)
 
-    partial, parcel, film = trunk(
-        image_rows,
-        north, south, west, east, own, film, conv_fine, conv_mid, norm_gains, arrived,
+    partial, parcel = trunk(
+        space_count // TILE_COLS,
+        north, south, west, east, own, conv_fine, conv_mid, norm_gains, arrived,
     )
     returned = lax.all_to_all(
         parcel.reshape(space_count, 2, 3 * DEPTH), "space", 0, 0, tiled=True

time: 109 us -> 154 us (1.41)
  the two profiles are of different devices: /device:TPU:33 before, /device:TPU:8 now
where the time goes in v9:
time: 154 us
  waiting for transfers between devices  67.5 us (44%)
  blocking collectives  38.2 us (25%)
  starting transfers between devices  20.6 us (13%)
  between operations  14.2 us (9%)
  Pallas kernels  8.63 us (6%)
  other arithmetic  2.44 us (2%)
  local copies, waits for them, and re-layouts  2.15 us (1%)
    all_to_all x1, blocking collectives, body(): lax.all_to_all(payload.reshape(space_count, 2, 3 * readings), 'space', 0,...  38.2 us
    psum x1, waiting for transfers between devices, body(): film = lax.psum(film_rows(steps, film_table), 'lead')  34.8 us
    all_to_all x1, waiting for transfers between devices, body(): lax.all_to_all(parcel.reshape(space_count, 2, 3 * DEPTH), 'space', 0, 0,...  25.3 us
    ppermute x4, starting transfers between devices, shifted(): return lax.ppermute(value, 'space', pairs)  10.3 us
    all_to_all x1, starting transfers between devices, body(): lax.all_to_all(parcel.reshape(space_count, 2, 3 * DEPTH), 'space', 0, 0,...  10.2 us
    pallas_call x6, Pallas kernels, call(): pl.pallas_call(kernel, out_shape=[jax.ShapeDtypeStruct(shape, dtype) for...  8.63 us
    ppermute x4, waiting for transfers between devices, shifted(): return lax.ppermute(value, 'space', pairs)  7.3 us
  transfers between devices with their start and end apart: 6, of which 6 were waited for; matrix products, arithmetic and copies ran while one was open for 0% of the time, Pallas kernels for 1%

profile of v9, /device:TPU:8, one launch (start us, length us, event | category | flops | bytes accessed | tf_op | source)
XLA Modules:
  0.0 153.8 jit_solution(14960301806955325268)
XLA Ops:
  7.2 0.7 broadcast_shift-right-arithmetic_fusion
  7.9 0.8 select_convert_fusion
  8.8 0.9 pad_maximum_fusion.records
  9.6 0.6 shard_map.140
  10.3 0.1 reshape.41
  10.3 38.2 %all_to_all.10 = bf16[128,2,384]{2,1,0:T(2,128)(2,1)S(1)} all-to-all(bf16[128,2,384]{2,1,0:T(2,128)(2,1)S(1)} %reshape.41), channel_id=1, replica_groups=mesh['space'=128,'lead'=4] {'space'}, dimensions={0} | all-to-all | bytes 393216 | tf_op jit(solution)/shard_map/all_to_all | solution.py:392
  48.7 0.5 shard_map.141
  49.2 3.5 %collective-permute-start = (bf16[160,256]{1,0:T(8,128)(2,1)S(1)}, bf16[160,256]{1,0:T(8,128)(2,1)S(1)}, u32[]{:S(2)}, u32[]{:S(2)}) collective-permute-start(bf16[160,256]{1,0:T(8,128)(2,1)S(1)} %get-tuple-element.15), channel_id=1, source_target_pairs={{0,32},{4,36},{8,40},{12,44},{16,48},{20,52},{24,56},{28,60},{32,6... | collective-permute-start | bytes 245768 | tf_op jit(solution)/shard_map/ppermute | solution.py:366
  52.7 1.3 collective-permute-start.1
  54.0 0.7 collective-permute-done.north
  54.7 4.3 %collective-permute-done.1.south = bf16[160,256]{1,0:T(8,128)(2,1)S(1)} collective-permute-done((bf16[160,256]{1,0:T(8,128)(2,1)S(1)}, bf16[160,256]{1,0:T(8,128)(2,1)S(1)}, u32[]{:S(2)}, u32[]{:S(2)}) %collective-permute-start.1) | collective-permute-done | bytes 81952 | tf_op jit(solution)/shard_map/ppermute | solution.py:366
  59.0 1.9 %collective-permute-start.2 = (bf16[26,8,256]{2,1,0:T(8,128)(2,1)S(1)}, bf16[26,8,256]{2,1,0:T(8,128)(2,1)S(1)}, u32[]{:S(2)}, u32[]{:S(2)}) collective-permute-start(bf16[26,8,256]{2,1,0:T(8,128)(2,1)S(1)} %get-tuple-element.18), channel_id=1, source_target_pairs={{0,4},{4,8},{8,12},{12,16},{16,20},{20,24},{24,28},{32,36},{36,40}... | collective-permute-start | bytes 319496 | tf_op jit(solution)/shard_map/ppermute | solution.py:366
  60.9 3.6 %collective-permute-start.3 = (bf16[26,8,256]{2,1,0:T(8,128)(2,1)S(1)}, bf16[26,8,256]{2,1,0:T(8,128)(2,1)S(1)}, u32[]{:S(2)}, u32[]{:S(2)}) collective-permute-start(bf16[26,8,256]{2,1,0:T(8,128)(2,1)S(1)} %get-tuple-element.19), channel_id=1, source_target_pairs={{4,0},{8,4},{12,8},{16,12},{20,16},{24,20},{28,24},{36,32},{40,36}... | collective-permute-start | bytes 319496 | tf_op jit(solution)/shard_map/ppermute | solution.py:366
  64.6 0.4 collective-permute-done.2.west
  65.0 1.8 %collective-permute-done.3.east = bf16[26,8,256]{2,1,0:T(8,128)(2,1)S(1)} collective-permute-done((bf16[26,8,256]{2,1,0:T(8,128)(2,1)S(1)}, bf16[26,8,256]{2,1,0:T(8,128)(2,1)S(1)}, u32[]{:S(2)}, u32[]{:S(2)}) %collective-permute-start.3) | collective-permute-done | bytes 106528 | tf_op jit(solution)/shard_map/ppermute | solution.py:366
  66.9 3.5 %shard_map.143 = (f32[512,256]{1,0:T(8,128)S(1)}, bf16[256,768]{1,0:T(8,128)(2,1)S(1)}) custom-call(bf16[160,256]{1,0:T(8,128)(2,1)S(1)} %collective-permute-done.north, bf16[160,256]{1,0:T(8,128)(2,1)S(1)} %collective-permute-done.1.south, bf16[26,8,256]{2,1,0:T(8,128)(2,1)S(1)} %collective-permute-done.2.west, ...), custom_call_target="tpu_custom_call" | custom-call | tf_op jit(solution)/shard_map/pallas_call | solution.py:279
  70.4 0.9 reshape.46
  71.3 10.2 %all-to-all-start.1 = ((bf16[128,2,768]{2,1,0:T(2,128)(2,1)}), bf16[128,2,768]{2,1,0:T(2,128)(2,1)S(1)}, u32[]{:S(2)}, u32[]{:S(2)}) async-start(bf16[128,2,768]{2,1,0:T(2,128)(2,1)} %reshape.46), calls=%async_computation.1 | async-start | bytes 786432 | tf_op jit(solution)/shard_map/all_to_all | solution.py:409
  81.6 0.9 shard_map.144
  82.5 25.3 %all-to-all-done.1 = bf16[128,2,768]{2,1,0:T(2,128)(2,1)S(1)} async-done(((bf16[128,2,768]{2,1,0:T(2,128)(2,1)}), bf16[128,2,768]{2,1,0:T(2,128)(2,1)S(1)}, u32[]{:S(2)}, u32[]{:S(2)}) %all-to-all-start.1) | async-done | bytes 393248 | tf_op jit(solution)/shard_map/all_to_all | solution.py:409
  107.8 0.1 reshape.47.returned
  108.0 34.8 %all-reduce.2.cloned.1.call-done.film = bf16[256,256]{1,0:T(8,128)(2,1)} async-done(((bf16[256,256]{1,0:T(8,128)(2,1)}), bf16[256,256]{1,0:T(8,128)(2,1)}) %all-reduce.2.cloned.1.call-update) | async-done | bytes 131088 | tf_op jit(solution)/shard_map/psum | solution.py:400
  142.8 0.9 copy-done.7
  143.7 3.2 %shard_map.145 = (bf16[512,256]{1,0:T(8,128)(2,1)}, bf16[256,256]{1,0:T(8,128)(2,1)}) custom-call(bf16[256,768]{1,0:T(8,128)(2,1)S(1)} %reshape.47.returned, bf16[3,768,256]{2,1,0:T(8,128)(2,1)S(1)} %bitcast.10, bf16[4,256]{1,0:T(4,128)(2,1)S(1)} %copy-done.9, f32[512,256]{1,0:T(8,128)S(1)} %get-tuple-element.21.partial, bf16[256,256]{1,0:T(8,128)(2,1)S(1)} %copy-done.7, ...), custom_call_target="tpu_custom_call" | custom-call | tf_op jit(solution)/shard_map/pallas_call | solution.py:279
  (27 shorter events, 0.2 us)
Async XLA Ops:
  7.2 41.5 %copy-start.3 = (bf16[1,16,32,256]{3,2,1,0:T(8,128)(2,1)S(1)}, bf16[1,16,32,256]{3,2,1,0:T(8,128)(2,1)}, u32[]{:S(2)}) copy-start(bf16[1,16,32,256]{3,2,1,0:T(8,128)(2,1)} %param.13) | copy-start | bytes 786436
  7.2 41.5 %copy-start.8 = (bf16[128,256]{1,0:T(8,128)(2,1)S(1)}, bf16[128,256]{1,0:T(8,128)(2,1)}, u32[]{:S(2)}) copy-start(bf16[128,256]{1,0:T(8,128)(2,1)} %embed.1) | copy-start | bytes 196612
  10.2 56.6 %copy-start = (bf16[3,3,256,256]{3,2,1,0:T(8,128)(2,1)S(1)}, bf16[3,3,256,256]{3,2,1,0:T(8,128)(2,1)}, u32[]{:S(2)}) copy-start(bf16[3,3,256,256]{3,2,1,0:T(8,128)(2,1)} %param.18) | copy-start | bytes 3538948
  10.2 56.6 %copy-start.1 = (bf16[3,3,256,256]{3,2,1,0:T(8,128)(2,1)S(1)}, bf16[3,3,256,256]{3,2,1,0:T(8,128)(2,1)}, u32[]{:S(2)}) copy-start(bf16[3,3,256,256]{3,2,1,0:T(8,128)(2,1)} %param.19) | copy-start | bytes 3538948
  10.2 56.6 %copy-start.9 = (bf16[4,256]{1,0:T(4,128)(2,1)S(1)}, bf16[4,256]{1,0:T(4,128)(2,1)}, u32[]{:S(2)}) copy-start(bf16[4,256]{1,0:T(4,128)(2,1)} %gains.3) | copy-start | bytes 6148
  49.2 5.5 %collective-permute-start = (bf16[160,256]{1,0:T(8,128)(2,1)S(1)}, bf16[160,256]{1,0:T(8,128)(2,1)S(1)}, u32[]{:S(2)}, u32[]{:S(2)}) collective-permute-start(bf16[160,256]{1,0:T(8,128)(2,1)S(1)} %get-tuple-element.15), channel_id=1, source_target_pairs={{0,32},{4,36},{8,40},{12,44},{16,48},{20,52},{24,56},{28,60},{32,6... | collective-permute-start | bytes 245768 | tf_op jit(solution)/shard_map/ppermute | solution.py:366
  52.7 6.3 %collective-permute-start.1 = (bf16[160,256]{1,0:T(8,128)(2,1)S(1)}, bf16[160,256]{1,0:T(8,128)(2,1)S(1)}, u32[]{:S(2)}, u32[]{:S(2)}) collective-permute-start(bf16[160,256]{1,0:T(8,128)(2,1)S(1)} %get-tuple-element.16), channel_id=1, source_target_pairs={{32,0},{36,4},{40,8},{44,12},{48,16},{52,20},{56,24},{60,28},{64,3... | collective-permute-start | bytes 245768 | tf_op jit(solution)/shard_map/ppermute | solution.py:366
  59.0 6.0 %collective-permute-start.2 = (bf16[26,8,256]{2,1,0:T(8,128)(2,1)S(1)}, bf16[26,8,256]{2,1,0:T(8,128)(2,1)S(1)}, u32[]{:S(2)}, u32[]{:S(2)}) collective-permute-start(bf16[26,8,256]{2,1,0:T(8,128)(2,1)S(1)} %get-tuple-element.18), channel_id=1, source_target_pairs={{0,4},{4,8},{8,12},{12,16},{16,20},{20,24},{24,28},{32,36},{36,40}... | collective-permute-start | bytes 319496 | tf_op jit(solution)/shard_map/ppermute | solution.py:366
  60.9 5.9 %collective-permute-start.3 = (bf16[26,8,256]{2,1,0:T(8,128)(2,1)S(1)}, bf16[26,8,256]{2,1,0:T(8,128)(2,1)S(1)}, u32[]{:S(2)}, u32[]{:S(2)}) collective-permute-start(bf16[26,8,256]{2,1,0:T(8,128)(2,1)S(1)} %get-tuple-element.19), channel_id=1, source_target_pairs={{4,0},{8,4},{12,8},{16,12},{20,16},{24,20},{28,24},{36,32},{40,36}... | collective-permute-start | bytes 319496 | tf_op jit(solution)/shard_map/ppermute | solution.py:366
  70.4 11.2 %copy-start.4 = (bf16[180,512]{1,0:T(8,128)(2,1)S(1)}, bf16[180,512]{1,0:T(8,128)(2,1)}, u32[]{:S(2)}) copy-start(bf16[180,512]{1,0:T(8,128)(2,1)} %film_table.1) | copy-start | bytes 552964
  70.4 11.2 %copy-start.10 = (s32[4]{0:T(128)S(1)}, s32[4]{0:T(128)}, u32[]{:S(2)}) copy-start(s32[4]{0:T(128)} %param.23) | copy-start | bytes 52
  71.3 71.5 %copy-start.2 = (bf16[3,3,256,256]{3,2,1,0:T(8,128)(2,1)S(1)}, bf16[3,3,256,256]{3,2,1,0:T(8,128)(2,1)}, u32[]{:S(2)}) copy-start(bf16[3,3,256,256]{3,2,1,0:T(8,128)(2,1)} %param.20) | copy-start | bytes 3538948
  71.3 71.5 %copy-start.5 = (bf16[256,256]{1,0:T(8,128)(2,1)S(1)}, bf16[256,256]{1,0:T(8,128)(2,1)}, u32[]{:S(2)}) copy-start(bf16[256,256]{1,0:T(8,128)(2,1)} %out_proj.1) | copy-start | bytes 393220
  71.3 71.5 %copy-start.6 = (bf16[256,256]{1,0:T(8,128)(2,1)S(1)}, bf16[256,256]{1,0:T(8,128)(2,1)}, u32[]{:S(2)}) copy-start(bf16[256,256]{1,0:T(8,128)(2,1)} %projector.1) | copy-start | bytes 393220
  71.3 36.5 %all-to-all-start.1 = ((bf16[128,2,768]{2,1,0:T(2,128)(2,1)}), bf16[128,2,768]{2,1,0:T(2,128)(2,1)S(1)}, u32[]{:S(2)}, u32[]{:S(2)}) async-start(bf16[128,2,768]{2,1,0:T(2,128)(2,1)} %reshape.46), calls=%async_computation.1 | async-start | bytes 786432 | tf_op jit(solution)/shard_map/all_to_all | solution.py:409
  81.5 61.3 %all-reduce.2.cloned.1.call-start = ((), (), s32[]{:S(2)}) async-start(), calls=%async_computation.2 | async-start | bytes 262144 | tf_op jit(solution)/shard_map/psum | solution.py:400
  142.8 0.9 copy-start.7
Sparse Core Ops, SparseCore 0:
  85.2 57.4 all-reduce.1

commit v10 on v9

--- a/solution.py
+++ b/solution.py
@@ -11,7 +11,7 @@
 TILE_H, TILE_W, DEPTH = 16, 32, 256
 CELLS = TILE_H * TILE_W
 EPS = 1e-06
-FILM_ROWS = 256
+FILM_ROWS = 16
 HALO = 5
 SIDE = 8
 FRAME_H, FRAME_W = TILE_H + 2 * HALO, TILE_W + 2 * SIDE
@@ -116,8 +116,8 @@
         at = jnp.where((sort & 3) == i, steps[0:1, i : i + 1] - offset, at)
     both = dot(ones_where(column((8, table_rows)) == at), film_table[...])
     rows = jnp.where(line((8, DEPTH)) < 4, both[:, :DEPTH], both[:, DEPTH:])
-    out[...] = jnp.zeros(out.shape, BF16)
-    out[:16] = jnp.concatenate([rows, jnp.zeros((8, DEPTH), F32)], axis=0).astype(BF16)
+    rest = jnp.zeros((FILM_ROWS - 8, DEPTH), F32)
+    out[...] = jnp.concatenate([rows, rest], axis=0).astype(BF16)
 
 
 def widen_kernel(north, south, own, first_cols, last_cols):
@@ -238,8 +238,8 @@
     low = (context - high.astype(F32)).astype(BF16)
 
     gain = gains[3:4].astype(F32)
-    lead, at = lax.axis_index("lead"), line((16, DEPTH))
-    rows = film[:16].astype(F32)
+    lead, at = lax.axis_index("lead"), line((FILM_ROWS, DEPTH))
+    rows = film[...].astype(F32)
     scale = 1.0 + jnp.sum(jnp.where(at == lead, rows, 0.0), axis=0, keepdims=True)
     shift = jnp.sum(jnp.where(at == lead + 4, rows, 0.0), axis=0, keepdims=True)
 
@@ -396,8 +396,6 @@
 
     north = shifted(last_rows, 1, 0)
     south = shifted(first_rows, -1, 0)
-    steps, last_rows = lax.optimization_barrier((horizon_step_list.reshape(1, -1), last_rows))
-    film = lax.psum(film_rows(steps, film_table), "lead")
     first_cols, last_cols = widen(north, south, own)
     west = shifted(last_cols, 0, 1)
     east = shifted(first_cols, 0, -1)
@@ -406,6 +404,8 @@
         space_count // TILE_COLS,
         north, south, west, east, own, conv_fine, conv_mid, norm_gains, arrived,
     )
+    steps, parcel = lax.optimization_barrier((horizon_step_list.reshape(1, -1), parcel))
+    film = lax.psum(film_rows(steps, film_table), "lead")
     returned = lax.all_to_all(
         parcel.reshape(space_count, 2, 3 * DEPTH), "space", 0, 0, tiled=True
     ).reshape(2 * space_count, 3 * DEPTH)

time: 154 us -> 107 us (0.69)
  the two profiles are of different devices: /device:TPU:8 before, /device:TPU:33 now
where the time goes in v10:
time: 107 us; the launch traced here: 106 us
  blocking collectives  48.4 us (45%)
  waiting for transfers between devices  25.2 us (24%)
  starting transfers between devices  20.3 us (19%)
  Pallas kernels  7.97 us (7%)
  other arithmetic  2.45 us (2%)
  local copies, waits for them, and re-layouts  1.26 us (1%)
    all_to_all x1, blocking collectives, body(): lax.all_to_all(payload.reshape(space_count, 2, 3 * readings), 'space', 0,...  39.2 us
    all_to_all x1, waiting for transfers between devices, body(): lax.all_to_all(parcel.reshape(space_count, 2, 3 * DEPTH), 'space', 0, 0,...  18.8 us
    ppermute x4, starting transfers between devices, shifted(): return lax.ppermute(value, 'space', pairs)  10.7 us
    all_to_all x1, starting transfers between devices, body(): lax.all_to_all(parcel.reshape(space_count, 2, 3 * DEPTH), 'space', 0, 0,...  9.51 us
    psum x1, blocking collectives, body(): film = lax.psum(film_rows(steps, film_table), 'lead')  9.14 us
    pallas_call x6, Pallas kernels, call(): pl.pallas_call(kernel, out_shape=[jax.ShapeDtypeStruct(shape, dtype) for...  7.97 us
    ppermute x4, waiting for transfers between devices, shifted(): return lax.ppermute(value, 'space', pairs)  6.42 us
  transfers between devices with their start and end apart: 5, of which 4 were waited for; matrix products, arithmetic and copies ran while one was open for 0% of the time, Pallas kernels for 0%

profile of v10, /device:TPU:33, one launch (start us, length us, event | category | flops | bytes accessed | tf_op | source)
XLA Modules:
  0.0 106.4 jit_solution(887809861136114421)
XLA Ops:
  0.7 0.7 broadcast_shift-right-arithmetic_fusion
  1.4 0.8 select_convert_fusion
  2.3 0.9 pad_maximum_fusion.records
  3.1 0.6 shard_map.140
  3.7 0.0 copy-start
  3.7 0.1 reshape.42
  3.8 39.2 %all_to_all.10 = bf16[128,2,384]{2,1,0:T(2,128)(2,1)S(1)} all-to-all(bf16[128,2,384]{2,1,0:T(2,128)(2,1)S(1)} %reshape.42), channel_id=1, replica_groups=mesh['space'=128,'lead'=4] {'space'}, dimensions={0} | all-to-all | bytes 393216 | tf_op jit(solution)/shard_map/all_to_all | solution.py:392
  43.0 0.1 reshape.43.arrived
  43.1 0.5 shard_map.141
  43.7 2.4 %collective-permute-start = (bf16[160,256]{1,0:T(8,128)(2,1)S(1)}, bf16[160,256]{1,0:T(8,128)(2,1)S(1)}, u32[]{:S(2)}, u32[]{:S(2)}) collective-permute-start(bf16[160,256]{1,0:T(8,128)(2,1)S(1)} %get-tuple-element.16), channel_id=1, source_target_pairs={{0,32},{4,36},{8,40},{12,44},{16,48},{20,52},{24,56},{28,60},{32,6... | collective-permute-start | bytes 245768 | tf_op jit(solution)/shard_map/ppermute | solution.py:366
  46.1 2.8 %collective-permute-start.1 = (bf16[160,256]{1,0:T(8,128)(2,1)S(1)}, bf16[160,256]{1,0:T(8,128)(2,1)S(1)}, u32[]{:S(2)}, u32[]{:S(2)}) collective-permute-start(bf16[160,256]{1,0:T(8,128)(2,1)S(1)} %get-tuple-element.17), channel_id=1, source_target_pairs={{32,0},{36,4},{40,8},{44,12},{48,16},{52,20},{56,24},{60,28},{64,3... | collective-permute-start | bytes 245768 | tf_op jit(solution)/shard_map/ppermute | solution.py:366
  49.0 0.2 collective-permute-done.north
  49.2 2.1 %collective-permute-done.1.south = bf16[160,256]{1,0:T(8,128)(2,1)S(1)} collective-permute-done((bf16[160,256]{1,0:T(8,128)(2,1)S(1)}, bf16[160,256]{1,0:T(8,128)(2,1)S(1)}, u32[]{:S(2)}, u32[]{:S(2)}) %collective-permute-start.1) | collective-permute-done | bytes 81952 | tf_op jit(solution)/shard_map/ppermute | solution.py:366
  51.3 3.5 %collective-permute-start.2 = (bf16[26,8,256]{2,1,0:T(8,128)(2,1)S(1)}, bf16[26,8,256]{2,1,0:T(8,128)(2,1)S(1)}, u32[]{:S(2)}, u32[]{:S(2)}) collective-permute-start(bf16[26,8,256]{2,1,0:T(8,128)(2,1)S(1)} %get-tuple-element.19), channel_id=1, source_target_pairs={{0,4},{4,8},{8,12},{12,16},{16,20},{20,24},{24,28},{32,36},{36,40}... | collective-permute-start | bytes 319496 | tf_op jit(solution)/shard_map/ppermute | solution.py:366
  54.9 1.9 %collective-permute-start.3 = (bf16[26,8,256]{2,1,0:T(8,128)(2,1)S(1)}, bf16[26,8,256]{2,1,0:T(8,128)(2,1)S(1)}, u32[]{:S(2)}, u32[]{:S(2)}) collective-permute-start(bf16[26,8,256]{2,1,0:T(8,128)(2,1)S(1)} %get-tuple-element.20), channel_id=1, source_target_pairs={{4,0},{8,4},{12,8},{16,12},{20,16},{24,20},{28,24},{36,32},{40,36}... | collective-permute-start | bytes 319496 | tf_op jit(solution)/shard_map/ppermute | solution.py:366
  56.8 4.1 %collective-permute-done.3.east = bf16[26,8,256]{2,1,0:T(8,128)(2,1)S(1)} collective-permute-done((bf16[26,8,256]{2,1,0:T(8,128)(2,1)S(1)}, bf16[26,8,256]{2,1,0:T(8,128)(2,1)S(1)}, u32[]{:S(2)}, u32[]{:S(2)}) %collective-permute-start.3) | collective-permute-done | bytes 106528 | tf_op jit(solution)/shard_map/ppermute | solution.py:366
  60.9 3.5 %shard_map.143 = (f32[512,256]{1,0:T(8,128)S(1)}, bf16[256,768]{1,0:T(8,128)(2,1)S(1)}) custom-call(bf16[160,256]{1,0:T(8,128)(2,1)S(1)} %collective-permute-done.north, bf16[160,256]{1,0:T(8,128)(2,1)S(1)} %collective-permute-done.1.south, bf16[26,8,256]{2,1,0:T(8,128)(2,1)S(1)} %collective-permute-done.2.west, ...), custom_call_target="tpu_custom_call" | custom-call | tf_op jit(solution)/shard_map/pallas_call | solution.py:279
  64.5 0.9 reshape.47
  65.4 9.5 %all-to-all-start.1 = ((bf16[128,2,768]{2,1,0:T(2,128)(2,1)}), bf16[128,2,768]{2,1,0:T(2,128)(2,1)S(1)}, u32[]{:S(2)}, u32[]{:S(2)}) async-start(bf16[128,2,768]{2,1,0:T(2,128)(2,1)} %reshape.47), calls=%async_computation.1 | async-start | bytes 786432 | tf_op jit(solution)/shard_map/all_to_all | solution.py:409
  74.9 0.2 shard_map.144
  75.1 9.1 %psum.7.film = bf16[16,256]{1,0:T(8,128)(2,1)S(1)} all-reduce(bf16[16,256]{1,0:T(8,128)(2,1)S(1)} %shard_map.144), channel_id=1, replica_groups=mesh['space'=128,'lead'=4] {'lead'}, use_global_device_ids=true, to_apply=%region_0.1 | all-reduce | flops 4096 | bytes 16384 | tf_op jit(solution)/shard_map/psum | solution.py:408
  84.3 18.8 %all-to-all-done.1 = bf16[128,2,768]{2,1,0:T(2,128)(2,1)S(1)} async-done(((bf16[128,2,768]{2,1,0:T(2,128)(2,1)}), bf16[128,2,768]{2,1,0:T(2,128)(2,1)S(1)}, u32[]{:S(2)}, u32[]{:S(2)}) %all-to-all-start.1) | async-done | bytes 393248 | tf_op jit(solution)/shard_map/all_to_all | solution.py:409
  103.1 0.1 reshape.48.returned
  103.2 3.2 %shard_map.145 = (bf16[512,256]{1,0:T(8,128)(2,1)}, bf16[256,256]{1,0:T(8,128)(2,1)}) custom-call(bf16[256,768]{1,0:T(8,128)(2,1)S(1)} %reshape.48.returned, bf16[3,768,256]{2,1,0:T(8,128)(2,1)S(1)} %bitcast.10, bf16[4,256]{1,0:T(4,128)(2,1)S(1)} %copy-done.8, f32[512,256]{1,0:T(8,128)S(1)} %get-tuple-element.23.partial, bf16[16,256]{1,0:T(8,128)(2,1)S(1)} %psum.7.film, ...), custom_call_target="tpu_custom_call" | custom-call | tf_op jit(solution)/shard_map/pallas_call | solution.py:279
  (23 shorter events, 0.1 us)
Async XLA Ops:
  0.6 42.5 %copy-start.7 = (bf16[128,256]{1,0:T(8,128)(2,1)S(1)}, bf16[128,256]{1,0:T(8,128)(2,1)}, u32[]{:S(2)}) copy-start(bf16[128,256]{1,0:T(8,128)(2,1)} %embed.1) | copy-start | bytes 196612
  0.6 42.5 %copy-start.3 = (bf16[1,16,32,256]{3,2,1,0:T(8,128)(2,1)S(1)}, bf16[1,16,32,256]{3,2,1,0:T(8,128)(2,1)}, u32[]{:S(2)}) copy-start(bf16[1,16,32,256]{3,2,1,0:T(8,128)(2,1)} %param.13) | copy-start | bytes 786436
  3.7 57.2 %copy-start = (bf16[3,3,256,256]{3,2,1,0:T(8,128)(2,1)S(1)}, bf16[3,3,256,256]{3,2,1,0:T(8,128)(2,1)}, u32[]{:S(2)}) copy-start(bf16[3,3,256,256]{3,2,1,0:T(8,128)(2,1)} %param.18) | copy-start | bytes 3538948
  3.7 57.2 %copy-start.1 = (bf16[3,3,256,256]{3,2,1,0:T(8,128)(2,1)S(1)}, bf16[3,3,256,256]{3,2,1,0:T(8,128)(2,1)}, u32[]{:S(2)}) copy-start(bf16[3,3,256,256]{3,2,1,0:T(8,128)(2,1)} %param.19) | copy-start | bytes 3538948
  3.7 57.2 %copy-start.8 = (bf16[4,256]{1,0:T(4,128)(2,1)S(1)}, bf16[4,256]{1,0:T(4,128)(2,1)}, u32[]{:S(2)}) copy-start(bf16[4,256]{1,0:T(4,128)(2,1)} %gains.3) | copy-start | bytes 6148
  43.7 5.5 %collective-permute-start = (bf16[160,256]{1,0:T(8,128)(2,1)S(1)}, bf16[160,256]{1,0:T(8,128)(2,1)S(1)}, u32[]{:S(2)}, u32[]{:S(2)}) collective-permute-start(bf16[160,256]{1,0:T(8,128)(2,1)S(1)} %get-tuple-element.16), channel_id=1, source_target_pairs={{0,32},{4,36},{8,40},{12,44},{16,48},{20,52},{24,56},{28,60},{32,6... | collective-permute-start | bytes 245768 | tf_op jit(solution)/shard_map/ppermute | solution.py:366
  46.1 5.2 %collective-permute-start.1 = (bf16[160,256]{1,0:T(8,128)(2,1)S(1)}, bf16[160,256]{1,0:T(8,128)(2,1)S(1)}, u32[]{:S(2)}, u32[]{:S(2)}) collective-permute-start(bf16[160,256]{1,0:T(8,128)(2,1)S(1)} %get-tuple-element.17), channel_id=1, source_target_pairs={{32,0},{36,4},{40,8},{44,12},{48,16},{52,20},{56,24},{60,28},{64,3... | collective-permute-start | bytes 245768 | tf_op jit(solution)/shard_map/ppermute | solution.py:366
  51.3 5.5 %collective-permute-start.2 = (bf16[26,8,256]{2,1,0:T(8,128)(2,1)S(1)}, bf16[26,8,256]{2,1,0:T(8,128)(2,1)S(1)}, u32[]{:S(2)}, u32[]{:S(2)}) collective-permute-start(bf16[26,8,256]{2,1,0:T(8,128)(2,1)S(1)} %get-tuple-element.19), channel_id=1, source_target_pairs={{0,4},{4,8},{8,12},{12,16},{16,20},{20,24},{24,28},{32,36},{36,40}... | collective-permute-start | bytes 319496 | tf_op jit(solution)/shard_map/ppermute | solution.py:366
  54.9 6.0 %collective-permute-start.3 = (bf16[26,8,256]{2,1,0:T(8,128)(2,1)S(1)}, bf16[26,8,256]{2,1,0:T(8,128)(2,1)S(1)}, u32[]{:S(2)}, u32[]{:S(2)}) collective-permute-start(bf16[26,8,256]{2,1,0:T(8,128)(2,1)S(1)} %get-tuple-element.20), channel_id=1, source_target_pairs={{4,0},{8,4},{12,8},{16,12},{20,16},{24,20},{28,24},{36,32},{40,36}... | collective-permute-start | bytes 319496 | tf_op jit(solution)/shard_map/ppermute | solution.py:366
  64.4 10.5 %copy-start.4 = (bf16[180,512]{1,0:T(8,128)(2,1)S(1)}, bf16[180,512]{1,0:T(8,128)(2,1)}, u32[]{:S(2)}) copy-start(bf16[180,512]{1,0:T(8,128)(2,1)} %film_table.1) | copy-start | bytes 552964
  64.4 10.5 %copy-start.9 = (s32[4]{0:T(128)S(1)}, s32[4]{0:T(128)}, u32[]{:S(2)}) copy-start(s32[4]{0:T(128)} %param.23) | copy-start | bytes 52
  64.4 38.8 %copy-start.2 = (bf16[3,3,256,256]{3,2,1,0:T(8,128)(2,1)S(1)}, bf16[3,3,256,256]{3,2,1,0:T(8,128)(2,1)}, u32[]{:S(2)}) copy-start(bf16[3,3,256,256]{3,2,1,0:T(8,128)(2,1)} %param.20) | copy-start | bytes 3538948
  64.4 38.8 %copy-start.5 = (bf16[256,256]{1,0:T(8,128)(2,1)S(1)}, bf16[256,256]{1,0:T(8,128)(2,1)}, u32[]{:S(2)}) copy-start(bf16[256,256]{1,0:T(8,128)(2,1)} %out_proj.1) | copy-start | bytes 393220
  64.5 38.8 %copy-start.6 = (bf16[256,256]{1,0:T(8,128)(2,1)S(1)}, bf16[256,256]{1,0:T(8,128)(2,1)}, u32[]{:S(2)}) copy-start(bf16[256,256]{1,0:T(8,128)(2,1)} %projector.1) | copy-start | bytes 393220
  65.4 37.7 %all-to-all-start.1 = ((bf16[128,2,768]{2,1,0:T(2,128)(2,1)}), bf16[128,2,768]{2,1,0:T(2,128)(2,1)S(1)}, u32[]{:S(2)}, u32[]{:S(2)}) async-start(bf16[128,2,768]{2,1,0:T(2,128)(2,1)} %reshape.47), calls=%async_computation.1 | async-start | bytes 786432 | tf_op jit(solution)/shard_map/all_to_all | solution.py:409

commit v11 on v10

--- a/solution.py
+++ b/solution.py
@@ -150,8 +150,8 @@
     frame[:HALO, inner] = above
     frame[HALO : HALO + TILE_H, inner] = own[...]
     frame[HALO + TILE_H :, inner] = below
-    frame[:, :SIDE] = west[...].astype(F32)
-    frame[:, SIDE + TILE_W :] = east[...].astype(F32)
+    frame[:, :SIDE] = jnp.where(col_at > 0, west[...].astype(F32), 0.0)
+    frame[:, SIDE + TILE_W :] = jnp.where(col_at < TILE_COLS - 1, east[...].astype(F32), 0.0)
     gain = gains[0:1].astype(F32)
     for y in range(FRAME_H):
         normed = rms_scale(frame[y], gain)
@@ -360,8 +360,8 @@
     count = lax.axis_size("space")
     pairs = []
     for source in range(count):
-        row, col = source // TILE_COLS + row_step, source % TILE_COLS + col_step
-        if 0 <= row < count // TILE_COLS and 0 <= col < TILE_COLS:
+        row, col = source // TILE_COLS + row_step, (source + col_step) % TILE_COLS
+        if 0 <= row < count // TILE_COLS:
             pairs.append((source, row * TILE_COLS + col))
     return lax.ppermute(value, "space", pairs)
 

time: 107 us -> 105 us (0.981)
  starting transfers between devices: 20.3 us -> 18.1 us
    ppermute x4, starting transfers between devices: 10.7 us -> 6.93 us  [shifted(): return lax.ppermute(value, 'space', pairs)]
    all_to_all x1, starting transfers between devices: 9.51 us -> 11.2 us  [body(): lax.all_to_all(parcel.reshape(space_count, 2, 3 * DEPTH), 'space', 0, 0,...]
  transfers between devices with their start and end apart: 5 -> 5, of which waited for: 4 -> 5; matrix products, arithmetic and copies ran while one was open for 0% -> 0% of each run, Pallas kernels for 0% -> 0%
where the time goes in v11:
time: 105 us
  blocking collectives  48.4 us (46%)
  waiting for transfers between devices  25.5 us (24%)
  starting transfers between devices  18.1 us (17%)
  Pallas kernels  7.99 us (8%)
  other arithmetic  2.45 us (2%)
  local copies, waits for them, and re-layouts  1.26 us (1%)
    all_to_all x1, blocking collectives, body(): lax.all_to_all(payload.reshape(space_count, 2, 3 * readings), 'space', 0,...  39.2 us
    all_to_all x1, waiting for transfers between devices, body(): lax.all_to_all(parcel.reshape(space_count, 2, 3 * DEPTH), 'space', 0, 0,...  18.8 us
    all_to_all x1, starting transfers between devices, body(): lax.all_to_all(parcel.reshape(space_count, 2, 3 * DEPTH), 'space', 0, 0,...  11.2 us
    psum x1, blocking collectives, body(): film = lax.psum(film_rows(steps, film_table), 'lead')  9.15 us
    pallas_call x6, Pallas kernels, call(): pl.pallas_call(kernel, out_shape=[jax.ShapeDtypeStruct(shape, dtype) for...  7.99 us
    ppermute x4, starting transfers between devices, shifted(): return lax.ppermute(value, 'space', pairs)  6.93 us
    ppermute x4, waiting for transfers between devices, shifted(): return lax.ppermute(value, 'space', pairs)  6.75 us
  transfers between devices with their start and end apart: 5, of which 5 were waited for; matrix products, arithmetic and copies ran while one was open for 0% of the time, Pallas kernels for 0%

profile of v11, /device:TPU:33, one launch (start us, length us, event | category | flops | bytes accessed | tf_op | source)
XLA Modules:
  0.0 104.6 jit_solution(9945463835943211296)
XLA Ops:
  0.7 0.7 broadcast_shift-right-arithmetic_fusion
  1.4 0.8 select_convert_fusion
  2.3 0.9 pad_maximum_fusion.records
  3.1 0.6 shard_map.140
  3.7 0.0 copy-start
  3.7 0.1 reshape.42
  3.8 39.2 %all_to_all.10 = bf16[128,2,384]{2,1,0:T(2,128)(2,1)S(1)} all-to-all(bf16[128,2,384]{2,1,0:T(2,128)(2,1)S(1)} %reshape.42), channel_id=1, replica_groups=mesh['space'=128,'lead'=4] {'space'}, dimensions={0} | all-to-all | bytes 393216 | tf_op jit(solution)/shard_map/all_to_all | solution.py:392
  43.0 0.1 reshape.43.arrived
  43.1 0.5 shard_map.141
  43.7 2.4 %collective-permute-start = (bf16[160,256]{1,0:T(8,128)(2,1)S(1)}, bf16[160,256]{1,0:T(8,128)(2,1)S(1)}, u32[]{:S(2)}, u32[]{:S(2)}) collective-permute-start(bf16[160,256]{1,0:T(8,128)(2,1)S(1)} %get-tuple-element.16), channel_id=1, source_target_pairs={{0,32},{4,36},{8,40},{12,44},{16,48},{20,52},{24,56},{28,60},{32,6... | collective-permute-start | bytes 245768 | tf_op jit(solution)/shard_map/ppermute | solution.py:366
  46.1 2.8 %collective-permute-start.1 = (bf16[160,256]{1,0:T(8,128)(2,1)S(1)}, bf16[160,256]{1,0:T(8,128)(2,1)S(1)}, u32[]{:S(2)}, u32[]{:S(2)}) collective-permute-start(bf16[160,256]{1,0:T(8,128)(2,1)S(1)} %get-tuple-element.17), channel_id=1, source_target_pairs={{32,0},{36,4},{40,8},{44,12},{48,16},{52,20},{56,24},{60,28},{64,3... | collective-permute-start | bytes 245768 | tf_op jit(solution)/shard_map/ppermute | solution.py:366
  49.0 0.2 collective-permute-done.north
  49.2 2.1 %collective-permute-done.1.south = bf16[160,256]{1,0:T(8,128)(2,1)S(1)} collective-permute-done((bf16[160,256]{1,0:T(8,128)(2,1)S(1)}, bf16[160,256]{1,0:T(8,128)(2,1)S(1)}, u32[]{:S(2)}, u32[]{:S(2)}) %collective-permute-start.1) | collective-permute-done | bytes 81952 | tf_op jit(solution)/shard_map/ppermute | solution.py:366
  51.3 1.6 %collective-permute-start.2 = (bf16[26,8,256]{2,1,0:T(8,128)(2,1)S(1)}, bf16[26,8,256]{2,1,0:T(8,128)(2,1)S(1)}, u32[]{:S(2)}, u32[]{:S(2)}) collective-permute-start(bf16[26,8,256]{2,1,0:T(8,128)(2,1)S(1)} %get-tuple-element.19), channel_id=1, source_target_pairs={{0,4},{4,8},{8,12},{12,16},{16,20},{20,24},{24,28},{28,0},{32,36},... | collective-permute-start | bytes 319496 | tf_op jit(solution)/shard_map/ppermute | solution.py:366
  53.0 1.7 %collective-permute-done.2.west = bf16[26,8,256]{2,1,0:T(8,128)(2,1)S(1)} collective-permute-done((bf16[26,8,256]{2,1,0:T(8,128)(2,1)S(1)}, bf16[26,8,256]{2,1,0:T(8,128)(2,1)S(1)}, u32[]{:S(2)}, u32[]{:S(2)}) %collective-permute-start.2) | collective-permute-done | bytes 106528 | tf_op jit(solution)/shard_map/ppermute | solution.py:366
  54.7 2.7 %collective-permute-done.3.east = bf16[26,8,256]{2,1,0:T(8,128)(2,1)S(1)} collective-permute-done((bf16[26,8,256]{2,1,0:T(8,128)(2,1)S(1)}, bf16[26,8,256]{2,1,0:T(8,128)(2,1)S(1)}, u32[]{:S(2)}, u32[]{:S(2)}) %collective-permute-start.3) | collective-permute-done | bytes 106528 | tf_op jit(solution)/shard_map/ppermute | solution.py:366
  57.4 3.5 %shard_map.143 = (f32[512,256]{1,0:T(8,128)S(1)}, bf16[256,768]{1,0:T(8,128)(2,1)S(1)}) custom-call(bf16[160,256]{1,0:T(8,128)(2,1)S(1)} %collective-permute-done.north, bf16[160,256]{1,0:T(8,128)(2,1)S(1)} %collective-permute-done.1.south, bf16[26,8,256]{2,1,0:T(8,128)(2,1)S(1)} %collective-permute-done.2.west, ...), custom_call_target="tpu_custom_call" | custom-call | tf_op jit(solution)/shard_map/pallas_call | solution.py:279
  61.0 0.9 reshape.47
  61.9 11.2 %all-to-all-start.1 = ((bf16[128,2,768]{2,1,0:T(2,128)(2,1)}), bf16[128,2,768]{2,1,0:T(2,128)(2,1)S(1)}, u32[]{:S(2)}, u32[]{:S(2)}) async-start(bf16[128,2,768]{2,1,0:T(2,128)(2,1)} %reshape.47), calls=%async_computation.1 | async-start | bytes 786432 | tf_op jit(solution)/shard_map/all_to_all | solution.py:409
  73.1 0.2 shard_map.144
  73.3 9.2 %psum.7.film = bf16[16,256]{1,0:T(8,128)(2,1)S(1)} all-reduce(bf16[16,256]{1,0:T(8,128)(2,1)S(1)} %shard_map.144), channel_id=1, replica_groups=mesh['space'=128,'lead'=4] {'lead'}, use_global_device_ids=true, to_apply=%region_0.1 | all-reduce | flops 4096 | bytes 16384 | tf_op jit(solution)/shard_map/psum | solution.py:408
  82.5 18.8 %all-to-all-done.1 = bf16[128,2,768]{2,1,0:T(2,128)(2,1)S(1)} async-done(((bf16[128,2,768]{2,1,0:T(2,128)(2,1)}), bf16[128,2,768]{2,1,0:T(2,128)(2,1)S(1)}, u32[]{:S(2)}, u32[]{:S(2)}) %all-to-all-start.1) | async-done | bytes 393248 | tf_op jit(solution)/shard_map/all_to_all | solution.py:409
  101.3 0.1 reshape.48.returned
  101.4 3.2 %shard_map.145 = (bf16[512,256]{1,0:T(8,128)(2,1)}, bf16[256,256]{1,0:T(8,128)(2,1)}) custom-call(bf16[256,768]{1,0:T(8,128)(2,1)S(1)} %reshape.48.returned, bf16[3,768,256]{2,1,0:T(8,128)(2,1)S(1)} %bitcast.10, bf16[4,256]{1,0:T(4,128)(2,1)S(1)} %copy-done.8, f32[512,256]{1,0:T(8,128)S(1)} %get-tuple-element.23.partial, bf16[16,256]{1,0:T(8,128)(2,1)S(1)} %psum.7.film, ...), custom_call_target="tpu_custom_call" | custom-call | tf_op jit(solution)/shard_map/pallas_call | solution.py:279
  (23 shorter events, 0.1 us)
Async XLA Ops:
  0.6 42.5 %copy-start.7 = (bf16[128,256]{1,0:T(8,128)(2,1)S(1)}, bf16[128,256]{1,0:T(8,128)(2,1)}, u32[]{:S(2)}) copy-start(bf16[128,256]{1,0:T(8,128)(2,1)} %embed.1) | copy-start | bytes 196612
  0.6 42.5 %copy-start.3 = (bf16[1,16,32,256]{3,2,1,0:T(8,128)(2,1)S(1)}, bf16[1,16,32,256]{3,2,1,0:T(8,128)(2,1)}, u32[]{:S(2)}) copy-start(bf16[1,16,32,256]{3,2,1,0:T(8,128)(2,1)} %param.13) | copy-start | bytes 786436
  3.7 53.7 %copy-start = (bf16[3,3,256,256]{3,2,1,0:T(8,128)(2,1)S(1)}, bf16[3,3,256,256]{3,2,1,0:T(8,128)(2,1)}, u32[]{:S(2)}) copy-start(bf16[3,3,256,256]{3,2,1,0:T(8,128)(2,1)} %param.18) | copy-start | bytes 3538948
  3.7 53.7 %copy-start.1 = (bf16[3,3,256,256]{3,2,1,0:T(8,128)(2,1)S(1)}, bf16[3,3,256,256]{3,2,1,0:T(8,128)(2,1)}, u32[]{:S(2)}) copy-start(bf16[3,3,256,256]{3,2,1,0:T(8,128)(2,1)} %param.19) | copy-start | bytes 3538948
  3.7 53.7 %copy-start.8 = (bf16[4,256]{1,0:T(4,128)(2,1)S(1)}, bf16[4,256]{1,0:T(4,128)(2,1)}, u32[]{:S(2)}) copy-start(bf16[4,256]{1,0:T(4,128)(2,1)} %gains.3) | copy-start | bytes 6148
  43.7 5.5 %collective-permute-start = (bf16[160,256]{1,0:T(8,128)(2,1)S(1)}, bf16[160,256]{1,0:T(8,128)(2,1)S(1)}, u32[]{:S(2)}, u32[]{:S(2)}) collective-permute-start(bf16[160,256]{1,0:T(8,128)(2,1)S(1)} %get-tuple-element.16), channel_id=1, source_target_pairs={{0,32},{4,36},{8,40},{12,44},{16,48},{20,52},{24,56},{28,60},{32,6... | collective-permute-start | bytes 245768 | tf_op jit(solution)/shard_map/ppermute | solution.py:366
  46.1 5.2 %collective-permute-start.1 = (bf16[160,256]{1,0:T(8,128)(2,1)S(1)}, bf16[160,256]{1,0:T(8,128)(2,1)S(1)}, u32[]{:S(2)}, u32[]{:S(2)}) collective-permute-start(bf16[160,256]{1,0:T(8,128)(2,1)S(1)} %get-tuple-element.17), channel_id=1, source_target_pairs={{32,0},{36,4},{40,8},{44,12},{48,16},{52,20},{56,24},{60,28},{64,3... | collective-permute-start | bytes 245768 | tf_op jit(solution)/shard_map/ppermute | solution.py:366
  51.3 3.4 %collective-permute-start.2 = (bf16[26,8,256]{2,1,0:T(8,128)(2,1)S(1)}, bf16[26,8,256]{2,1,0:T(8,128)(2,1)S(1)}, u32[]{:S(2)}, u32[]{:S(2)}) collective-permute-start(bf16[26,8,256]{2,1,0:T(8,128)(2,1)S(1)} %get-tuple-element.19), channel_id=1, source_target_pairs={{0,4},{4,8},{8,12},{12,16},{16,20},{20,24},{24,28},{28,0},{32,36},... | collective-permute-start | bytes 319496 | tf_op jit(solution)/shard_map/ppermute | solution.py:366
  53.0 4.4 %collective-permute-start.3 = (bf16[26,8,256]{2,1,0:T(8,128)(2,1)S(1)}, bf16[26,8,256]{2,1,0:T(8,128)(2,1)S(1)}, u32[]{:S(2)}, u32[]{:S(2)}) collective-permute-start(bf16[26,8,256]{2,1,0:T(8,128)(2,1)S(1)} %get-tuple-element.20), channel_id=1, source_target_pairs={{0,28},{4,0},{8,4},{12,8},{16,12},{20,16},{24,20},{28,24},{32,60},... | collective-permute-start | bytes 319496 | tf_op jit(solution)/shard_map/ppermute | solution.py:366
  60.9 12.2 %copy-start.4 = (bf16[180,512]{1,0:T(8,128)(2,1)S(1)}, bf16[180,512]{1,0:T(8,128)(2,1)}, u32[]{:S(2)}) copy-start(bf16[180,512]{1,0:T(8,128)(2,1)} %film_table.1) | copy-start | bytes 552964
  60.9 12.2 %copy-start.9 = (s32[4]{0:T(128)S(1)}, s32[4]{0:T(128)}, u32[]{:S(2)}) copy-start(s32[4]{0:T(128)} %param.23) | copy-start | bytes 52
  60.9 40.5 %copy-start.2 = (bf16[3,3,256,256]{3,2,1,0:T(8,128)(2,1)S(1)}, bf16[3,3,256,256]{3,2,1,0:T(8,128)(2,1)}, u32[]{:S(2)}) copy-start(bf16[3,3,256,256]{3,2,1,0:T(8,128)(2,1)} %param.20) | copy-start | bytes 3538948
  61.0 40.5 %copy-start.5 = (bf16[256,256]{1,0:T(8,128)(2,1)S(1)}, bf16[256,256]{1,0:T(8,128)(2,1)}, u32[]{:S(2)}) copy-start(bf16[256,256]{1,0:T(8,128)(2,1)} %out_proj.1) | copy-start | bytes 393220
  61.0 40.5 %copy-start.6 = (bf16[256,256]{1,0:T(8,128)(2,1)S(1)}, bf16[256,256]{1,0:T(8,128)(2,1)}, u32[]{:S(2)}) copy-start(bf16[256,256]{1,0:T(8,128)(2,1)} %projector.1) | copy-start | bytes 393220
  61.9 39.4 %all-to-all-start.1 = ((bf16[128,2,768]{2,1,0:T(2,128)(2,1)}), bf16[128,2,768]{2,1,0:T(2,128)(2,1)S(1)}, u32[]{:S(2)}, u32[]{:S(2)}) async-start(bf16[128,2,768]{2,1,0:T(2,128)(2,1)} %reshape.47), calls=%async_computation.1 | async-start | bytes 786432 | tf_op jit(solution)/shard_map/all_to_all | solution.py:409

commit v12 on v11

--- a/solution.py
+++ b/solution.py
@@ -120,7 +120,8 @@
     out[...] = jnp.concatenate([rows, rest], axis=0).astype(BF16)
 
 
-def widen_kernel(north, south, own, first_cols, last_cols):
+def widen_kernel(image_rows, north, south, own, first_cols, last_cols):
+    row_at, _ = grid_place()
     for y in range(FRAME_H):
         for target, cols in (
             (first_cols, slice(0, SIDE)),
@@ -128,11 +129,12 @@
         ):
             start = y % (HALO + TILE_H) * TILE_W + cols.start
             if y < HALO:
-                rows = north[start : start + SIDE].astype(F32)
+                rows = jnp.where(row_at > 0, north[start : start + SIDE].astype(F32), 0.0)
             elif y < HALO + TILE_H:
                 rows = own[y - HALO, cols]
             else:
                 rows = south[start : start + SIDE].astype(F32)
+                rows = jnp.where(row_at < image_rows - 1, rows, 0.0)
             target[y] = rows.astype(BF16)
 
 
@@ -147,9 +149,9 @@
         rows[: HALO * TILE_W].astype(F32).reshape(HALO, TILE_W, DEPTH) for rows in (north, south)
     )
     inner = slice(SIDE, SIDE + TILE_W)
-    frame[:HALO, inner] = above
+    frame[:HALO, inner] = jnp.where(row_at > 0, above, 0.0)
     frame[HALO : HALO + TILE_H, inner] = own[...]
-    frame[HALO + TILE_H :, inner] = below
+    frame[HALO + TILE_H :, inner] = jnp.where(row_at < image_rows - 1, below, 0.0)
     frame[:, :SIDE] = jnp.where(col_at > 0, west[...].astype(F32), 0.0)
     frame[:, SIDE + TILE_W :] = jnp.where(col_at < TILE_COLS - 1, east[...].astype(F32), 0.0)
     gain = gains[0:1].astype(F32)
@@ -310,9 +312,9 @@
     )
 
 
-def widen(north, south, own):
+def widen(image_rows, north, south, own):
     shape = (FRAME_H, SIDE, DEPTH)
-    return call(widen_kernel, [(shape, BF16), (shape, BF16)], [], [north, south, own])
+    return call(functools.partial(widen_kernel, image_rows), [(shape, BF16), (shape, BF16)], [], [north, south, own])
 
 
 def trunk(image_rows, north, south, west, east, own, conv_fine, conv_mid, gains, arrived):
@@ -360,9 +362,8 @@
     count = lax.axis_size("space")
     pairs = []
     for source in range(count):
-        row, col = source // TILE_COLS + row_step, (source + col_step) % TILE_COLS
-        if 0 <= row < count // TILE_COLS:
-            pairs.append((source, row * TILE_COLS + col))
+        row = (source // TILE_COLS + row_step) % (count // TILE_COLS)
+        pairs.append((source, row * TILE_COLS + (source + col_step) % TILE_COLS))
     return lax.ppermute(value, "space", pairs)
 
 
@@ -396,7 +397,7 @@
 
     north = shifted(last_rows, 1, 0)
     south = shifted(first_rows, -1, 0)
-    first_cols, last_cols = widen(north, south, own)
+    first_cols, last_cols = widen(space_count // TILE_COLS, north, south, own)
     west = shifted(last_cols, 0, 1)
     east = shifted(first_cols, 0, -1)
 

time: 105 us -> 105 us (level)
  no operation moved by 1% of the time
where the time goes in v12:
time: 105 us
  blocking collectives  48.4 us (46%)
  waiting for transfers between devices  25.5 us (24%)
  starting transfers between devices  18.1 us (17%)
  Pallas kernels  8 us (8%)
  other arithmetic  2.45 us (2%)
  local copies, waits for them, and re-layouts  1.26 us (1%)
    all_to_all x1, blocking collectives, body(): lax.all_to_all(payload.reshape(space_count, 2, 3 * readings), 'space', 0,...  39.2 us
    all_to_all x1, waiting for transfers between devices, body(): lax.all_to_all(parcel.reshape(space_count, 2, 3 * DEPTH), 'space', 0, 0,...  18.8 us
    all_to_all x1, starting transfers between devices, body(): lax.all_to_all(parcel.reshape(space_count, 2, 3 * DEPTH), 'space', 0, 0,...  11.2 us
    psum x1, blocking collectives, body(): film = lax.psum(film_rows(steps, film_table), 'lead')  9.15 us
    pallas_call x6, Pallas kernels, call(): pl.pallas_call(kernel, out_shape=[jax.ShapeDtypeStruct(shape, dtype) for...  8 us
    ppermute x4, starting transfers between devices, shifted(): return lax.ppermute(value, 'space', pairs)  6.93 us
    ppermute x4, waiting for transfers between devices, shifted(): return lax.ppermute(value, 'space', pairs)  6.75 us
  transfers between devices with their start and end apart: 5, of which 5 were waited for; matrix products, arithmetic and copies ran while one was open for 0% of the time, Pallas kernels for 0%

profile of v12, /device:TPU:33, one launch (start us, length us, event | category | flops | bytes accessed | tf_op | source)
XLA Modules:
  0.0 104.6 jit_solution(5253697650793948585)
XLA Ops:
  0.7 0.7 broadcast_shift-right-arithmetic_fusion
  1.4 0.8 select_convert_fusion
  2.3 0.9 pad_maximum_fusion.records
  3.1 0.6 shard_map.140
  3.7 0.0 copy-start
  3.7 0.1 reshape.42
  3.8 39.2 %all_to_all.10 = bf16[128,2,384]{2,1,0:T(2,128)(2,1)S(1)} all-to-all(bf16[128,2,384]{2,1,0:T(2,128)(2,1)S(1)} %reshape.42), channel_id=1, replica_groups=mesh['space'=128,'lead'=4] {'space'}, dimensions={0} | all-to-all | bytes 393216 | tf_op jit(solution)/shard_map/all_to_all | solution.py:393
  43.0 0.1 reshape.43.arrived
  43.1 0.5 shard_map.141
  43.7 2.4 %collective-permute-start = (bf16[160,256]{1,0:T(8,128)(2,1)S(1)}, bf16[160,256]{1,0:T(8,128)(2,1)S(1)}, u32[]{:S(2)}, u32[]{:S(2)}) collective-permute-start(bf16[160,256]{1,0:T(8,128)(2,1)S(1)} %get-tuple-element.16), channel_id=1, source_target_pairs={{0,32},{4,36},{8,40},{12,44},{16,48},{20,52},{24,56},{28,60},{32,6... | collective-permute-start | bytes 245768 | tf_op jit(solution)/shard_map/ppermute | solution.py:367
  46.1 2.8 %collective-permute-start.1 = (bf16[160,256]{1,0:T(8,128)(2,1)S(1)}, bf16[160,256]{1,0:T(8,128)(2,1)S(1)}, u32[]{:S(2)}, u32[]{:S(2)}) collective-permute-start(bf16[160,256]{1,0:T(8,128)(2,1)S(1)} %get-tuple-element.17), channel_id=1, source_target_pairs={{0,480},{4,484},{8,488},{12,492},{16,496},{20,500},{24,504},{28,50... | collective-permute-start | bytes 245768 | tf_op jit(solution)/shard_map/ppermute | solution.py:367
  49.0 0.2 collective-permute-done.north
  49.2 2.1 %collective-permute-done.1.south = bf16[160,256]{1,0:T(8,128)(2,1)S(1)} collective-permute-done((bf16[160,256]{1,0:T(8,128)(2,1)S(1)}, bf16[160,256]{1,0:T(8,128)(2,1)S(1)}, u32[]{:S(2)}, u32[]{:S(2)}) %collective-permute-start.1) | collective-permute-done | bytes 81952 | tf_op jit(solution)/shard_map/ppermute | solution.py:367
  51.3 1.6 %collective-permute-start.2 = (bf16[26,8,256]{2,1,0:T(8,128)(2,1)S(1)}, bf16[26,8,256]{2,1,0:T(8,128)(2,1)S(1)}, u32[]{:S(2)}, u32[]{:S(2)}) collective-permute-start(bf16[26,8,256]{2,1,0:T(8,128)(2,1)S(1)} %get-tuple-element.19), channel_id=1, source_target_pairs={{0,4},{4,8},{8,12},{12,16},{16,20},{20,24},{24,28},{28,0},{32,36},... | collective-permute-start | bytes 319496 | tf_op jit(solution)/shard_map/ppermute | solution.py:367
  53.0 1.7 %collective-permute-done.2.west = bf16[26,8,256]{2,1,0:T(8,128)(2,1)S(1)} collective-permute-done((bf16[26,8,256]{2,1,0:T(8,128)(2,1)S(1)}, bf16[26,8,256]{2,1,0:T(8,128)(2,1)S(1)}, u32[]{:S(2)}, u32[]{:S(2)}) %collective-permute-start.2) | collective-permute-done | bytes 106528 | tf_op jit(solution)/shard_map/ppermute | solution.py:367
  54.7 2.7 %collective-permute-done.3.east = bf16[26,8,256]{2,1,0:T(8,128)(2,1)S(1)} collective-permute-done((bf16[26,8,256]{2,1,0:T(8,128)(2,1)S(1)}, bf16[26,8,256]{2,1,0:T(8,128)(2,1)S(1)}, u32[]{:S(2)}, u32[]{:S(2)}) %collective-permute-start.3) | collective-permute-done | bytes 106528 | tf_op jit(solution)/shard_map/ppermute | solution.py:367
  57.4 3.5 %shard_map.143 = (f32[512,256]{1,0:T(8,128)S(1)}, bf16[256,768]{1,0:T(8,128)(2,1)S(1)}) custom-call(bf16[160,256]{1,0:T(8,128)(2,1)S(1)} %collective-permute-done.north, bf16[160,256]{1,0:T(8,128)(2,1)S(1)} %collective-permute-done.1.south, bf16[26,8,256]{2,1,0:T(8,128)(2,1)S(1)} %collective-permute-done.2.west, ...), custom_call_target="tpu_custom_call" | custom-call | tf_op jit(solution)/shard_map/pallas_call | solution.py:281
  61.0 0.9 reshape.47
  61.9 11.2 %all-to-all-start.1 = ((bf16[128,2,768]{2,1,0:T(2,128)(2,1)}), bf16[128,2,768]{2,1,0:T(2,128)(2,1)S(1)}, u32[]{:S(2)}, u32[]{:S(2)}) async-start(bf16[128,2,768]{2,1,0:T(2,128)(2,1)} %reshape.47), calls=%async_computation.1 | async-start | bytes 786432 | tf_op jit(solution)/shard_map/all_to_all | solution.py:410
  73.1 0.2 shard_map.144
  73.3 9.2 %psum.7.film = bf16[16,256]{1,0:T(8,128)(2,1)S(1)} all-reduce(bf16[16,256]{1,0:T(8,128)(2,1)S(1)} %shard_map.144), channel_id=1, replica_groups=mesh['space'=128,'lead'=4] {'lead'}, use_global_device_ids=true, to_apply=%region_0.1 | all-reduce | flops 4096 | bytes 16384 | tf_op jit(solution)/shard_map/psum | solution.py:409
  82.5 18.8 %all-to-all-done.1 = bf16[128,2,768]{2,1,0:T(2,128)(2,1)S(1)} async-done(((bf16[128,2,768]{2,1,0:T(2,128)(2,1)}), bf16[128,2,768]{2,1,0:T(2,128)(2,1)S(1)}, u32[]{:S(2)}, u32[]{:S(2)}) %all-to-all-start.1) | async-done | bytes 393248 | tf_op jit(solution)/shard_map/all_to_all | solution.py:410
  101.3 0.1 reshape.48.returned
  101.5 3.2 %shard_map.145 = (bf16[512,256]{1,0:T(8,128)(2,1)}, bf16[256,256]{1,0:T(8,128)(2,1)}) custom-call(bf16[256,768]{1,0:T(8,128)(2,1)S(1)} %reshape.48.returned, bf16[3,768,256]{2,1,0:T(8,128)(2,1)S(1)} %bitcast.10, bf16[4,256]{1,0:T(4,128)(2,1)S(1)} %copy-done.8, f32[512,256]{1,0:T(8,128)S(1)} %get-tuple-element.23.partial, bf16[16,256]{1,0:T(8,128)(2,1)S(1)} %psum.7.film, ...), custom_call_target="tpu_custom_call" | custom-call | tf_op jit(solution)/shard_map/pallas_call | solution.py:281
  (23 shorter events, 0.1 us)
Async XLA Ops:
  0.6 42.5 %copy-start.7 = (bf16[128,256]{1,0:T(8,128)(2,1)S(1)}, bf16[128,256]{1,0:T(8,128)(2,1)}, u32[]{:S(2)}) copy-start(bf16[128,256]{1,0:T(8,128)(2,1)} %embed.1) | copy-start | bytes 196612
  0.6 42.5 %copy-start.3 = (bf16[1,16,32,256]{3,2,1,0:T(8,128)(2,1)S(1)}, bf16[1,16,32,256]{3,2,1,0:T(8,128)(2,1)}, u32[]{:S(2)}) copy-start(bf16[1,16,32,256]{3,2,1,0:T(8,128)(2,1)} %param.13) | copy-start | bytes 786436
  3.7 53.7 %copy-start = (bf16[3,3,256,256]{3,2,1,0:T(8,128)(2,1)S(1)}, bf16[3,3,256,256]{3,2,1,0:T(8,128)(2,1)}, u32[]{:S(2)}) copy-start(bf16[3,3,256,256]{3,2,1,0:T(8,128)(2,1)} %param.18) | copy-start | bytes 3538948
  3.7 53.7 %copy-start.1 = (bf16[3,3,256,256]{3,2,1,0:T(8,128)(2,1)S(1)}, bf16[3,3,256,256]{3,2,1,0:T(8,128)(2,1)}, u32[]{:S(2)}) copy-start(bf16[3,3,256,256]{3,2,1,0:T(8,128)(2,1)} %param.19) | copy-start | bytes 3538948
  3.7 53.7 %copy-start.8 = (bf16[4,256]{1,0:T(4,128)(2,1)S(1)}, bf16[4,256]{1,0:T(4,128)(2,1)}, u32[]{:S(2)}) copy-start(bf16[4,256]{1,0:T(4,128)(2,1)} %gains.3) | copy-start | bytes 6148
  43.7 5.5 %collective-permute-start = (bf16[160,256]{1,0:T(8,128)(2,1)S(1)}, bf16[160,256]{1,0:T(8,128)(2,1)S(1)}, u32[]{:S(2)}, u32[]{:S(2)}) collective-permute-start(bf16[160,256]{1,0:T(8,128)(2,1)S(1)} %get-tuple-element.16), channel_id=1, source_target_pairs={{0,32},{4,36},{8,40},{12,44},{16,48},{20,52},{24,56},{28,60},{32,6... | collective-permute-start | bytes 245768 | tf_op jit(solution)/shard_map/ppermute | solution.py:367
  46.1 5.2 %collective-permute-start.1 = (bf16[160,256]{1,0:T(8,128)(2,1)S(1)}, bf16[160,256]{1,0:T(8,128)(2,1)S(1)}, u32[]{:S(2)}, u32[]{:S(2)}) collective-permute-start(bf16[160,256]{1,0:T(8,128)(2,1)S(1)} %get-tuple-element.17), channel_id=1, source_target_pairs={{0,480},{4,484},{8,488},{12,492},{16,496},{20,500},{24,504},{28,50... | collective-permute-start | bytes 245768 | tf_op jit(solution)/shard_map/ppermute | solution.py:367
  51.3 3.4 %collective-permute-start.2 = (bf16[26,8,256]{2,1,0:T(8,128)(2,1)S(1)}, bf16[26,8,256]{2,1,0:T(8,128)(2,1)S(1)}, u32[]{:S(2)}, u32[]{:S(2)}) collective-permute-start(bf16[26,8,256]{2,1,0:T(8,128)(2,1)S(1)} %get-tuple-element.19), channel_id=1, source_target_pairs={{0,4},{4,8},{8,12},{12,16},{16,20},{20,24},{24,28},{28,0},{32,36},... | collective-permute-start | bytes 319496 | tf_op jit(solution)/shard_map/ppermute | solution.py:367
  53.0 4.4 %collective-permute-start.3 = (bf16[26,8,256]{2,1,0:T(8,128)(2,1)S(1)}, bf16[26,8,256]{2,1,0:T(8,128)(2,1)S(1)}, u32[]{:S(2)}, u32[]{:S(2)}) collective-permute-start(bf16[26,8,256]{2,1,0:T(8,128)(2,1)S(1)} %get-tuple-element.20), channel_id=1, source_target_pairs={{0,28},{4,0},{8,4},{12,8},{16,12},{20,16},{24,20},{28,24},{32,60},... | collective-permute-start | bytes 319496 | tf_op jit(solution)/shard_map/ppermute | solution.py:367
  60.9 12.2 %copy-start.4 = (bf16[180,512]{1,0:T(8,128)(2,1)S(1)}, bf16[180,512]{1,0:T(8,128)(2,1)}, u32[]{:S(2)}) copy-start(bf16[180,512]{1,0:T(8,128)(2,1)} %film_table.1) | copy-start | bytes 552964
  60.9 12.2 %copy-start.9 = (s32[4]{0:T(128)S(1)}, s32[4]{0:T(128)}, u32[]{:S(2)}) copy-start(s32[4]{0:T(128)} %param.23) | copy-start | bytes 52
  61.0 40.5 %copy-start.2 = (bf16[3,3,256,256]{3,2,1,0:T(8,128)(2,1)S(1)}, bf16[3,3,256,256]{3,2,1,0:T(8,128)(2,1)}, u32[]{:S(2)}) copy-start(bf16[3,3,256,256]{3,2,1,0:T(8,128)(2,1)} %param.20) | copy-start | bytes 3538948
  61.0 40.5 %copy-start.5 = (bf16[256,256]{1,0:T(8,128)(2,1)S(1)}, bf16[256,256]{1,0:T(8,128)(2,1)}, u32[]{:S(2)}) copy-start(bf16[256,256]{1,0:T(8,128)(2,1)} %out_proj.1) | copy-start | bytes 393220
  61.0 40.5 %copy-start.6 = (bf16[256,256]{1,0:T(8,128)(2,1)S(1)}, bf16[256,256]{1,0:T(8,128)(2,1)}, u32[]{:S(2)}) copy-start(bf16[256,256]{1,0:T(8,128)(2,1)} %projector.1) | copy-start | bytes 393220
  61.9 39.4 %all-to-all-start.1 = ((bf16[128,2,768]{2,1,0:T(2,128)(2,1)}), bf16[128,2,768]{2,1,0:T(2,128)(2,1)S(1)}, u32[]{:S(2)}, u32[]{:S(2)}) async-start(bf16[128,2,768]{2,1,0:T(2,128)(2,1)} %reshape.47), calls=%async_computation.1 | async-start | bytes 786432 | tf_op jit(solution)/shard_map/all_to_all | solution.py:410
